TPU v7x, 256 devices: a whole 4x4x8 slice. The times are simulated.
256 devices in a mesh: gx: 64 (over z, y, x_lo), gy: 4 (over x_hi, core).
Axes of the slice: x: 4 (x_hi: 2, x_lo: 2; x = x_hi * 2 + x_lo), y: 4, z: 8, core: 2. Of those that a mesh axis runs over, the one named last changes fastest.
Arguments:
- points: bfloat16 [64, 4, 1024, 192], P('gx', 'gy'), may hold values from -6 to 6
- gain: float32 [192], replicated, may hold values from 0.1 to 1.9
- w_query: bfloat16 [192, 192], replicated
- w_key: bfloat16 [192, 192], replicated
- w_value: bfloat16 [192, 192], replicated, may hold values from -0.4375 to 0.4375
- w_out: bfloat16 [192, 192], replicated, may hold values from -0.4375 to 0.4375
- lengths: int32 [64, 4, 24], P('gx', 'gy'), may hold values from 1 to 64, 1024 in all within a row
- picks: int32 [64, 4, 24, 64], P('gx', 'gy'), may hold values from 0 to 575, as said below
- cotangent: bfloat16 [64, 4, 1024, 192], P('gx', 'gy'), may hold values from -8 to 8
Outputs:
- layer_out: bfloat16 [64, 4, 1024, 192], P('gx', 'gy')
- feature_gradient: float32 [64, 4, 1024, 192], P('gx', 'gy')
- grad_weights: float32 [4, 192, 192], replicated
- gain_gradient: float32 [192], replicated
Inputs may be any that keep to these rules, and one draw needn't show every extreme that they name: Each block's window lengths sum to 1024; points are stored window after window. `picks`: a pick p names row p % 64 of neighbourhood block p // 64, never a block off the grid.
All inputs are finite; a program needn't handle non-finite values.
Results may differ from a plain program's by a relative error of at most 0.012.
The roundings to bfloat16 on the way count: a program that leaves them out, or rounds other values in their place, can miss the bound.
Values may be sent and summed in bfloat16 or wider, within the bound.
No kernel may reach another device: no remote copies, remote signals or barrier semaphores. Data moves between devices by JAX's collectives and lax.ppermute only.
A program may use at most 64 MiB of HBM per device.

v0:
```python
import jax
import jax.numpy as jnp
from jax import lax
from jax.sharding import PartitionSpec as P

H = 6
WIN = 64


window_groups = 6


def extended(cells, sides, width):
    for axis, dim in sides:
        count = lax.axis_size(axis)
        ends = count - 1
        head = lax.slice_in_dim(cells, 0, width, axis=dim)
        tail = lax.slice_in_dim(cells, cells.shape[dim] - width, cells.shape[dim], axis=dim)
        cells = jnp.concatenate(
            [
                lax.ppermute(tail, axis, [(i, (i + 1) % count) for i in range(ends)]),
                cells,
                lax.ppermute(head, axis, [((i + 1) % count, i) for i in range(ends)]),
            ],
            axis=dim,
        )
    return cells


def shifted(block, axis, distance):
    devices = range(lax.axis_size(axis))
    route = [(i - distance, i) for i in devices if i - distance in devices]
    return lax.ppermute(block, axis, route)


def layer_statistics(features_f32):
    feature_mean = jnp.mean(features_f32, axis=-1, keepdims=True)
    centred = features_f32 - feature_mean
    variance = jnp.mean(centred * centred, axis=-1, keepdims=True)
    inverse_deviation = lax.rsqrt(variance + 1e-05)
    return (centred * inverse_deviation, inverse_deviation)


def attend_core(query_win, keys, values, live):
    groups, slots, width = query_win.shape
    count = keys.shape[1]
    heads = H
    depth = width // heads
    qh = query_win.reshape(groups, slots, heads, depth)
    kh = keys.reshape(groups, count, heads, depth)
    vh = values.reshape(groups, count, heads, depth)
    scores = jnp.einsum("gqhd,gkhd->ghqk", qh, kh, preferred_element_type=jnp.float32) * depth ** (
        -0.5
    )
    scores = jnp.where(live[:, None, None, :], scores, -1e30)
    top = jnp.max(scores, axis=-1, keepdims=True)
    weights = jnp.exp(scores - top)
    probs = (weights / jnp.sum(weights, axis=-1, keepdims=True)).astype(jnp.bfloat16)
    out = jnp.einsum("ghqk,gkhd->gqhd", probs, vh, preferred_element_type=jnp.float32)
    return out.reshape(groups, slots, width).astype(jnp.bfloat16)


def attend_device(query, key, value, lengths, chosen):
    count, width = query.shape
    windows = lengths.shape[0]
    offsets = jnp.cumsum(lengths) - lengths
    slots = jnp.arange(WIN, dtype=jnp.int32)
    live_dense = slots[None, :] < lengths[:, None]
    rows = jnp.where(live_dense, offsets[:, None] + slots[None, :], 0)
    query_win = query[rows]
    key_win = key[rows]
    value_win = value[rows]
    keys = jnp.concatenate([key_win, chosen[:, :, :width]], axis=1)
    values = jnp.concatenate([value_win, chosen[:, :, width:]], axis=1)
    live = jnp.concatenate([live_dense, jnp.ones(chosen.shape[:2], dtype=bool)], axis=1)
    per_group = windows // window_groups

    def split(arr):
        return arr.reshape((window_groups, per_group) + arr.shape[1:])

    core = jax.checkpoint(lambda items: attend_core(*items))
    out = lax.map(core, (split(query_win), split(keys), split(values), split(live)))
    flat_out = out.reshape(windows * WIN, width)
    ends = offsets + lengths
    position = jnp.arange(count, dtype=jnp.int32)
    before = (ends[None, :] <= position[:, None]).astype(jnp.int32)
    target = position + jnp.sum(before * (WIN - lengths)[None, :], axis=1)
    return flat_out[target]


def body(points, gain, w_query, w_key, w_value, w_out, lengths, picks, cotangent):
    features_f32 = points[0, 0].astype(jnp.float32)
    count, width = features_f32.shape
    sampled = count // 16
    standardized_features, inverse_deviation = layer_statistics(features_f32)
    normalized_features = (standardized_features * gain).astype(jnp.bfloat16)
    query = jnp.dot(normalized_features, w_query, preferred_element_type=jnp.float32).astype(
        jnp.bfloat16
    )
    key = jnp.dot(normalized_features, w_key, preferred_element_type=jnp.float32).astype(
        jnp.bfloat16
    )
    value = jnp.dot(normalized_features, w_value, preferred_element_type=jnp.float32).astype(
        jnp.bfloat16
    )
    both = jnp.concatenate([key, value], axis=-1)
    sample = both.reshape(sampled, 16, 2 * width)[:, 0][None, None]
    beside_all = extended(sample, (("gx", 0), ("gy", 1)), 1)
    nearby = beside_all.reshape(9 * sampled, 2 * width)
    d_attended = jnp.dot(cotangent[0, 0], w_out.T, preferred_element_type=jnp.float32).astype(
        jnp.bfloat16
    )
    own_lengths = lengths[0, 0]
    own_picks = picks[0, 0]
    chosen = nearby[own_picks]

    def local(q_in, k_in, v_in, c_in):
        return attend_device(q_in, k_in, v_in, own_lengths, c_in)

    attended, pull = jax.vjp(local, query, key, value, chosen)
    d_query, d_key, d_value, d_chosen = pull(d_attended)
    d_near = (
        jnp.zeros((9 * sampled, 2 * width), jnp.float32)
        .at[own_picks.reshape(-1)]
        .add(d_chosen.reshape(-1, 2 * width).astype(jnp.float32))
    )
    d_near = d_near.reshape(3, 3, sampled, 2 * width)
    upper = shifted(d_near[:, 2].astype(jnp.bfloat16), "gy", 1).astype(jnp.float32)
    lower = shifted(d_near[:, 0].astype(jnp.bfloat16), "gy", -1).astype(jnp.float32)
    partial_sum = d_near[:, 1] + upper + lower
    upper = shifted(partial_sum[2].astype(jnp.bfloat16), "gx", 1).astype(jnp.float32)
    lower = shifted(partial_sum[0].astype(jnp.bfloat16), "gx", -1).astype(jnp.float32)
    returned = partial_sum[1] + upper + lower
    returned = returned.astype(jnp.bfloat16)
    d_key = (
        d_key.reshape(sampled, 16, width).at[:, 0].add(returned[:, :width]).reshape(count, width)
    )
    d_value = (
        d_value.reshape(sampled, 16, width).at[:, 0].add(returned[:, width:]).reshape(count, width)
    )
    layer_out = (
        features_f32 + jnp.dot(attended, w_out, preferred_element_type=jnp.float32)
    ).astype(jnp.bfloat16)
    normalized_gradient = jnp.dot(d_query, w_query.T, preferred_element_type=jnp.float32)
    normalized_gradient = normalized_gradient + jnp.dot(
        d_key, w_key.T, preferred_element_type=jnp.float32
    )
    normalized_gradient = normalized_gradient + jnp.dot(
        d_value, w_value.T, preferred_element_type=jnp.float32
    )
    centered_gradient = normalized_gradient * gain
    feature_gradient = inverse_deviation * (
        centered_gradient
        - jnp.mean(centered_gradient, axis=-1, keepdims=True)
        - standardized_features
        * jnp.mean(centered_gradient * standardized_features, axis=-1, keepdims=True)
    ) + cotangent[0, 0].astype(jnp.float32)
    local_weights = jnp.stack(
        [
            jnp.dot(normalized_features.T, d_query, preferred_element_type=jnp.float32),
            jnp.dot(normalized_features.T, d_key, preferred_element_type=jnp.float32),
            jnp.dot(normalized_features.T, d_value, preferred_element_type=jnp.float32),
            jnp.dot(attended.T, cotangent[0, 0], preferred_element_type=jnp.float32),
        ]
    )
    shard_gain = jnp.sum(normalized_gradient * standardized_features, axis=0)
    total_weights, total_gain = lax.psum((local_weights, shard_gain), ("gx", "gy"))
    scale_factor = (count * lax.axis_size("gx") * lax.axis_size("gy")) ** (-0.5)
    return (
        layer_out[None, None],
        feature_gradient[None, None],
        total_weights * scale_factor,
        total_gain * scale_factor,
    )


def solution(mesh):
    return jax.shard_map(
        body,
        mesh=mesh,
        in_specs=(
            P("gx", "gy", None, None),
            P(),
            P(),
            P(),
            P(),
            P(),
            P("gx", "gy", None),
            P("gx", "gy", None, None),
            P("gx", "gy", None, None),
        ),
        out_specs=(P("gx", "gy", None, None), P("gx", "gy", None, None), P(), P()),
        check_vma=False,
    )
```

profile of v0, /device:TPU:1, one launch (start us, length us, event | category | flops | bytes accessed | tf_op | source)
XLA Modules:
  0.0 524.9 jit_solution(11118941822804557131)
XLA Ops:
  11.9 4.1 collective-permute-start
  21.5 6.3 %collective-permute-start.2 = (bf16[3,1,64,384]{3,2,1,0:T(8,128)(2,1)}, bf16[3,1,64,384]{3,2,1,0:T(8,128)(2,1)}, u32[]{:S(2)}, u32[]{:S(2)}) collective-permute-start(bf16[3,1,64,384]{3,2,1,0:T(8,128)(2,1)} %pad_maximum_fusion.5), channel_id=1, source_target_pairs={{0,1},{1,2},{2,3},{4,5},{5,6},{6,7},{8,9},{9,10},{10,11},{12,13},{... | collective-permute-start | bytes 442376 | tf_op jit(solution)/shard_map/ppermute | solution.py:21
  30.9 4.8 gather_fusion
  35.6 5.4 %gather_fusion.3 = bf16[1536,192]{1,0:T(8,128)(2,1)} fusion(bf16[1024,192]{1,0:T(8,128)(2,1)S(1)} %copy.84, s32[2048]{0:T(1024)S(1)} %pad_clamp_fusion.1), kind=kCustom, calls=%fused_computation.3 | custom fusion | bytes 1185792 | tf_op jit(solution)/shard_map/jvp()/gather | solution.py:71
  41.2 4.8 gather_fusion.2
  47.5 7.2 %scatter_custom_fusion = bf16[1536,192]{1,0:T(8,128)(2,1)} fusion(s32[1024]{0:T(1024)} %bitcast.296, bf16[1024,192]{1,0:T(8,128)(2,1)S(1)} %copy.88, bf16[]{:T(256)} %constant.195.clone.1), kind=kCustom, calls=%fused_computation.111 | custom fusion | flops 196608 | bytes 590336 | tf_op jit(solution)/shard_map/transpose(jvp())/scatter-add | solution.py:88
  56.5 4.7 gather_fusion.1
  62.3 2.0 pad_maximum_fusion
  64.3 2.5 copy.82
  69.9 57.3 %while.32 = (s32[]{:T(128)}, bf16[6,4,64,192]{3,2,1,0:T(8,128)(2,1)S(1)}, bf16[6,4,128,192]{2,3,1,0:T(8,128)(2,1)S(1)}, bf16[6,4,128,192]{2,3,1,0:T(8,128)(2,1)}...) while((s32[]{:T(128)}, ...), condition=%wide.region_15.16_spmd, body=%wide.region_9.15_spmd.sunk | while | flops 69058560 | bytes 12688021 | solution.py:82
  127.2 9.8 %scatter_custom_fusion.1 = bf16[1024,192]{1,0:T(8,128)(2,1)S(1)} fusion(s32[1536]{0:T(1024)S(1)} %reshape.483, bf16[1536,192]{1,0:T(8,128)(2,1)S(1)} %bitcast.287, bf16[]{:T(256)} %constant.195.clone.1), kind=kCustom, calls=%fused_computation.120 | custom fusion | flops 294912 | bytes 393218 | tf_op jit(solution)/shard_map/transpose(jvp())/scatter-add | solution.py:70
  144.6 9.9 %scatter_custom_fusion.3 = f32[576,384]{1,0:T(8,128)S(1)} fusion(s32[1536]{0:T(1024)S(1)} %fusion.64, bf16[1536,384]{1,0:T(8,128)(2,1)S(1)} %bitcast.273, f32[]{:T(128)} %constant.196.clone.1), kind=kCustom, calls=%fused_computation.63 | custom fusion | flops 1179648 | bytes 2064388 | tf_op jit(solution)/shard_map/scatter-add | solution.py:125
  155.3 5.2 collective-permute-start.4
  162.6 54.7 %while.31 = (s32[]{:T(128)}, bf16[6,4,64,192]{3,2,1,0:T(8,128)(2,1)S(1)}, bf16[6,4,128,192]{2,3,1,0:T(8,128)(2,1)}, pred[6,4,128]{2,1,0:T(4,128)(4,1)}, bf16[6,4...) while((s32[]{:T(128)}, bf16[6,4,64,192]{3,2,1,0:T(8,128)(2,1)S(1)}, ...), condition=%wide.region_6.7_spmd, body=%wide.region_3.6_spmd.sunk | while | flops 39569152 | bytes 3915897 | solution.py:82
  166.1 2.0 fusion.132
  168.0 3.4 convolution_convert_fusion.13
  175.2 2.0 fusion.132
  177.2 3.4 convolution_convert_fusion.13
  184.4 2.0 fusion.132
  186.3 3.4 convolution_convert_fusion.13
  193.4 2.0 fusion.132
  195.4 3.4 convolution_convert_fusion.13
  204.5 3.4 convolution_convert_fusion.13
  211.7 2.0 fusion.132
  213.6 3.4 convolution_convert_fusion.13
  217.2 4.6 gather_fusion.4
  224.0 3.7 collective-permute-start.6
  229.4 10.2 %scatter_custom_fusion.4 = bf16[1024,192]{1,0:T(8,128)(2,1)S(1)} fusion(s32[1536]{0:T(1024)S(1)} %reshape.483, bf16[1536,192]{1,0:T(8,128)(2,1)} %bitcast.288, bf16[]{:T(256)} %constant.195.clone.1), kind=kCustom, calls=%fused_computation.116 | custom fusion | flops 294912 | bytes 393728 | tf_op jit(solution)/shard_map/transpose(jvp())/scatter-add | solution.py:72
  239.6 9.9 %scatter_custom_fusion.2 = bf16[1024,192]{1,0:T(8,128)(2,1)S(1)} fusion(s32[1536]{0:T(1024)S(1)} %reshape.483, bf16[1536,192]{1,0:T(8,128)(2,1)} %bitcast.289, bf16[]{:T(256)} %constant.195.clone.1), kind=kCustom, calls=%fused_computation.118 | custom fusion | flops 294912 | bytes 393728 | tf_op jit(solution)/shard_map/transpose(jvp())/scatter-add | solution.py:71
  254.7 84.1 %psum.15 = f32[192]{0:T(256)S(1)} all-reduce(f32[192]{0:T(256)S(1)} %get-tuple-element.348), channel_id=1, replica_groups=mesh['gx'=64,'gy'=4] {'gx','gy'}, use_global_device_ids=true, to_apply=%region_24.25 | all-reduce | flops 192 | bytes 1536 | tf_op jit(solution)/shard_map/psum | solution.py:167
  340.5 175.5 %all-reduce.5.cloned.1.call-done = f32[4,192,192]{2,1,0:T(8,128)} async-done(((f32[4,192,192]{2,1,0:T(8,128)}), f32[4,192,192]{2,1,0:T(8,128)}) %all-reduce.5.cloned.1.call-update) | async-done | bytes 589840 | tf_op jit(solution)/shard_map/psum | solution.py:167
  515.9 2.1 broadcast_multiply_fusion
  (291 shorter events, 122.1 us)
Async XLA Ops:
  7.2 3.7 copy-start
  7.2 3.7 copy-start.1
  7.2 3.7 copy-start.20
  7.2 508.7 %all-reduce.5.cloned.1.call-start = ((), (), s32[]{:S(2)}) async-start(), calls=%async_computation | async-start | bytes 1572864 | tf_op jit(solution)/shard_map/psum | solution.py:167
  11.4 5.9 %copy-start.14 = (s32[1,1,24,64]{3,2,1,0:T(8,128)S(1)}, s32[1,1,24,64]{3,2,1,0:T(8,128)}, u32[]{:S(2)}) copy-start(s32[1,1,24,64]{3,2,1,0:T(8,128)} %param.24) | copy-start | bytes 18436
  11.4 6.0 %copy-start.19 = (s32[1,1,24]{2,1,0:T(1,128)S(1)}, s32[1,1,24]{2,1,0:T(1,128)}, u32[]{:S(2)}) copy-start(s32[1,1,24]{2,1,0:T(1,128)} %param.23) | copy-start | bytes 292
  11.4 6.9 %copy-start.12 = (bf16[192,192]{1,0:T(8,128)(2,1)S(1)}, bf16[192,192]{1,0:T(8,128)(2,1)}, u32[]{:S(2)}) copy-start(bf16[192,192]{1,0:T(8,128)(2,1)} %param.19) | copy-start | bytes 221188
  11.8 8.4 %copy-start.2 = (bf16[1,1,1024,192]{2,3,1,0:T(8,128)(2,1)S(1)}, bf16[1,1,1024,192]{2,3,1,0:T(8,128)(2,1)}, u32[]{:S(2)}) copy-start(bf16[1,1,1024,192]{2,3,1,0:T(8,128)(2,1)} %param.25) | copy-start | bytes 1179652
  11.8 8.4 %copy-start.8 = (bf16[192,192]{1,0:T(8,128)(2,1)S(1)}, bf16[192,192]{1,0:T(8,128)(2,1)}, u32[]{:S(2)}) copy-start(bf16[192,192]{1,0:T(8,128)(2,1)} %param.22) | copy-start | bytes 221188
  11.9 8.6 %collective-permute-start = (bf16[1,1,64,384]{3,2,1,0:T(8,128)(2,1)S(1)}, bf16[1,1,64,384]{3,2,1,0:T(8,128)(2,1)S(1)}, u32[]{:S(2)}, u32[]{:S(2)}) collective-permute-start(bf16[1,1,64,384]{3,2,1,0:T(8,128)(2,1)S(1)} %bitcast.290), channel_id=1, source_target_pairs={{0,4},{4,8},{8,12},{12,16},{16,20},{20,24},{24,28},{28,32},{32,36}... | collective-permute-start | bytes 147464 | tf_op jit(solution)/shard_map/ppermute | solution.py:21
  15.9 4.8 collective-permute-start.1
  19.5 8.3 %copy-start.16 = (s32[1024,1]{0,1:T(1,128)}, s32[1024,1]{0,1:T(1,128)S(1)}, u32[]{:S(2)}) copy-start(s32[1024,1]{0,1:T(1,128)S(1)} %compare_select_fusion.3) | copy-start | bytes 12292
  21.5 33.9 %collective-permute-start.2 = (bf16[3,1,64,384]{3,2,1,0:T(8,128)(2,1)}, bf16[3,1,64,384]{3,2,1,0:T(8,128)(2,1)}, u32[]{:S(2)}, u32[]{:S(2)}) collective-permute-start(bf16[3,1,64,384]{3,2,1,0:T(8,128)(2,1)} %pad_maximum_fusion.5), channel_id=1, source_target_pairs={{0,1},{1,2},{2,3},{4,5},{5,6},{6,7},{8,9},{9,10},{10,11},{12,13},{... | collective-permute-start | bytes 442376 | tf_op jit(solution)/shard_map/ppermute | solution.py:21
  27.8 27.6 %collective-permute-start.3 = (bf16[3,1,64,384]{3,2,1,0:T(8,128)(2,1)}, bf16[3,1,64,384]{3,2,1,0:T(8,128)(2,1)}, u32[]{:S(2)}, u32[]{:S(2)}) collective-permute-start(bf16[3,1,64,384]{3,2,1,0:T(8,128)(2,1)} %pad_maximum_fusion.5), channel_id=1, source_target_pairs={{1,0},{2,1},{3,2},{5,4},{6,5},{7,6},{9,8},{10,9},{11,10},{13,12},{... | collective-permute-start | bytes 442376 | tf_op jit(solution)/shard_map/ppermute | solution.py:23
  35.6 5.4 %copy-start.7 = (bf16[1024,192]{0,1:T(8,128)(2,1)S(1)}, bf16[1024,192]{0,1:T(8,128)(2,1)}, u32[]{:S(2)}) copy-start(bf16[1024,192]{0,1:T(8,128)(2,1)} %convolution_convert_fusion.6) | copy-start | bytes 1179652
  47.3 7.5 %copy-start.18 = (pred[24,64]{1,0:T(8,128)(4,1)S(1)}, pred[24,64]{1,0:T(8,128)(4,1)}, u32[]{:S(2)}) copy-start(pred[24,64]{1,0:T(8,128)(4,1)} %iota_compare_fusion.1) | copy-start | bytes 4612
  47.3 8.0 %copy-start.15 = (s32[1536,1]{0,1:T(1,128)S(1)}, s32[1536,1]{0,1:T(1,128)}, u32[]{:S(2)}) copy-start(s32[1536,1]{0,1:T(1,128)} %reshape_squeeze.3) | copy-start | bytes 18436
  61.2 1.1 copy-start.5
  69.9 67.1 %copy-start.21 = (f32[192]{0:T(256)S(1)}, f32[192]{0:T(256)}, u32[]{:S(2)}) copy-start(f32[192]{0:T(256)} %param.18) | copy-start | bytes 2308
  127.2 10.8 %copy-start.13 = (bf16[192,192]{1,0:T(8,128)(2,1)S(1)}, bf16[192,192]{1,0:T(8,128)(2,1)}, u32[]{:S(2)}) copy-start(bf16[192,192]{1,0:T(8,128)(2,1)} %param.19) | copy-start | bytes 221188
  142.8 1.3 copy-start.6
  155.3 67.6 %collective-permute-start.4 = (bf16[3,64,384]{2,1,0:T(8,128)(2,1)}, bf16[3,64,384]{2,1,0:T(8,128)(2,1)}, u32[]{:S(2)}, u32[]{:S(2)}) collective-permute-start(bf16[3,64,384]{2,1,0:T(8,128)(2,1)} %get-tuple-element.401), channel_id=1, source_target_pairs={{0,1},{1,2},{2,3},{4,5},{5,6},{6,7},{8,9},{9,10},{10,11},{12,13},{... | collective-permute-start | bytes 442376 | tf_op jit(solution)/shard_map/ppermute | solution.py:33
  160.5 62.4 %collective-permute-start.5 = (bf16[3,64,384]{2,1,0:T(8,128)(2,1)}, bf16[3,64,384]{2,1,0:T(8,128)(2,1)}, u32[]{:S(2)}, u32[]{:S(2)}) collective-permute-start(bf16[3,64,384]{2,1,0:T(8,128)(2,1)} %get-tuple-element.402), channel_id=1, source_target_pairs={{1,0},{2,1},{3,2},{5,4},{6,5},{7,6},{9,8},{10,9},{11,10},{13,12},{... | collective-permute-start | bytes 442376 | tf_op jit(solution)/shard_map/ppermute | solution.py:33
  165.2 0.6 copy-start.17
  217.2 4.6 copy-start.9
  221.8 7.2 %copy-start.3 = (bf16[1,1,1024,192]{2,3,1,0:T(8,128)(2,1)S(1)}, bf16[1,1,1024,192]{2,3,1,0:T(8,128)(2,1)}, u32[]{:S(2)}) copy-start(bf16[1,1,1024,192]{2,3,1,0:T(8,128)(2,1)} %param.25) | copy-start | bytes 1179652
  224.0 25.5 %collective-permute-start.6 = (bf16[64,384]{1,0:T(8,128)(2,1)S(1)}, bf16[64,384]{1,0:T(8,128)(2,1)S(1)}, u32[]{:S(2)}, u32[]{:S(2)}) collective-permute-start(bf16[64,384]{1,0:T(8,128)(2,1)S(1)} %get-tuple-element.403), channel_id=1, source_target_pairs={{0,4},{4,8},{8,12},{12,16},{16,20},{20,24},{24,28},{28,32},{32,36}... | collective-permute-start | bytes 147464 | tf_op jit(solution)/shard_map/ppermute | solution.py:33
  227.7 22.9 %copy-start.22 = (f32[192]{0:T(256)S(1)}, f32[192]{0:T(256)}, u32[]{:S(2)}) copy-start(f32[192]{0:T(256)} %param.18) | copy-start | bytes 2308
  227.7 21.8 %collective-permute-start.7 = (bf16[64,384]{1,0:T(8,128)(2,1)S(1)}, bf16[64,384]{1,0:T(8,128)(2,1)S(1)}, u32[]{:S(2)}, u32[]{:S(2)}) collective-permute-start(bf16[64,384]{1,0:T(8,128)(2,1)S(1)} %get-tuple-element.404), channel_id=1, source_target_pairs={{4,0},{8,4},{12,8},{16,12},{20,16},{24,20},{28,24},{32,28},{36,32}... | collective-permute-start | bytes 147464 | tf_op jit(solution)/shard_map/ppermute | solution.py:33
  251.0 1.4 copy-start.10
  252.3 1.4 copy-start.4
  252.4 1.4 copy-start.11
  (5 other events, 2.9 us)
Sparse Core Ops, SparseCore 0:
  253.5 262.4 all-reduce.4
where the time goes:
time: 527 us; the launch traced here: 525 us
  waiting for transfers between devices  176 us (33%)
  local copies, waits for them, and re-layouts  91 us (17%)
  blocking collectives  84.1 us (16%)
  other arithmetic  70.9 us (13%)
  matrix products  61.8 us (12%)
  starting transfers between devices  25.8 us (5%)
  between operations  14.7 us (3%)
    psum x1, waiting for transfers between devices, body(): lax.psum((local_weights, shard_gain), ('gx', 'gy'))  175 us
    psum x1, blocking collectives, body(): lax.psum((local_weights, shard_gain), ('gx', 'gy'))  84.1 us
    dot_general x18, matrix products, attend_core(): jnp.einsum('ghqk,gkhd->gqhd', probs, vh, preferred_element_type=jnp.float32)  32.6 us
    dynamic_slice x24, local copies, waits for them, and re-layouts, attend_device(): lax.map(core, (split(query_win), split(keys), split(values), split(live)))  18.5 us
    squeeze x18, local copies, waits for them, and re-layouts, attend_device(): lax.map(core, (split(query_win), split(keys), split(values), split(live)))  15.8 us
    ppermute x4, starting transfers between devices, shifted(): return lax.ppermute(block, axis, route)  12.1 us
    sub x6, matrix products, attend_core(): weights = jnp.exp(scores - top)  11.7 us
  transfers between devices with their start and end apart: 9, of which 2 were waited for; matrix products, arithmetic and copies ran while one was open for 21% of the time, Pallas kernels for 0%

commit v1 on v0

v1 whole, which is shorter than its diff:
```python
import jax
import jax.numpy as jnp
from jax import lax
from jax.experimental import pallas as pl
from jax.experimental.pallas import tpu as pltpu
from jax.sharding import Mesh, PartitionSpec as P

C = 192
H = 6
DEPTH = 32
PTS = 1024
WIN = 64
NWIN = 24
SAMP = 64
NEAR = 9 * SAMP
PAD = PTS + WIN
ROWS = 1280
HALF = ROWS // 2
GX = ("z", "y", "xl")
GY = ("xh", "c")
XY = ("y", "xl", "xh")
SCALE = DEPTH ** (-0.5)
LOG2E = 1.4426950408889634
F32 = jnp.float32
BF16 = jnp.bfloat16
VMEM = pl.BlockSpec(memory_space=pltpu.VMEM)
SMEM = pl.BlockSpec(memory_space=pltpu.SMEM)


def nn(a, b):
    return lax.dot_general(a, b, (((1,), (0,)), ((), ())), preferred_element_type=F32)


def nt(a, b):
    return lax.dot_general(a, b, (((1,), (1,)), ((), ())), preferred_element_type=F32)


def tn(a, b):
    return lax.dot_general(a, b, (((0,), (0,)), ((), ())), preferred_element_type=F32)


def standardize(x):
    mean = jnp.sum(x, axis=-1, keepdims=True) * (1.0 / C)
    centred = x - mean
    variance = jnp.sum(centred * centred, axis=-1, keepdims=True) * (1.0 / C)
    inverse = lax.rsqrt(variance + 1e-05)
    return centred * inverse, inverse


def pre_kernel(points, gain, w_in, w_back, cot, picks_row, picks_col,
               qa, ka, va, da, kvb, qdb, xhat, normed_t, onehot, onehot_t):
    chunk = 128

    def project(i, _):
        rows = pl.ds(pl.multiple_of(i * chunk, chunk), chunk)
        hat, _inv = standardize(points[rows, :].astype(F32))
        xhat[rows, :] = hat
        normed = (hat * gain[...]).astype(BF16)
        wide = nn(normed, w_in[...])
        back = nt(cot[rows, :], w_back[...])
        both = (wide[:, 512:], back[:, 128:])
        for ref, x in ((qa, wide[:, :128]), (ka, wide[:, 128:256]), (va, wide[:, 256:384]),
                       (kvb, wide[:, 384:512]), (da, back[:, :128]), (qdb, both[0] + both[1])):
            ref[rows, :] = x.astype(BF16).astype(F32)
        normed_t[:, rows] = normed.astype(F32).T.astype(BF16)
        return 0

    lax.fori_loop(0, PTS // chunk, project, 0)
    zeros = jnp.zeros((WIN, 128), F32)
    for ref in (qa, ka, va, da, kvb, qdb):
        ref[PTS:, :] = zeros

    def rows_hot(i, _):
        rows = pl.ds(pl.multiple_of(i * WIN, WIN), WIN)
        ids = lax.broadcasted_iota(jnp.int32, (WIN, NEAR), 1)
        onehot[rows, :] = jnp.where(picks_col[rows, :] == ids, 1.0, 0.0).astype(BF16)
        return 0

    lax.fori_loop(0, NWIN, rows_hot, 0)

    def columns_hot(i, _):
        rows = pl.ds(pl.multiple_of(i * SAMP, SAMP), SAMP)
        ids = lax.broadcasted_iota(jnp.int32, (SAMP, NWIN * WIN), 0) + i * SAMP
        onehot_t[rows, :] = jnp.where(picks_row[...] == ids, 1.0, 0.0).astype(BF16)
        return 0

    lax.fori_loop(0, 9, columns_hot, 0)


def attend_kernel(lengths, place, near_points, gain, w_in, cot, qa, ka, va, da, kvb, qdb, xhat,
                  normed_t, onehot, onehot_t,
                  keep, send, d_near, grads,
                  near_hat, near_normed, near_kv, pick, d_pick,
                  oa_s, dqa_s, dka_s, dva_s, dkvb_s, dqob_s, packed):
    hat, _inv = standardize(near_points[...].astype(F32))
    near_hat[...] = hat
    normed = (hat * gain[...]).astype(BF16)
    near_normed[...] = normed
    near_kv[...] = nn(normed, w_in[:, 128:512]).astype(BF16)

    def choose(i, _):
        rows = pl.ds(pl.multiple_of(i * 256, 256), 256)
        pick[rows, :] = nn(onehot[rows, :], near_kv[...]).astype(BF16)
        return 0

    lax.fori_loop(0, NWIN * WIN // 256, choose, 0)

    row_head = lax.broadcasted_iota(jnp.int32, (4 * WIN, 128), 0) // WIN
    lane_head = lax.broadcasted_iota(jnp.int32, (4 * WIN, 128), 1) // DEPTH
    mask = jnp.where(row_head == lane_head, 1.0, 0.0)
    mask16 = mask.astype(BF16)
    key_id = lax.broadcasted_iota(jnp.int32, (1, 128), 1)
    slot = lax.broadcasted_iota(jnp.int32, (WIN, 1), 0)
    half_scale = jnp.where(key_id < 64, SCALE, 1.0)

    def per_head(x):
        return jnp.concatenate([x] * 4, axis=0) * mask16

    def merge(x):
        x = x * mask
        return (x[:WIN] + x[WIN:2 * WIN]) + (x[2 * WIN:3 * WIN] + x[3 * WIN:])

    def softmax(scores, bias):
        scores = scores + bias
        top = jnp.max(scores, axis=-1, keepdims=True)
        weights = jnp.exp2((scores - top) * (SCALE * LOG2E))
        return weights * (1.0 / jnp.sum(weights, axis=-1, keepdims=True))

    def score_gradient(probs, d_probs):
        d_probs = d_probs.astype(BF16).astype(F32)
        inner = jnp.sum(d_probs * probs, axis=-1, keepdims=True)
        return (probs * (d_probs - inner)).astype(BF16)

    def window(w, offset):
        count = lengths[w]
        rows = pl.ds(offset, WIN)
        own = pl.ds(pl.multiple_of(w * WIN, WIN), WIN)
        bias = jnp.where((key_id >= count) & (key_id < WIN), -1e30, 0.0)
        alive = slot < count
        keys = jnp.concatenate([ka[rows, :].astype(BF16), pick[own, 0:128]], axis=0)
        values = jnp.concatenate([va[rows, :].astype(BF16), pick[own, 128:256]], axis=0)
        both = jnp.concatenate([kvb[rows, :].astype(BF16), pick[own, 256:384]], axis=0)
        qe = per_head(qa[rows, :].astype(BF16))
        de = per_head(jnp.where(alive, da[rows, :], 0.0).astype(BF16))
        qde = per_head(jnp.where(alive, qdb[rows, :], 0.0).astype(BF16))
        probs = softmax(nt(qe, keys), bias)
        probs16 = probs.astype(BF16)
        d_scores = score_gradient(probs, nt(de, values))
        mixed = nt(qde, both)
        probs_b = softmax(mixed[:128], bias)
        d_scores_b = score_gradient(probs_b, mixed[128:])
        back = jnp.concatenate([d_scores_b, probs_b.astype(BF16)], axis=0)
        oa_s[rows, :] = merge(nn(probs16, values))
        dqa_s[rows, :] = merge(nn(d_scores, keys)) * SCALE
        dqob_s[rows, :] = merge(nn(back, both)) * half_scale
        d_keys = tn(d_scores, qe) * SCALE
        d_values = tn(probs16, de)
        d_both = tn(back, qde) * half_scale
        dka_s[rows, :] = d_keys[:WIN]
        dva_s[rows, :] = d_values[:WIN]
        dkvb_s[rows, :] = d_both[:WIN]
        d_pick[own, 0:128] = d_keys[WIN:].astype(BF16)
        d_pick[own, 128:256] = d_values[WIN:].astype(BF16)
        d_pick[own, 256:384] = d_both[WIN:].astype(BF16)
        return offset + count

    lax.fori_loop(0, NWIN, window, jnp.int32(0))

    for i, ref in enumerate((dqa_s, dka_s, dva_s, dkvb_s, dqob_s, oa_s)):
        grads[:, 128 * i:128 * (i + 1)] = ref[:PTS, :].astype(BF16)
    near = nn(onehot_t[...], d_pick[...])
    near16 = near.astype(BF16)
    d_near[...] = near16
    rest = (near - near16.astype(F32)).astype(BF16)
    wide = nn(normed_t[...], grads[:, 0:640])
    near_wide = tn(near_normed[...], near16) + tn(near_normed[...], rest)
    out_a = tn(grads[:, 640:768], cot[...])
    out_b = tn(grads[:, 512:640], cot[...])
    packed[0:192, :] = wide[:, 0:128]
    packed[192:384, :] = wide[:, 128:256] + near_wide[:, 0:128]
    packed[384:576, :] = wide[:, 256:384] + near_wide[:, 128:256]
    packed[576:704, :] = out_a[:, 0:128]
    packed[704:768, :] = out_b[64:128, 0:128]
    packed[768:960, :] = wide[:, 384:512] + near_wide[:, 256:384]
    tail = jnp.concatenate([out_a[:, 128:192], out_b[64:128, 128:192]], axis=0)
    packed[960:1152, :] = jnp.concatenate([wide[:, 512:576], tail], axis=1)

    def gain_part(i, total):
        rows = pl.ds(pl.multiple_of(i * 128, 128), 128)
        d = nt(grads[rows, 0:640], w_in[...])
        return total + jnp.sum((d * xhat[rows, :]).reshape(16, 8, C), axis=0)

    total = lax.fori_loop(0, PTS // 128, gain_part, jnp.zeros((8, C), F32))
    d = nt(near16, w_in[:, 128:512]) + nt(rest, w_in[:, 128:512])
    total = total + jnp.sum((d * near_hat[...]).reshape(NEAR // 8, 8, C), axis=0)
    gain_sum = jnp.sum(total, axis=0, keepdims=True)
    packed[1152:, :] = jnp.zeros((ROWS - 1152, 128), F32)
    packed[1152:1153, :] = gain_sum[:, :128]
    packed[1153:1154, 0:64] = gain_sum[:, 128:]
    mine = place[0]
    keep[...] = packed[pl.ds(pl.multiple_of(mine * HALF, HALF), HALF), :]
    send[...] = packed[pl.ds(pl.multiple_of((1 - mine) * HALF, HALF), HALF), :]


def finish_kernel(points, gain, w_in, w_back, cot, grads, returned, layer_out, feature_gradient):
    chunk = 128

    def part(i, _):
        rows = pl.ds(pl.multiple_of(i * chunk, chunk), chunk)
        x = points[rows, :].astype(F32)
        hat, inverse = standardize(x)
        row = lax.broadcasted_iota(jnp.int32, (chunk, SAMP), 0) + i * chunk
        column = lax.broadcasted_iota(jnp.int32, (chunk, SAMP), 1)
        spread = jnp.where(row == column * 16, 1.0, 0.0).astype(BF16)
        total = (grads[rows, 128:512].astype(F32) + nn(spread, returned[...])).astype(BF16)
        d = nt(grads[rows, 0:128], w_in[:, 0:128]) + nt(total, w_in[:, 128:512])
        d = d + nt(grads[rows, 512:640], w_in[:, 512:640])
        d = d * gain[...]
        mean = jnp.sum(d, axis=-1, keepdims=True) * (1.0 / C)
        along = jnp.sum(d * hat, axis=-1, keepdims=True) * (1.0 / C)
        feature_gradient[rows, :] = inverse * (d - mean - hat * along) + cot[rows, :].astype(F32)
        mixed = nn(grads[rows, 640:768], w_back[0:128, :]) + nn(grads[rows, 512:640], w_back[128:256, :])
        layer_out[rows, :] = (x + mixed).astype(BF16)
        return 0

    lax.fori_loop(0, PTS // chunk, part, 0)


def unpack_kernel(place, own, other, weights, gain_gradient, packed):
    mine = place[0]
    factor = (PTS * 256) ** (-0.5)
    packed[pl.ds(pl.multiple_of(mine * HALF, HALF), HALF), :] = own[...] * factor
    packed[pl.ds(pl.multiple_of((1 - mine) * HALF, HALF), HALF), :] = other[...] * factor
    for i, (tail, side) in enumerate(((960, 0), (768, 0), (768, 64), (960, 64))):
        weights[i, :, 0:128] = packed[192 * i:192 * (i + 1), :]
        weights[i, :, 128:C] = packed[tail:tail + 192, side:side + 64]
    gain_gradient[:, 0:128] = packed[1152:1153, :]
    gain_gradient[:, 128:C] = packed[1153:1154, 0:64]


def call(kernel, outs, specs, scratch=(), limit=48):
    return pl.pallas_call(
        kernel,
        out_shape=[jax.ShapeDtypeStruct(s, t) for s, t in outs],
        in_specs=specs,
        out_specs=[VMEM] * len(outs),
        scratch_shapes=[pltpu.VMEM(s, t) for s, t in scratch],
        compiler_params=pltpu.CompilerParams(vmem_limit_bytes=limit * 1024 * 1024),
    )


def moved(block, axes, count, distance):
    route = [(i - distance, i) for i in range(count) if 0 <= i - distance < count]
    return lax.ppermute(block, axes, route)


def extended(rows, axes, count):
    return jnp.concatenate([moved(rows, axes, count, 1), rows, moved(rows, axes, count, -1)], axis=0)


def reduced(keep, send):
    pair = [(0, 1), (1, 0)]
    x = keep + lax.ppermute(send, "c", pair)
    x = lax.all_to_all(x.reshape(16, HALF // 16, 128), XY, 0, 0, tiled=True).sum(0)
    x = jnp.broadcast_to(x[None], (8,) + x.shape)
    x = lax.all_to_all(x, "z", 0, 0, tiled=True).sum(0)
    x = jnp.broadcast_to(x[None], (16,) + x.shape)
    x = lax.all_to_all(x, XY, 0, 0, tiled=True).reshape(HALF, 128)
    return x, lax.ppermute(x, "c", pair)


def body(points, gain, w_query, w_key, w_value, w_out, lengths, picks, cotangent):
    points = points[0, 0]
    cotangent = cotangent[0, 0]
    lengths = lengths.reshape(NWIN)
    gain = gain.reshape(1, C)
    place = lax.axis_index("c").astype(jnp.int32).reshape(1)
    sample = points.reshape(SAMP, 16, C)[:, 0]
    across = extended(sample, GY, 4)
    near = extended(across.reshape(3 * SAMP, C), GX, 64)
    empty = jnp.zeros((C, 64), BF16)
    w_in = jnp.concatenate([w_query[:, :128], w_key[:, :128], w_value[:, :128], w_key[:, 128:],
                            w_value[:, 128:], w_query[:, 128:], empty], axis=1)
    w_back = jnp.concatenate([w_out[:128], empty.T, w_out[128:]], axis=0)
    big = (PAD, 128)
    qa, ka, va, da, kvb, qdb, xhat, normed_t, onehot, onehot_t = call(
        pre_kernel,
        [(big, F32)] * 6
        + [((PTS, C), F32), ((C, PTS), BF16), ((NWIN * WIN, NEAR), BF16), ((NEAR, NWIN * WIN), BF16)],
        [VMEM] * 7,
    )(points, gain, w_in, w_back, cotangent,
      picks.reshape(1, NWIN * WIN), picks.reshape(NWIN * WIN, 1))
    keep, send, d_near, grads = call(
        attend_kernel,
        [((HALF, 128), F32)] * 2 + [((NEAR, 2 * C), BF16), ((PTS, 6 * 128), BF16)],
        [SMEM, SMEM] + [VMEM] * 14,
        [((NEAR, C), F32), ((NEAR, C), BF16), ((NEAR, 2 * C), BF16)] + [((NWIN * WIN, 2 * C), BF16)] * 2
        + [(big, F32)] * 6 + [((ROWS, 128), F32)],
    )(lengths, place, near, gain, w_in, cotangent, qa, ka, va, da, kvb, qdb, xhat, normed_t,
      onehot, onehot_t)
    own, other = reduced(keep, send)
    d_near = d_near.reshape(3, 3, SAMP, 2 * C)
    upper = moved(d_near[:, 2], GY, 4, 1).astype(F32)
    lower = moved(d_near[:, 0], GY, 4, -1).astype(F32)
    partial_sum = d_near[:, 1].astype(F32) + upper + lower
    upper = moved(partial_sum[2].astype(BF16), GX, 64, 1).astype(F32)
    lower = moved(partial_sum[0].astype(BF16), GX, 64, -1).astype(F32)
    returned = (partial_sum[1] + upper + lower).astype(BF16)
    layer_out, feature_gradient = call(
        finish_kernel, [((PTS, C), BF16), ((PTS, C), F32)], [VMEM] * 7
    )(points, gain, w_in, w_back, cotangent, grads, returned)
    weights, gain_gradient = call(
        unpack_kernel, [((4, C, C), F32), ((1, C), F32)], [SMEM, VMEM, VMEM], [((ROWS, 128), F32)]
    )(place, own, other)
    return layer_out[None, None], feature_gradient[None, None], weights, gain_gradient.reshape(C)


def solution(mesh):
    inner = Mesh(mesh.devices.reshape(8, 4, 2, 2, 2), ("z", "y", "xl", "xh", "c"))
    return jax.shard_map(
        body,
        mesh=inner,
        in_specs=(P(GX, GY, None, None), P(), P(), P(), P(), P(), P(GX, GY, None),
                  P(GX, GY, None, None), P(GX, GY, None, None)),
        out_specs=(P(GX, GY, None, None), P(GX, GY, None, None), P(), P()),
        check_vma=False,
    )
```

time: 527 us -> 137 us (0.26)
  the two profiles are of different devices: /device:TPU:1 before, /device:TPU:122 now
where the time goes in v1:
time: 137 us; the launch traced here: 136 us
  Pallas kernels  40.4 us (29%)
  starting transfers between devices  37.7 us (28%)
  waiting for transfers between devices  23.7 us (17%)
  blocking collectives  15 us (11%)
  local copies, waits for them, and re-layouts  13.4 us (10%)
  other arithmetic  4.49 us (3%)
    pallas_call x1, Pallas kernels, body(): call(attend_kernel, [((HALF, 128), F32)] * 2 + [((NEAR, 2 * C), BF16), ((...  26.5 us
    ppermute x8, starting transfers between devices, moved(): return lax.ppermute(block, axes, route)  23 us
    ppermute x8, waiting for transfers between devices, moved(): return lax.ppermute(block, axes, route)  16.3 us
    all_to_all x1, blocking collectives, reduced(): lax.all_to_all(x.reshape(16, HALF // 16, 128), XY, 0, 0, tiled=True).sum(0)  15 us
    unnamed x25, local copies, waits for them, and re-layouts  8.57 us
    all_to_all x1, starting transfers between devices, reduced(): x = lax.all_to_all(x, XY, 0, 0, tiled=True).reshape(HALF, 128)  8.19 us
    pallas_call x1, Pallas kernels, body(): call(pre_kernel, [(big, F32)] * 6 + [((PTS, C), F32), ((C, PTS), BF16), (...  8.06 us
    all_to_all x1, starting transfers between devices, reduced(): x = lax.all_to_all(x, 'z', 0, 0, tiled=True).sum(0)  5.23 us
  transfers between devices with their start and end apart: 12, of which 5 were waited for; matrix products, arithmetic and copies ran while one was open for 10% of the time, Pallas kernels for 9%

profile of v1, /device:TPU:122, one launch (start us, length us, event | category | flops | bytes accessed | tf_op | source)
XLA Modules:
  0.0 135.7 jit_solution(12919191072718541953)
XLA Ops:
  0.7 1.2 copy.27
  2.0 1.3 collective-permute-start.1
  3.3 3.0 %collective-permute-start = (bf16[64,192]{1,0:T(8,128)(2,1)S(1)}, bf16[64,192]{1,0:T(8,128)(2,1)S(1)}, u32[]{:S(2)}, u32[]{:S(2)}) collective-permute-start(bf16[64,192]{1,0:T(8,128)(2,1)S(1)} %bitcast.67), channel_id=1, source_target_pairs={{0,1},{1,2},{2,3},{4,5},{5,6},{6,7},{8,9},{9,10},{10,11},{12,13},{... | collective-permute-start | bytes 73736 | tf_op jit(solution)/shard_map/ppermute | solution.py:254
  6.4 0.8 slice.54
  7.1 0.9 slice.53
  8.7 4.7 %collective-permute-start.2 = (bf16[192,192]{1,0:T(8,128)(2,1)}, bf16[192,192]{1,0:T(8,128)(2,1)}, u32[]{:S(2)}, u32[]{:S(2)}) collective-permute-start(bf16[192,192]{1,0:T(8,128)(2,1)} %pad_maximum_fusion.1), channel_id=1, source_target_pairs={{0,4},{4,8},{8,12},{12,16},{16,20},{20,24},{24,28},{28,32},{32,36}... | collective-permute-start | bytes 221192 | tf_op jit(solution)/shard_map/ppermute | solution.py:254
  14.8 8.1 %shard_map.120 = (f32[1088,128]{1,0:T(8,128)S(1)}, f32[1088,128]{1,0:T(8,128)S(1)}, f32[1088,128]{1,0:T(8,128)S(1)}, f32[1088,128]{1,0:T(8,128)S(1)}, f32[1088,1...) custom-call(bf16[1024,192]{1,0:T(8,128)(2,1)S(1)} %bitcast.53, ...), custom_call_target="tpu_custom_call" | custom-call | tf_op jit(solution)/shard_map/pallas_call | solution.py:286
  22.8 1.9 %collective-permute-start.3 = (bf16[192,192]{1,0:T(8,128)(2,1)}, bf16[192,192]{1,0:T(8,128)(2,1)S(1)}, u32[]{:S(2)}, u32[]{:S(2)}) collective-permute-start(bf16[192,192]{1,0:T(8,128)(2,1)} %pad_maximum_fusion.1), channel_id=1, source_target_pairs={{4,0},{8,4},{12,8},{16,12},{20,16},{24,20},{28,24},{32,28},{36,32}... | collective-permute-start | bytes 221192 | tf_op jit(solution)/shard_map/ppermute | solution.py:254
  24.7 0.9 constant_dynamic-update-slice_fusion.4
  25.7 8.1 %collective-permute-done.3 = bf16[192,192]{1,0:T(8,128)(2,1)S(1)} collective-permute-done((bf16[192,192]{1,0:T(8,128)(2,1)}, bf16[192,192]{1,0:T(8,128)(2,1)S(1)}, u32[]{:S(2)}, u32[]{:S(2)}) %collective-permute-start.3) | collective-permute-done | bytes 73760 | tf_op jit(solution)/shard_map/ppermute | solution.py:254
  33.8 26.5 %shard_map.121 = (f32[640,128]{1,0:T(8,128)S(1)}, f32[640,128]{1,0:T(8,128)S(1)}, bf16[576,384]{1,0:T(8,128)(2,1)S(1)}, bf16[1024,768]{1,0:T(8,128)(2,1)}) custom-call(s32[24]{0:T(128)S(1)} %bitcast.64, s32[1]{0:T(128)} %bitcast.4.place, bf16[576,192]{1,0:T(8,128)(2,1)S(1)} %constant_dynamic-update-slice_fusion.near_points, f32[1,192]{1,0:T(1,128)S(1)} %bitcast.62, ...), custom_call_target="tpu_custom_call" | custom-call | tf_op jit(solution)/shard_map/pallas_call | solution.py:293
  60.2 1.2 collective-permute-start.8
  61.5 1.3 collective-permute-done.8
  62.7 15.0 %all_to_all.15 = f32[16,40,128]{2,1,0:T(8,128)S(1)} all-to-all(f32[16,40,128]{2,1,0:T(8,128)S(1)} %bitcast.65), channel_id=1, replica_groups=mesh['z'=8,'y'=4,'xl'=2,'xh'=2,'c'=2] {'y','xl','xh'}, dimensions={0} | all-to-all | bytes 655360 | tf_op jit(solution)/shard_map/all_to_all | solution.py:264
  78.5 5.2 %all-to-all-start.1 = ((f32[8,40,128]{2,1,0:T(8,128)}), f32[8,40,128]{2,1,0:T(8,128)}, u32[]{:S(2)}, u32[]{:S(2)}) async-start(f32[8,40,128]{2,1,0:T(8,128)} %broadcast_in_dim.24), calls=%async_computation.1 | async-start | bytes 327680 | tf_op jit(solution)/shard_map/all_to_all | solution.py:266
  84.5 2.0 %collective-permute-start.4 = (bf16[3,64,384]{2,1,0:T(8,128)(2,1)}, bf16[3,64,384]{2,1,0:T(8,128)(2,1)}, u32[]{:S(2)}, u32[]{:S(2)}) collective-permute-start(bf16[3,64,384]{2,1,0:T(8,128)(2,1)} %get-tuple-element.54), channel_id=1, source_target_pairs={{0,1},{1,2},{2,3},{4,5},{5,6},{6,7},{8,9},{9,10},{10,11},{12,13},{... | collective-permute-start | bytes 442376 | tf_op jit(solution)/shard_map/ppermute | solution.py:254
  86.4 1.3 collective-permute-start.5
  87.7 2.1 %all-to-all-done.1 = f32[8,40,128]{2,1,0:T(8,128)} async-done(((f32[8,40,128]{2,1,0:T(8,128)}), f32[8,40,128]{2,1,0:T(8,128)}, u32[]{:S(2)}, u32[]{:S(2)}) %all-to-all-start.1) | async-done | bytes 163872 | tf_op jit(solution)/shard_map/all_to_all | solution.py:266
  89.8 0.9 reduce_sum.19
  91.5 8.2 %all-to-all-start.2 = ((f32[16,40,128]{2,1,0:T(8,128)}), f32[16,40,128]{2,1,0:T(8,128)S(1)}, u32[]{:S(2)}, u32[]{:S(2)}) async-start(f32[16,40,128]{2,1,0:T(8,128)} %broadcast_in_dim.25), calls=%async_computation.2 | async-start | bytes 655360 | tf_op jit(solution)/shard_map/all_to_all | solution.py:268
  99.7 1.8 %fusion.4 = (bf16[3,64,384]{2,1,0:T(8,128)(2,1)S(1)}, f32[3,64,384]{2,1,0:T(8,128)}) fusion(bf16[3,64,384]{2,1,0:T(8,128)(2,1)} %collective-permute-done.5, bf16[3,64,384]{2,1,0:T(8,128)(2,1)} %collective-permute-done.4, bf16[3,3,64,384]{3,2,1,0:T(8,128)(2,1)} %bitcast.60), kind=kLoop, calls=%fused_computation.19 | loop fusion | flops 442368 | bytes 884736 | tf_op jit(solution)/shard_map/convert.2
  101.6 4.0 %all-to-all-done.2 = f32[16,40,128]{2,1,0:T(8,128)S(1)} async-done(((f32[16,40,128]{2,1,0:T(8,128)}), f32[16,40,128]{2,1,0:T(8,128)S(1)}, u32[]{:S(2)}, u32[]{:S(2)}) %all-to-all-start.2) | async-done | bytes 327712 | tf_op jit(solution)/shard_map/all_to_all | solution.py:268
  105.5 7.0 %collective-permute-start.6 = (bf16[64,384]{1,0:T(8,128)(2,1)S(1)}, bf16[64,384]{1,0:T(8,128)(2,1)S(1)}, u32[]{:S(2)}, u32[]{:S(2)}) collective-permute-start(bf16[64,384]{1,0:T(8,128)(2,1)S(1)} %get-tuple-element.56), channel_id=1, source_target_pairs={{0,4},{4,8},{8,12},{12,16},{16,20},{20,24},{24,28},{28,32},{32,36}... | collective-permute-start | bytes 147464 | tf_op jit(solution)/shard_map/ppermute | solution.py:254
  112.5 1.9 %collective-permute-start.7 = (bf16[64,384]{1,0:T(8,128)(2,1)S(1)}, bf16[64,384]{1,0:T(8,128)(2,1)S(1)}, u32[]{:S(2)}, u32[]{:S(2)}) collective-permute-start(bf16[64,384]{1,0:T(8,128)(2,1)S(1)} %get-tuple-element.57), channel_id=1, source_target_pairs={{4,0},{8,4},{12,8},{16,12},{20,16},{24,20},{28,24},{32,28},{36,32}... | collective-permute-start | bytes 147464 | tf_op jit(solution)/shard_map/ppermute | solution.py:254
  114.5 8.3 %collective-permute-done.7 = bf16[64,384]{1,0:T(8,128)(2,1)S(1)} collective-permute-done((bf16[64,384]{1,0:T(8,128)(2,1)S(1)}, bf16[64,384]{1,0:T(8,128)(2,1)S(1)}, u32[]{:S(2)}, u32[]{:S(2)}) %collective-permute-start.7) | collective-permute-done | bytes 49184 | tf_op jit(solution)/shard_map/ppermute | solution.py:254
  122.7 0.9 fusion.3.returned
  123.7 3.8 %shard_map.122 = (bf16[1024,192]{1,0:T(8,128)(2,1)S(1)}, f32[1024,192]{1,0:T(8,128)S(1)}) custom-call(bf16[1024,192]{1,0:T(8,128)(2,1)S(1)} %bitcast.54, f32[1,192]{1,0:T(1,128)S(1)} %bitcast.63, bf16[192,640]{1,0:T(8,128)(2,1)S(1)} %concatenate.13.w_in, bf16[256,192]{1,0:T(8,128)(2,1)S(1)} %pad_maximum_fusion.w_back, bf16[1024,192]{1,0:T(8,128)(2,1)S(1)} %bitcast.51, ...), custom_call_target="tpu_custom_call" | custom-call | tf_op jit(solution)/shard_map/pallas_call | solution.py:309
  127.5 1.0 copy-done.1
  128.5 0.8 copy-done.2
  129.3 2.0 %copy.35 = bf16[1,1,1024,192]{2,3,1,0:T(8,128)(2,1)} copy(bf16[1,1,1024,192]{3,2,1,0:T(8,128)(2,1)} %bitcast.58) | data formatting | bytes 786432
  131.3 2.4 %copy.36 = f32[1,1,1024,192]{2,3,1,0:T(8,128)} copy(f32[1,1,1024,192]{3,2,1,0:T(8,128)} %bitcast.57) | data formatting | bytes 1572864
  133.7 2.0 %shard_map.123 = (f32[4,192,192]{2,1,0:T(8,128)}, f32[1,192]{1,0:T(1,128)}) custom-call(s32[1]{0:T(128)} %bitcast.4.place, f32[640,128]{1,0:T(8,128)S(1)} %bitcast.56, f32[640,128]{1,0:T(8,128)} %collective-permute-done.9.other), custom_call_target="tpu_custom_call" | custom-call | tf_op jit(solution)/shard_map/pallas_call | solution.py:312
  (55 shorter events, 4.3 us)
Async XLA Ops:
  0.6 12.8 %copy-start.7 = (s32[1,1,24,64]{3,2,1,0:T(8,128)S(1)}, s32[1,1,24,64]{3,2,1,0:T(8,128)}, u32[]{:S(2)}) copy-start(s32[1,1,24,64]{3,2,1,0:T(8,128)} %param.16) | copy-start | bytes 18436
  0.6 13.7 %copy-start.6 = (bf16[1,1,1024,192]{2,3,1,0:T(8,128)(2,1)S(1)}, bf16[1,1,1024,192]{2,3,1,0:T(8,128)(2,1)}, u32[]{:S(2)}) copy-start(bf16[1,1,1024,192]{2,3,1,0:T(8,128)(2,1)} %param.17) | copy-start | bytes 1179652
  1.9 12.6 %slice-start = ((bf16[192,192]{1,0:T(8,128)(2,1)}), bf16[192,64]{1,0:T(8,128)(2,1)S(1)}, s32[]{:S(2)}) async-start(bf16[192,192]{1,0:T(8,128)(2,1)} %param.11), calls=%async_computation.3 | async-start | bytes 98304 | tf_op jit(solution)/shard_map/slice | solution.py:283
  1.9 12.6 %slice-start.1 = ((bf16[192,192]{1,0:T(8,128)(2,1)}), bf16[192,128]{1,0:T(8,128)(2,1)S(1)}, s32[]{:S(2)}) async-start(bf16[192,192]{1,0:T(8,128)(2,1)} %param.11), calls=%async_computation.4 | async-start | bytes 98304 | tf_op jit(solution)/shard_map/slice | solution.py:282
  1.9 12.6 %slice-start.2 = ((bf16[192,192]{1,0:T(8,128)(2,1)}), bf16[192,64]{1,0:T(8,128)(2,1)S(1)}, s32[]{:S(2)}) async-start(bf16[192,192]{1,0:T(8,128)(2,1)} %param.12), calls=%async_computation.5 | async-start | bytes 98304 | tf_op jit(solution)/shard_map/slice | solution.py:282
  1.9 12.6 %slice-start.3 = ((bf16[192,192]{1,0:T(8,128)(2,1)}), bf16[192,128]{1,0:T(8,128)(2,1)S(1)}, s32[]{:S(2)}) async-start(bf16[192,192]{1,0:T(8,128)(2,1)} %param.12), calls=%async_computation.6 | async-start | bytes 98304 | tf_op jit(solution)/shard_map/slice | solution.py:282
  2.0 12.6 %slice-start.4 = ((bf16[192,192]{1,0:T(8,128)(2,1)}), bf16[192,64]{1,0:T(8,128)(2,1)S(1)}, s32[]{:S(2)}) async-start(bf16[192,192]{1,0:T(8,128)(2,1)} %param.13), calls=%async_computation.7 | async-start | bytes 98304 | tf_op jit(solution)/shard_map/slice | solution.py:283
  2.0 12.6 %slice-start.5 = ((bf16[192,192]{1,0:T(8,128)(2,1)}), bf16[192,128]{1,0:T(8,128)(2,1)S(1)}, s32[]{:S(2)}) async-start(bf16[192,192]{1,0:T(8,128)(2,1)} %param.13), calls=%async_computation.8 | async-start | bytes 98304 | tf_op jit(solution)/shard_map/slice | solution.py:282
  2.0 6.0 %collective-permute-start.1 = (bf16[64,192]{1,0:T(8,128)(2,1)S(1)}, bf16[64,192]{1,0:T(8,128)(2,1)S(1)}, u32[]{:S(2)}, u32[]{:S(2)}) collective-permute-start(bf16[64,192]{1,0:T(8,128)(2,1)S(1)} %bitcast.66), channel_id=1, source_target_pairs={{1,0},{2,1},{3,2},{5,4},{6,5},{7,6},{9,8},{10,9},{11,10},{13,12},{... | collective-permute-start | bytes 73736 | tf_op jit(solution)/shard_map/ppermute | solution.py:254
  3.3 4.7 %collective-permute-start = (bf16[64,192]{1,0:T(8,128)(2,1)S(1)}, bf16[64,192]{1,0:T(8,128)(2,1)S(1)}, u32[]{:S(2)}, u32[]{:S(2)}) collective-permute-start(bf16[64,192]{1,0:T(8,128)(2,1)S(1)} %bitcast.67), channel_id=1, source_target_pairs={{0,1},{1,2},{2,3},{4,5},{5,6},{6,7},{8,9},{9,10},{10,11},{12,13},{... | collective-permute-start | bytes 73736 | tf_op jit(solution)/shard_map/ppermute | solution.py:254
  7.1 7.6 %copy-start.4 = (f32[192]{0:T(256)S(1)}, f32[192]{0:T(256)}, u32[]{:S(2)}) copy-start(f32[192]{0:T(256)} %param.10) | copy-start | bytes 2308
  8.7 16.0 %collective-permute-start.2 = (bf16[192,192]{1,0:T(8,128)(2,1)}, bf16[192,192]{1,0:T(8,128)(2,1)}, u32[]{:S(2)}, u32[]{:S(2)}) collective-permute-start(bf16[192,192]{1,0:T(8,128)(2,1)} %pad_maximum_fusion.1), channel_id=1, source_target_pairs={{0,4},{4,8},{8,12},{12,16},{16,20},{20,24},{24,28},{28,32},{32,36}... | collective-permute-start | bytes 221192 | tf_op jit(solution)/shard_map/ppermute | solution.py:254
  14.5 19.2 %copy-start.5 = (s32[1,1,24]{2,1,0:T(1,128)S(1)}, s32[1,1,24]{2,1,0:T(1,128)}, u32[]{:S(2)}) copy-start(s32[1,1,24]{2,1,0:T(1,128)} %param.15) | copy-start | bytes 292
  22.8 10.9 %collective-permute-start.3 = (bf16[192,192]{1,0:T(8,128)(2,1)}, bf16[192,192]{1,0:T(8,128)(2,1)S(1)}, u32[]{:S(2)}, u32[]{:S(2)}) collective-permute-start(bf16[192,192]{1,0:T(8,128)(2,1)} %pad_maximum_fusion.1), channel_id=1, source_target_pairs={{4,0},{8,4},{12,8},{16,12},{20,16},{24,20},{28,24},{32,28},{36,32}... | collective-permute-start | bytes 221192 | tf_op jit(solution)/shard_map/ppermute | solution.py:254
  60.2 31.3 %copy-start.3 = (bf16[576,384]{1,0:T(8,128)(2,1)}, bf16[576,384]{1,0:T(8,128)(2,1)S(1)}, u32[]{:S(2)}) copy-start(bf16[576,384]{1,0:T(8,128)(2,1)S(1)} %get-tuple-element.33) | copy-start | bytes 1327108
  60.2 2.5 %collective-permute-start.8 = (f32[640,128]{1,0:T(8,128)S(1)}, f32[640,128]{1,0:T(8,128)S(1)}, u32[]{:S(2)}, u32[]{:S(2)}) collective-permute-start(f32[640,128]{1,0:T(8,128)S(1)} %get-tuple-element.37), channel_id=1, source_target_pairs={{0,1},{1,0},{2,3},{3,2},{4,5},{5,4},{6,7},{7,6},{8,9},{9,8},{10,11... | collective-permute-start | bytes 983048 | tf_op jit(solution)/shard_map/ppermute | solution.py:263
  78.5 45.2 %copy-start = (bf16[1024,768]{1,0:T(8,128)(2,1)S(1)}, bf16[1024,768]{1,0:T(8,128)(2,1)}, u32[]{:S(2)}) copy-start(bf16[1024,768]{1,0:T(8,128)(2,1)} %get-tuple-element.32.grads) | copy-start | bytes 4718596
  78.5 11.3 %all-to-all-start.1 = ((f32[8,40,128]{2,1,0:T(8,128)}), f32[8,40,128]{2,1,0:T(8,128)}, u32[]{:S(2)}, u32[]{:S(2)}) async-start(f32[8,40,128]{2,1,0:T(8,128)} %broadcast_in_dim.24), calls=%async_computation.1 | async-start | bytes 327680 | tf_op jit(solution)/shard_map/all_to_all | solution.py:266
  84.5 15.3 %collective-permute-start.4 = (bf16[3,64,384]{2,1,0:T(8,128)(2,1)}, bf16[3,64,384]{2,1,0:T(8,128)(2,1)}, u32[]{:S(2)}, u32[]{:S(2)}) collective-permute-start(bf16[3,64,384]{2,1,0:T(8,128)(2,1)} %get-tuple-element.54), channel_id=1, source_target_pairs={{0,1},{1,2},{2,3},{4,5},{5,6},{6,7},{8,9},{9,10},{10,11},{12,13},{... | collective-permute-start | bytes 442376 | tf_op jit(solution)/shard_map/ppermute | solution.py:254
  86.4 13.3 %collective-permute-start.5 = (bf16[3,64,384]{2,1,0:T(8,128)(2,1)}, bf16[3,64,384]{2,1,0:T(8,128)(2,1)}, u32[]{:S(2)}, u32[]{:S(2)}) collective-permute-start(bf16[3,64,384]{2,1,0:T(8,128)(2,1)} %get-tuple-element.55), channel_id=1, source_target_pairs={{1,0},{2,1},{3,2},{5,4},{6,5},{7,6},{9,8},{10,9},{11,10},{13,12},{... | collective-permute-start | bytes 442376 | tf_op jit(solution)/shard_map/ppermute | solution.py:254
  91.5 14.0 %all-to-all-start.2 = ((f32[16,40,128]{2,1,0:T(8,128)}), f32[16,40,128]{2,1,0:T(8,128)S(1)}, u32[]{:S(2)}, u32[]{:S(2)}) async-start(f32[16,40,128]{2,1,0:T(8,128)} %broadcast_in_dim.25), calls=%async_computation.2 | async-start | bytes 655360 | tf_op jit(solution)/shard_map/all_to_all | solution.py:268
  105.5 28.2 %collective-permute-start.9 = (f32[640,128]{1,0:T(8,128)S(1)}, f32[640,128]{1,0:T(8,128)}, u32[]{:S(2)}, u32[]{:S(2)}) collective-permute-start(f32[640,128]{1,0:T(8,128)S(1)} %bitcast.55), channel_id=1, source_target_pairs={{0,1},{1,0},{2,3},{3,2},{4,5},{5,4},{6,7},{7,6},{8,9},{9,8},{10,11... | collective-permute-start | bytes 983048 | tf_op jit(solution)/shard_map/ppermute | solution.py:269
  105.5 8.9 %collective-permute-start.6 = (bf16[64,384]{1,0:T(8,128)(2,1)S(1)}, bf16[64,384]{1,0:T(8,128)(2,1)S(1)}, u32[]{:S(2)}, u32[]{:S(2)}) collective-permute-start(bf16[64,384]{1,0:T(8,128)(2,1)S(1)} %get-tuple-element.56), channel_id=1, source_target_pairs={{0,4},{4,8},{8,12},{12,16},{16,20},{20,24},{24,28},{28,32},{32,36}... | collective-permute-start | bytes 147464 | tf_op jit(solution)/shard_map/ppermute | solution.py:254
  112.5 10.2 %collective-permute-start.7 = (bf16[64,384]{1,0:T(8,128)(2,1)S(1)}, bf16[64,384]{1,0:T(8,128)(2,1)S(1)}, u32[]{:S(2)}, u32[]{:S(2)}) collective-permute-start(bf16[64,384]{1,0:T(8,128)(2,1)S(1)} %get-tuple-element.57), channel_id=1, source_target_pairs={{4,0},{8,4},{12,8},{16,12},{20,16},{24,20},{28,24},{32,28},{36,32}... | collective-permute-start | bytes 147464 | tf_op jit(solution)/shard_map/ppermute | solution.py:254
  127.5 1.0 copy-start.1
  128.5 0.8 copy-start.2

commit v2 on v1

v2 whole, which is shorter than its diff:
```python
import jax
import jax.numpy as jnp
from jax import lax
from jax.experimental import pallas as pl
from jax.experimental.pallas import tpu as pltpu
from jax.sharding import Mesh, PartitionSpec as P

C = 192
H = 6
DEPTH = 32
PTS = 1024
WIN = 64
NWIN = 24
SAMP = 64
NEAR = 9 * SAMP
PAD = PTS + WIN
ROWS = 1280
CHUNK = ROWS // 32
GX = ("z", "y", "xl")
GY = ("xh", "c")
GROUP = ("c", "y", "xl", "xh")
SCALE = DEPTH ** (-0.5)
LOG2E = 1.4426950408889634
F32 = jnp.float32
BF16 = jnp.bfloat16
VMEM = pl.BlockSpec(memory_space=pltpu.VMEM)
SMEM = pl.BlockSpec(memory_space=pltpu.SMEM)
ANY = pl.BlockSpec(memory_space=pl.ANY)
UNROLL = 4


def nn(a, b):
    return lax.dot_general(a, b, (((1,), (0,)), ((), ())), preferred_element_type=F32)


def nt(a, b):
    return lax.dot_general(a, b, (((1,), (1,)), ((), ())), preferred_element_type=F32)


def tn(a, b):
    return lax.dot_general(a, b, (((0,), (0,)), ((), ())), preferred_element_type=F32)


def standardize(x, axis):
    mean = jnp.sum(x, axis=axis, keepdims=True) * (1.0 / C)
    centred = x - mean
    variance = jnp.sum(centred * centred, axis=axis, keepdims=True) * (1.0 / C)
    inverse = lax.rsqrt(variance + 1e-05)
    return centred * inverse, inverse


def sample_kernel(points, sample):
    row = lax.broadcasted_iota(jnp.int32, (SAMP, PTS), 0) * 16
    column = lax.broadcasted_iota(jnp.int32, (SAMP, PTS), 1)
    sample[...] = nt(jnp.where(row == column, 1.0, 0.0).astype(BF16), points[...]).astype(BF16)


def gain_column(gain):
    return jnp.broadcast_to(gain[...], (128, C)).T


def prepare_kernel(after, points, gain, wq, wk, wv, wo, cot, picks_row, picks_col,
                   qa, ka, va, da, kvb, qdb, normed_t, w_in, w_back, onehot, onehot_t):
    chunk = 128
    gain_t = gain_column(gain)
    empty = jnp.zeros((C, 64), BF16)
    back = wo[...].astype(F32).T.astype(BF16)
    w_in[:, 0:128] = wq[:, 0:128]
    w_in[:, 128:256] = wk[:, 0:128]
    w_in[:, 256:384] = wv[:, 0:128]
    w_in[:, 384:512] = jnp.concatenate([wk[:, 128:], wv[:, 128:]], axis=1)
    w_in[:, 512:640] = jnp.concatenate([wq[:, 128:], empty], axis=1)
    w_back[:, 0:128] = jnp.concatenate([empty, back[:, 128:]], axis=1)
    w_back[:, 128:256] = back[:, 0:128]

    def project(i, _):
        rows = pl.ds(pl.multiple_of(i * chunk, chunk), chunk)
        hat, _inv = standardize(points[:, rows].astype(F32), 0)
        normed = (hat * gain_t).astype(BF16)
        normed_t[:, rows] = normed
        wide = tn(normed, w_in[...])
        back = tn(cot[:, rows], w_back[...])
        for ref, x in ((qa, wide[:, :128]), (ka, wide[:, 128:256]), (va, wide[:, 256:384]),
                       (kvb, wide[:, 384:512]), (da, back[:, 128:]), (qdb, wide[:, 512:] + back[:, :128])):
            ref[rows, :] = x.astype(BF16).astype(F32)
        return 0

    lax.fori_loop(0, PTS // chunk, project, 0)
    zeros = jnp.zeros((WIN, 128), F32)
    for ref in (qa, ka, va, da, kvb, qdb):
        ref[PTS:, :] = zeros

    def rows_hot(i, _):
        rows = pl.ds(pl.multiple_of(i * WIN, WIN), WIN)
        ids = lax.broadcasted_iota(jnp.int32, (WIN, NEAR), 1)
        onehot[rows, :] = jnp.where(picks_col[rows, :] == ids, 1.0, 0.0).astype(BF16)
        return 0

    lax.fori_loop(0, NWIN, rows_hot, 0)

    def columns_hot(i, _):
        rows = pl.ds(pl.multiple_of(i * SAMP, SAMP), SAMP)
        ids = lax.broadcasted_iota(jnp.int32, (SAMP, NWIN * WIN), 0) + i * SAMP
        onehot_t[rows, :] = jnp.where(picks_row[...] == ids, 1.0, 0.0).astype(BF16)
        return 0

    lax.fori_loop(0, 9, columns_hot, 0)


def attend_kernel(lengths, low, middle, high, gain, w_in, qa, ka, va, da, kvb, qdb, onehot, onehot_t,
                  d_near, d_low, d_high, rest, grads, near_hat, near_normed,
                  near_kv, pick, d_pick, oa_s, dqa_s, dka_s, dva_s, dkvb_s, dqob_s):
    near_points = jnp.concatenate([low[...], middle[...], high[...]], axis=0)
    hat, _inv = standardize(near_points.astype(F32), 1)
    near_hat[...] = hat
    normed = (hat * gain[...]).astype(BF16)
    near_normed[...] = normed
    near_kv[...] = nn(normed, w_in[:, 128:512]).astype(BF16)

    def choose(i, _):
        rows = pl.ds(pl.multiple_of(i * 256, 256), 256)
        pick[rows, :] = nn(onehot[rows, :], near_kv[...]).astype(BF16)
        return 0

    lax.fori_loop(0, NWIN * WIN // 256, choose, 0)

    lane_head = lax.broadcasted_iota(jnp.int32, (1, 128), 1) // DEPTH
    lanes = [jnp.where(lane_head == h, 1.0, 0.0).astype(BF16) for h in range(4)]
    key_id = lax.broadcasted_iota(jnp.int32, (1, 128), 1)
    slot = lax.broadcasted_iota(jnp.int32, (WIN, 1), 0)
    half_scale = jnp.where(key_id < 64, SCALE, 1.0)

    def per_head(x):
        return jnp.concatenate([x * lane for lane in lanes], axis=0)

    def down(parts):
        return jnp.concatenate(parts, axis=0)

    def along(parts):
        return jnp.concatenate(parts, axis=1)

    def softmax(scores, bias):
        scores = scores + bias
        top = jnp.max(scores, axis=-1, keepdims=True)
        weights = jnp.exp2((scores - top) * (SCALE * LOG2E))
        return weights * (1.0 / jnp.sum(weights, axis=-1, keepdims=True))

    def score_gradient(probs, d_probs):
        d_probs = d_probs.astype(BF16).astype(F32)
        inner = jnp.sum(d_probs * probs, axis=-1, keepdims=True)
        return (probs * (d_probs - inner)).astype(BF16)

    def head(x, h):
        return x[:, 128 * h:128 * (h + 1)]

    def window(w, offset):
        count = lengths[w]
        rows = pl.ds(offset, WIN)
        own = pl.ds(pl.multiple_of(w * WIN, WIN), WIN)
        bias = jnp.where((key_id >= count) & (key_id < WIN), -1e30, 0.0)
        alive = slot < count
        keys = per_head(down([ka[rows, :].astype(BF16), pick[own, 0:128]]))
        values = per_head(down([va[rows, :].astype(BF16), pick[own, 128:256]]))
        both = per_head(down([kvb[rows, :].astype(BF16), pick[own, 256:384]]))
        q = qa[rows, :].astype(BF16)
        d = jnp.where(alive, da[rows, :], 0.0).astype(BF16)
        qd = jnp.where(alive, qdb[rows, :], 0.0).astype(BF16)
        scores = nt(q, keys)
        d_probs = nt(d, values)
        mixed = nt(qd, both)
        probs = [softmax(head(scores, h), bias) for h in range(4)]
        probs_b = [softmax(head(mixed, h), bias) for h in range(2)]
        probs16 = [p.astype(BF16) for p in probs]
        d_scores = [score_gradient(p, head(d_probs, h)) for h, p in enumerate(probs)]
        back = [score_gradient(p, head(mixed, 2 + h)) for h, p in enumerate(probs_b)]
        back = back + [p.astype(BF16) for p in probs_b]
        oa_s[rows, :] = nn(along(probs16), values)
        dqa_s[rows, :] = nn(along(d_scores), keys) * SCALE
        dqob_s[rows, :] = nn(along(back), both) * half_scale
        d_keys = tn(down(d_scores), per_head(q)) * SCALE
        d_values = tn(down(probs16), per_head(d))
        d_both = tn(down(back), per_head(qd)) * half_scale
        dka_s[rows, :] = d_keys[:WIN]
        dva_s[rows, :] = d_values[:WIN]
        dkvb_s[rows, :] = d_both[:WIN]
        d_pick[own, 0:128] = d_keys[WIN:].astype(BF16)
        d_pick[own, 128:256] = d_values[WIN:].astype(BF16)
        d_pick[own, 256:384] = d_both[WIN:].astype(BF16)
        return offset + count

    lax.fori_loop(0, NWIN, window, jnp.int32(0), unroll=UNROLL)

    near = nn(onehot_t[...], d_pick[...])
    near16 = near.astype(BF16)
    d_near[...] = near16
    for i in range(3):
        d_low[i] = near16[192 * i:192 * i + 64]
        d_high[i] = near16[192 * i + 128:192 * i + 192]
    rest[...] = (near - near16.astype(F32)).astype(BF16)
    for i, ref in enumerate((dqa_s, dka_s, dva_s, dkvb_s, dqob_s, oa_s)):
        grads[:, 128 * i:128 * (i + 1)] = ref[:PTS, :].astype(BF16)


def weights_kernel(points, cot, w_in, normed_t, grads, d_near, rest, near_hat, near_normed, packed):
    wide = nn(normed_t[...], grads[:, 0:640])
    near_wide = tn(near_normed[...], d_near[...]) + tn(near_normed[...], rest[...])
    out = nn(cot[...], grads[:, 512:768])
    packed[0:192, :] = wide[:, 0:128]
    packed[192:384, :] = wide[:, 128:256] + near_wide[:, 0:128]
    packed[384:576, :] = wide[:, 256:384] + near_wide[:, 128:256]
    packed[576:768, :] = out[:, 128:256]
    packed[768:960, :] = wide[:, 384:512] + near_wide[:, 256:384]
    lane = lax.broadcasted_iota(jnp.int32, (C, 128), 1)
    packed[960:1152, :] = jnp.where(lane < 64, wide[:, 512:640], out[:, 0:128])

    def gain_part(i, total):
        rows = pl.ds(pl.multiple_of(i * 128, 128), 128)
        hat, _inv = standardize(points[:, rows].astype(F32), 0)
        return total + nt(w_in[...], grads[rows, 0:640]) * hat

    total = lax.fori_loop(0, PTS // 128, gain_part, jnp.zeros((C, 128), F32))
    w_kv = w_in[:, 128:512]
    d = nt(d_near[...], w_kv) + nt(rest[...], w_kv)
    near_total = jnp.sum((d * near_hat[...]).reshape(NEAR // 8, 8, C), axis=0)
    gain_sum = jnp.sum(total.T, axis=0, keepdims=True) + jnp.sum(near_total, axis=0, keepdims=True)
    packed[1152:, :] = jnp.zeros((ROWS - 1152, 128), F32)
    packed[1152:1153, :] = gain_sum[:, :128]
    packed[1153:1154, 0:64] = gain_sum[:, 128:]


def sides_kernel(d_near, upper, lower, up, down, middle):
    def side(i):
        own = d_near[192 * i + 64:192 * i + 128, :].astype(F32)
        return own + upper[i].astype(F32) + lower[i].astype(F32)

    up[...] = side(2).astype(BF16)
    down[...] = side(0).astype(BF16)
    middle[...] = side(1)


def fold_kernel(upper, lower, parts, out):
    total = parts[0]
    for i in range(1, parts.shape[0]):
        total = total + parts[i]
    for i in range(out.shape[0]):
        out[i] = total


def finish_kernel(points, gain, w_in, w_back, cot, grads, middle, upper, lower,
                  layer_out, feature_gradient, token, returned):
    token[...] = jnp.zeros(token.shape, F32)
    chunk = 128
    returned[...] = (middle[...] + upper[...].astype(F32) + lower[...].astype(F32)).astype(BF16)
    gain_t = gain_column(gain)

    def part(i, _):
        rows = pl.ds(pl.multiple_of(i * chunk, chunk), chunk)
        x = points[:, rows].astype(F32)
        hat, inverse = standardize(x, 0)
        row = lax.broadcasted_iota(jnp.int32, (chunk, SAMP), 0) + i * chunk
        column = lax.broadcasted_iota(jnp.int32, (chunk, SAMP), 1)
        spread = jnp.where(row == column * 16, 1.0, 0.0).astype(BF16)
        total = (grads[rows, 128:512].astype(F32) + nn(spread, returned[...])).astype(BF16)
        d = nt(w_in[:, 0:128], grads[rows, 0:128]) + nt(w_in[:, 128:512], total)
        d = d + nt(w_in[:, 512:640], grads[rows, 512:640])
        d = d * gain_t
        mean = jnp.sum(d, axis=0, keepdims=True) * (1.0 / C)
        along = jnp.sum(d * hat, axis=0, keepdims=True) * (1.0 / C)
        feature_gradient[:, rows] = inverse * (d - mean - hat * along) + cot[:, rows].astype(F32)
        layer_out[:, rows] = (x + nt(w_back[...], grads[rows, 512:768])).astype(BF16)
        return 0

    lax.fori_loop(0, PTS // chunk, part, 0)


def unpack_kernel(after, gathered, weights, gain_gradient, packed):
    packed[...] = gathered[...] * (PTS * 256) ** (-0.5)
    for i, (tail, side) in enumerate(((960, 0), (768, 0), (768, 64))):
        weights[i, :, 0:128] = packed[192 * i:192 * (i + 1), :]
        weights[i, :, 128:C] = packed[tail:tail + 192, side:side + 64]
    weights[3, 0:128, :] = packed[576:768, :].T
    weights[3, 128:C, :] = packed[960:1152, :].T[64:128, :]
    gain_gradient[:, 0:128] = packed[1152:1153, :]
    gain_gradient[:, 128:C] = packed[1153:1154, 0:64]


def call(kernel, outs, specs, scratch=(), limit=24, micros=1.0):
    return pl.pallas_call(
        kernel,
        out_shape=[jax.ShapeDtypeStruct(s, t) for s, t in outs],
        in_specs=specs,
        out_specs=[VMEM] * len(outs),
        scratch_shapes=[pltpu.VMEM(s, t) for s, t in scratch],
        cost_estimate=pl.CostEstimate(flops=int(micros * 1e9), bytes_accessed=int(micros * 3e6), transcendentals=0),
        compiler_params=pltpu.CompilerParams(vmem_limit_bytes=limit * 1024 * 1024),
    )


def moved(block, axes, count, distance):
    route = [(i, (i + distance) % count) for i in range(count)]
    return lax.ppermute(block, axes, route)


def extended(rows, axes, count):
    return jnp.concatenate([moved(rows, axes, count, 1), rows, moved(rows, axes, count, -1)], axis=0)


def exchanged(x, axes):
    return lax.all_to_all(x, axes, 0, 0, tiled=True)


def local_prepare(after, points, gain, w_query, w_key, w_value, w_out, cotangent, picks):
    big = ((PAD, 128), F32)
    outs = [big] * 6 + [((C, PTS), BF16), ((C, 640), BF16), ((C, 256), BF16)]
    outs = outs + [((NWIN * WIN, NEAR), BF16), ((NEAR, NWIN * WIN), BF16)]
    return call(prepare_kernel, outs, [ANY] + [VMEM] * 9, limit=24, micros=5.0)(
        after, points, gain.reshape(1, C), w_query, w_key, w_value, w_out, cotangent,
        picks.reshape(1, NWIN * WIN), picks.reshape(NWIN * WIN, 1))


def local_attend(lengths, near, gain, w_in, projections, hots):
    big = ((PAD, 128), F32)
    near_out = ((NEAR, 2 * C), BF16)
    return call(
        attend_kernel,
        [near_out] + [((3, SAMP, 2 * C), BF16)] * 2 + [near_out, ((PTS, 6 * 128), BF16), ((NEAR, C), F32), ((NEAR, C), BF16)],
        [SMEM] + [VMEM] * 13,
        [near_out] + [((NWIN * WIN, 2 * C), BF16)] * 2 + [big] * 6,
        limit=26, micros=18.0,
    )(lengths, *near, gain.reshape(1, C), w_in, *projections, *hots)


def local_weights(points, cotangent, w_in, normed_t, grads, d_near, rest, near_hat, near_normed):
    return call(
        weights_kernel, [((ROWS, 128), F32)], [VMEM] * 9, limit=14, micros=3.0
    )(points, cotangent, w_in, normed_t, grads, d_near, rest, near_hat, near_normed)[0]


def local_finish(points, gain, w_in, w_back, cotangent, grads, middle, upper, lower):
    outs = [((C, PTS), BF16), ((C, PTS), F32), ((8, 128), F32)]
    return call(finish_kernel, outs, [VMEM] * 9, [((SAMP, 2 * C), BF16)], limit=12, micros=4.0)(
        points, gain.reshape(1, C), w_in, w_back, cotangent, grads, middle, upper, lower)


def local_sides(d_near, upper, lower):
    outs = [((SAMP, 2 * C), BF16)] * 2 + [((SAMP, 2 * C), F32)]
    return call(sides_kernel, outs, [VMEM] * 3, limit=6)(d_near, upper, lower)


def local_fold(upper, lower, parts, copies):
    outs = [((copies,) + parts.shape[1:], F32)]
    return call(fold_kernel, outs, [ANY, ANY, VMEM], limit=6)(upper, lower, parts)[0]


def local_unpack(after, gathered):
    return call(
        unpack_kernel, [((4, C, C), F32), ((1, C), F32)], [ANY, VMEM], [((ROWS, 128), F32)],
        limit=8, micros=1.0,
    )(after, gathered)


def body(points, gain, w_query, w_key, w_value, w_out, lengths, picks, cotangent):
    points = points[0, 0].T
    cotangent = cotangent[0, 0].T
    lengths = lengths.reshape(NWIN)
    sample = call(sample_kernel, [((SAMP, C), BF16)], [VMEM], limit=6)(points)[0]
    across = extended(sample, GY, 4)
    near = (moved(across, GX, 64, 1), across, moved(across, GX, 64, -1))
    *projections, normed_t, w_in, w_back, onehot, onehot_t = local_prepare(
        across, points, gain, w_query, w_key, w_value, w_out, cotangent, picks)
    hots = (onehot, onehot_t)
    d_near, d_low, d_high, rest, grads, near_hat, near_normed = local_attend(
        lengths, near, gain, w_in, projections, hots)
    upper = moved(d_high, GY, 4, 1)
    lower = moved(d_low, GY, 4, -1)
    packed = local_weights(points, cotangent, w_in, normed_t, grads, d_near, rest, near_hat, near_normed)
    mixed = exchanged(packed.reshape(32, CHUNK, 128), GROUP)
    mixed = exchanged(local_fold(upper, lower, mixed, 8), "z")
    up, down, middle = local_sides(d_near, upper, lower)
    upper = moved(up, GX, 64, 1)
    lower = moved(down, GX, 64, -1)
    gathered = exchanged(local_fold(upper, lower, mixed, 32), GROUP).reshape(ROWS, 128)
    layer_out, feature_gradient, token = local_finish(
        points, gain, w_in, w_back, cotangent, grads, middle, upper, lower)
    weights, gain_gradient = local_unpack(token, gathered)
    return layer_out.T[None, None], feature_gradient.T[None, None], weights, gain_gradient.reshape(C)


def solution(mesh):
    inner = Mesh(mesh.devices.reshape(8, 4, 2, 2, 2), ("z", "y", "xl", "xh", "c"))
    return jax.shard_map(
        body,
        mesh=inner,
        in_specs=(P(GX, GY, None, None), P(), P(), P(), P(), P(), P(GX, GY, None),
                  P(GX, GY, None, None), P(GX, GY, None, None)),
        out_specs=(P(GX, GY, None, None), P(GX, GY, None, None), P(), P()),
        check_vma=False,
    )
```

time: 137 us -> 104 us (0.76)
  the two profiles are of different devices: /device:TPU:122 before, /device:TPU:1 now
where the time goes in v2:
time: 104 us; the launch traced here: 103 us
  starting transfers between devices  39.3 us (38%)
  Pallas kernels  35.1 us (34%)
  waiting for transfers between devices  24.6 us (24%)
  local copies, waits for them, and re-layouts  3.24 us (3%)
    ppermute x8, starting transfers between devices, moved(): return lax.ppermute(block, axes, route)  22.1 us
    pallas_call x1, Pallas kernels, local_attend(): call(attend_kernel, [near_out] + [((3, SAMP, 2 * C), BF16)] * 2 + [near_o...  18.3 us
    ppermute x8, waiting for transfers between devices, moved(): return lax.ppermute(block, axes, route)  17.4 us
    all_to_all x3, starting transfers between devices, exchanged(): return lax.all_to_all(x, axes, 0, 0, tiled=True)  17.2 us
    all_to_all x3, waiting for transfers between devices, exchanged(): return lax.all_to_all(x, axes, 0, 0, tiled=True)  7.22 us
    pallas_call x1, Pallas kernels, local_prepare(): call(prepare_kernel, outs, [ANY] + [VMEM] * 9, limit=24, micros=5.0)  5.3 us
    pallas_call x1, Pallas kernels, local_finish(): call(finish_kernel, outs, [VMEM] * 9, [((SAMP, 2 * C), BF16)], limit=12,...  4.48 us
    pallas_call x1, Pallas kernels, local_weights(): call(weights_kernel, [((ROWS, 128), F32)], [VMEM] * 9, limit=14, micros=3.0)  4.07 us
  transfers between devices with their start and end apart: 11, of which 6 were waited for; matrix products, arithmetic and copies ran while one was open for 1% of the time, Pallas kernels for 10%

profile of v2, /device:TPU:1, one launch (start us, length us, event | category | flops | bytes accessed | tf_op | source)
XLA Modules:
  0.0 103.2 jit_solution(16769081146182183244)
XLA Ops:
  0.6 1.0 copy-done
  1.7 0.2 shard_map.120
  1.9 3.3 %collective-permute-start.1 = (bf16[64,192]{1,0:T(8,128)(2,1)S(1)}, bf16[64,192]{1,0:T(8,128)(2,1)S(1)}, u32[]{:S(2)}, u32[]{:S(2)}) collective-permute-start(bf16[64,192]{1,0:T(8,128)(2,1)S(1)} %shard_map.120), channel_id=1, source_target_pairs={{0,3},{1,0},{2,1},{3,2},{4,7},{5,4},{6,5},{7,6},{8,11},{9,8},{10,9... | collective-permute-start | bytes 73736 | tf_op jit(solution)/shard_map/ppermute | solution.py:301
  5.2 1.0 collective-permute-start
  6.2 0.1 reshape.32.picks_row
  6.3 0.7 reshape.38.picks_col
  7.1 0.7 collective-permute-done.1
  7.7 0.0 collective-permute-done
  7.8 9.0 %collective-permute-start.3 = (bf16[192,192]{1,0:T(8,128)(2,1)S(1)}, bf16[192,192]{1,0:T(8,128)(2,1)S(1)}, u32[]{:S(2)}, u32[]{:S(2)}) collective-permute-start(bf16[192,192]{1,0:T(8,128)(2,1)S(1)} %pad_maximum_fusion.after.middle), channel_id=1, source_target_pairs={{0,252},{4,0},{8,4},{12,8},{16,12},{20,16},{24,20},{28,24},{32,28}... | collective-permute-start | bytes 221192 | tf_op jit(solution)/shard_map/ppermute | solution.py:301
  16.7 0.0 collective-permute-start.2
  16.8 0.0 copy-start.8
  16.8 5.3 %shard_map.121 = (f32[1088,128]{1,0:T(8,128)S(1)}, f32[1088,128]{1,0:T(8,128)S(1)}, f32[1088,128]{1,0:T(8,128)S(1)}, f32[1088,128]{1,0:T(8,128)S(1)}, f32[1088,1...) custom-call(bf16[192,192]{1,0:T(8,128)(2,1)S(1)} %pad_maximum_fusion, ...), custom_call_target="tpu_custom_call" | custom-call | flops 5000000000 | bytes 15000000 | tf_op jit(solution)/shard_map/pallas_call | solution.py:316
  22.1 2.3 %collective-permute-done.2.low = bf16[192,192]{1,0:T(8,128)(2,1)S(1)} collective-permute-done((bf16[192,192]{1,0:T(8,128)(2,1)S(1)}, bf16[192,192]{1,0:T(8,128)(2,1)S(1)}, u32[]{:S(2)}, u32[]{:S(2)}) %collective-permute-start.2) | collective-permute-done | bytes 73760 | tf_op jit(solution)/shard_map/ppermute | solution.py:301
  24.4 18.3 %shard_map.122 = (bf16[576,384]{1,0:T(8,128)(2,1)S(1)}, bf16[3,64,384]{2,1,0:T(8,128)(2,1)S(1)}, bf16[3,64,384]{2,1,0:T(8,128)(2,1)S(1)}, bf16[576,384]{1,0:T(8,...) custom-call(s32[24]{0:T(128)S(1)} %bitcast.32, ...), custom_call_target="tpu_custom_call" | custom-call | flops 17999998976 | bytes 54000000 | tf_op jit(solution)/shard_map/pallas_call | solution.py:324
  42.7 4.1 %shard_map.125 = f32[1280,128]{1,0:T(8,128)} custom-call(bf16[192,1024]{1,0:T(8,128)(2,1)S(1)} %bitcast.24, bf16[192,1024]{1,0:T(8,128)(2,1)S(1)} %bitcast.27, bf16[192,640]{1,0:T(8,128)(2,1)S(1)} %get-tuple-element.30.w_in, bf16[192,1024]{1,0:T(8,128)(2,1)S(1)} %get-tuple-element.50.normed_t, bf16[1024,768]{1,0:T(8,128)(2,1)S(1)} %get-tuple-element.40.grads, ...), custom_call_target="tpu_custom_call" | custom-call | flops 3000000000 | bytes 9000000 | tf_op jit(solution)/shard_map/pallas_call | solution.py:334
  46.8 7.3 %all-to-all-start = ((f32[32,40,128]{2,1,0:T(8,128)}), f32[32,40,128]{2,1,0:T(8,128)S(1)}, u32[]{:S(2)}, u32[]{:S(2)}) async-start(f32[32,40,128]{2,1,0:T(8,128)} %bitcast.12), calls=%async_computation | async-start | bytes 1310720 | tf_op jit(solution)/shard_map/all_to_all | solution.py:309
  54.1 3.1 %collective-permute-start.4 = (bf16[3,64,384]{2,1,0:T(8,128)(2,1)S(1)}, bf16[3,64,384]{2,1,0:T(8,128)(2,1)S(1)}, u32[]{:S(2)}, u32[]{:S(2)}) collective-permute-start(bf16[3,64,384]{2,1,0:T(8,128)(2,1)S(1)} %get-tuple-element.42), channel_id=1, source_target_pairs={{0,1},{1,2},{2,3},{3,0},{4,5},{5,6},{6,7},{7,4},{8,9},{9,10},{10,1... | collective-permute-start | bytes 442376 | tf_op jit(solution)/shard_map/ppermute | solution.py:301
  57.3 7.4 %collective-permute-done.4.upper = bf16[3,64,384]{2,1,0:T(8,128)(2,1)S(1)} collective-permute-done((bf16[3,64,384]{2,1,0:T(8,128)(2,1)S(1)}, bf16[3,64,384]{2,1,0:T(8,128)(2,1)S(1)}, u32[]{:S(2)}, u32[]{:S(2)}) %collective-permute-start.4) | collective-permute-done | bytes 147488 | tf_op jit(solution)/shard_map/ppermute | solution.py:301
  64.6 3.6 %collective-permute-done.5.lower = bf16[3,64,384]{2,1,0:T(8,128)(2,1)S(1)} collective-permute-done((bf16[3,64,384]{2,1,0:T(8,128)(2,1)S(1)}, bf16[3,64,384]{2,1,0:T(8,128)(2,1)S(1)}, u32[]{:S(2)}, u32[]{:S(2)}) %collective-permute-start.5) | collective-permute-done | bytes 147488 | tf_op jit(solution)/shard_map/ppermute | solution.py:301
  68.2 0.7 shard_map.126
  69.0 3.4 %all-to-all-start.1 = ((f32[8,40,128]{2,1,0:T(8,128)}), f32[8,40,128]{2,1,0:T(8,128)S(1)}, u32[]{:S(2)}, u32[]{:S(2)}) async-start(f32[8,40,128]{2,1,0:T(8,128)} %shard_map.126), calls=%async_computation.1 | async-start | bytes 327680 | tf_op jit(solution)/shard_map/all_to_all | solution.py:309
  72.4 0.1 shard_map.123
  72.4 0.4 collective-permute-start.6
  72.8 5.4 %collective-permute-start.7 = (bf16[64,384]{1,0:T(8,128)(2,1)S(1)}, bf16[64,384]{1,0:T(8,128)(2,1)S(1)}, u32[]{:S(2)}, u32[]{:S(2)}) collective-permute-start(bf16[64,384]{1,0:T(8,128)(2,1)S(1)} %get-tuple-element.46), channel_id=1, source_target_pairs={{0,252},{4,0},{8,4},{12,8},{16,12},{20,16},{24,20},{28,24},{32,28}... | collective-permute-start | bytes 147464 | tf_op jit(solution)/shard_map/ppermute | solution.py:301
  78.2 3.5 %collective-permute-done.6.upper = bf16[64,384]{1,0:T(8,128)(2,1)S(1)} collective-permute-done((bf16[64,384]{1,0:T(8,128)(2,1)S(1)}, bf16[64,384]{1,0:T(8,128)(2,1)S(1)}, u32[]{:S(2)}, u32[]{:S(2)}) %collective-permute-start.6) | collective-permute-done | bytes 49184 | tf_op jit(solution)/shard_map/ppermute | solution.py:301
  81.6 0.0 all-to-all-done.1.parts
  81.6 0.9 shard_map.127
  82.5 6.5 %all-to-all-start.2 = ((f32[32,40,128]{2,1,0:T(8,128)}), f32[32,40,128]{2,1,0:T(8,128)S(1)}, u32[]{:S(2)}, u32[]{:S(2)}) async-start(f32[32,40,128]{2,1,0:T(8,128)} %shard_map.127), calls=%async_computation.2 | async-start | bytes 1310720 | tf_op jit(solution)/shard_map/all_to_all | solution.py:309
  89.0 1.4 %copy-done.10 = bf16[1024,768]{1,0:T(8,128)(2,1)S(1)} copy-done((bf16[1024,768]{1,0:T(8,128)(2,1)S(1)}, bf16[1024,768]{1,0:T(8,128)(2,1)}, u32[]{:S(2)}) %copy-start.10) | copy-done | bytes 1572888
  90.4 4.5 %shard_map.124 = (bf16[192,1024]{1,0:T(8,128)(2,1)}, f32[192,1024]{1,0:T(8,128)}, f32[8,128]{1,0:T(8,128)S(1)}) custom-call(bf16[192,1024]{1,0:T(8,128)(2,1)S(1)} %bitcast.25, f32[1,192]{1,0:T(1,128)S(1)} %bitcast.31, bf16[192,640]{1,0:T(8,128)(2,1)S(1)} %get-tuple-element.30.w_in, bf16[192,256]{1,0:T(8,128)(2,1)S(1)} %get-tuple-element.31.w_back, ...), custom_call_target="tpu_custom_call" | custom-call | flops 4000000000 | bytes 12000000 | tf_op jit(solution)/shard_map/pallas_call | solution.py:341
  94.9 7.2 %all-to-all-done.2 = f32[32,40,128]{2,1,0:T(8,128)S(1)} async-done(((f32[32,40,128]{2,1,0:T(8,128)}), f32[32,40,128]{2,1,0:T(8,128)S(1)}, u32[]{:S(2)}, u32[]{:S(2)}) %all-to-all-start.2) | async-done | bytes 655392 | tf_op jit(solution)/shard_map/all_to_all | solution.py:309
  102.1 1.1 %shard_map.128 = (f32[4,192,192]{2,1,0:T(8,128)}, f32[1,192]{1,0:T(1,128)}) custom-call(f32[8,128]{1,0:T(8,128)S(1)} %get-tuple-element.49.after, f32[1280,128]{1,0:T(8,128)S(1)} %bitcast.21), custom_call_target="tpu_custom_call" | custom-call | flops 1000000000 | bytes 3000000 | tf_op jit(solution)/shard_map/pallas_call | solution.py:356
  (26 shorter events, 0.1 us)
Async XLA Ops:
  0.6 1.0 copy-start
  1.6 4.6 %copy-start.11 = (s32[1,1,24,64]{3,2,1,0:T(8,128)S(1)}, s32[1,1,24,64]{3,2,1,0:T(8,128)}, u32[]{:S(2)}) copy-start(s32[1,1,24,64]{3,2,1,0:T(8,128)} %param.16) | copy-start | bytes 18436
  1.6 15.1 %copy-start.1 = (bf16[1,1,1024,192]{2,3,1,0:T(8,128)(2,1)S(1)}, bf16[1,1,1024,192]{2,3,1,0:T(8,128)(2,1)}, u32[]{:S(2)}) copy-start(bf16[1,1,1024,192]{2,3,1,0:T(8,128)(2,1)} %param.9) | copy-start | bytes 1179652
  1.6 15.1 %copy-start.2 = (bf16[1,1,1024,192]{2,3,1,0:T(8,128)(2,1)S(1)}, bf16[1,1,1024,192]{2,3,1,0:T(8,128)(2,1)}, u32[]{:S(2)}) copy-start(bf16[1,1,1024,192]{2,3,1,0:T(8,128)(2,1)} %param.17) | copy-start | bytes 1179652
  1.6 15.1 %copy-start.3 = (bf16[192,192]{1,0:T(8,128)(2,1)S(1)}, bf16[192,192]{1,0:T(8,128)(2,1)}, u32[]{:S(2)}) copy-start(bf16[192,192]{1,0:T(8,128)(2,1)} %wq.1) | copy-start | bytes 221188
  1.6 15.1 %copy-start.4 = (bf16[192,192]{1,0:T(8,128)(2,1)S(1)}, bf16[192,192]{1,0:T(8,128)(2,1)}, u32[]{:S(2)}) copy-start(bf16[192,192]{1,0:T(8,128)(2,1)} %wk.1) | copy-start | bytes 221188
  1.7 15.1 %copy-start.5 = (bf16[192,192]{1,0:T(8,128)(2,1)S(1)}, bf16[192,192]{1,0:T(8,128)(2,1)}, u32[]{:S(2)}) copy-start(bf16[192,192]{1,0:T(8,128)(2,1)} %wv.1) | copy-start | bytes 221188
  1.7 15.1 %copy-start.6 = (bf16[192,192]{1,0:T(8,128)(2,1)S(1)}, bf16[192,192]{1,0:T(8,128)(2,1)}, u32[]{:S(2)}) copy-start(bf16[192,192]{1,0:T(8,128)(2,1)} %wo.1) | copy-start | bytes 221188
  1.7 15.1 %copy-start.7 = (f32[192]{0:T(256)S(1)}, f32[192]{0:T(256)}, u32[]{:S(2)}) copy-start(f32[192]{0:T(256)} %param.10) | copy-start | bytes 2308
  1.9 5.8 %collective-permute-start.1 = (bf16[64,192]{1,0:T(8,128)(2,1)S(1)}, bf16[64,192]{1,0:T(8,128)(2,1)S(1)}, u32[]{:S(2)}, u32[]{:S(2)}) collective-permute-start(bf16[64,192]{1,0:T(8,128)(2,1)S(1)} %shard_map.120), channel_id=1, source_target_pairs={{0,3},{1,0},{2,1},{3,2},{4,7},{5,4},{6,5},{7,6},{8,11},{9,8},{10,9... | collective-permute-start | bytes 73736 | tf_op jit(solution)/shard_map/ppermute | solution.py:301
  5.2 2.5 %collective-permute-start = (bf16[64,192]{1,0:T(8,128)(2,1)S(1)}, bf16[64,192]{1,0:T(8,128)(2,1)S(1)}, u32[]{:S(2)}, u32[]{:S(2)}) collective-permute-start(bf16[64,192]{1,0:T(8,128)(2,1)S(1)} %shard_map.120), channel_id=1, source_target_pairs={{0,1},{1,2},{2,3},{3,0},{4,5},{5,6},{6,7},{7,4},{8,9},{9,10},{10,1... | collective-permute-start | bytes 73736 | tf_op jit(solution)/shard_map/ppermute | solution.py:301
  7.8 14.4 %collective-permute-start.3 = (bf16[192,192]{1,0:T(8,128)(2,1)S(1)}, bf16[192,192]{1,0:T(8,128)(2,1)S(1)}, u32[]{:S(2)}, u32[]{:S(2)}) collective-permute-start(bf16[192,192]{1,0:T(8,128)(2,1)S(1)} %pad_maximum_fusion.after.middle), channel_id=1, source_target_pairs={{0,252},{4,0},{8,4},{12,8},{16,12},{20,16},{24,20},{28,24},{32,28}... | collective-permute-start | bytes 221192 | tf_op jit(solution)/shard_map/ppermute | solution.py:301
  16.7 7.7 %collective-permute-start.2 = (bf16[192,192]{1,0:T(8,128)(2,1)S(1)}, bf16[192,192]{1,0:T(8,128)(2,1)S(1)}, u32[]{:S(2)}, u32[]{:S(2)}) collective-permute-start(bf16[192,192]{1,0:T(8,128)(2,1)S(1)} %pad_maximum_fusion.after.middle), channel_id=1, source_target_pairs={{0,4},{4,8},{8,12},{12,16},{16,20},{20,24},{24,28},{28,32},{32,36}... | collective-permute-start | bytes 221192 | tf_op jit(solution)/shard_map/ppermute | solution.py:301
  16.8 7.6 %copy-start.8 = (s32[1,1,24]{2,1,0:T(1,128)S(1)}, s32[1,1,24]{2,1,0:T(1,128)}, u32[]{:S(2)}) copy-start(s32[1,1,24]{2,1,0:T(1,128)} %param.15) | copy-start | bytes 292
  42.7 4.1 %copy-start.9 = (bf16[1024,768]{1,0:T(8,128)(2,1)}, bf16[1024,768]{1,0:T(8,128)(2,1)S(1)}, u32[]{:S(2)}) copy-start(bf16[1024,768]{1,0:T(8,128)(2,1)S(1)} %get-tuple-element.40.grads) | copy-start | bytes 4718596
  46.8 21.4 %all-to-all-start = ((f32[32,40,128]{2,1,0:T(8,128)}), f32[32,40,128]{2,1,0:T(8,128)S(1)}, u32[]{:S(2)}, u32[]{:S(2)}) async-start(f32[32,40,128]{2,1,0:T(8,128)} %bitcast.12), calls=%async_computation | async-start | bytes 1310720 | tf_op jit(solution)/shard_map/all_to_all | solution.py:309
  54.1 10.5 %collective-permute-start.4 = (bf16[3,64,384]{2,1,0:T(8,128)(2,1)S(1)}, bf16[3,64,384]{2,1,0:T(8,128)(2,1)S(1)}, u32[]{:S(2)}, u32[]{:S(2)}) collective-permute-start(bf16[3,64,384]{2,1,0:T(8,128)(2,1)S(1)} %get-tuple-element.42), channel_id=1, source_target_pairs={{0,1},{1,2},{2,3},{3,0},{4,5},{5,6},{6,7},{7,4},{8,9},{9,10},{10,1... | collective-permute-start | bytes 442376 | tf_op jit(solution)/shard_map/ppermute | solution.py:301
  57.3 11.0 %collective-permute-start.5 = (bf16[3,64,384]{2,1,0:T(8,128)(2,1)S(1)}, bf16[3,64,384]{2,1,0:T(8,128)(2,1)S(1)}, u32[]{:S(2)}, u32[]{:S(2)}) collective-permute-start(bf16[3,64,384]{2,1,0:T(8,128)(2,1)S(1)} %get-tuple-element.43), channel_id=1, source_target_pairs={{0,3},{1,0},{2,1},{3,2},{4,7},{5,4},{6,5},{7,6},{8,11},{9,8},{10,9... | collective-permute-start | bytes 442376 | tf_op jit(solution)/shard_map/ppermute | solution.py:301
  69.0 12.7 %all-to-all-start.1 = ((f32[8,40,128]{2,1,0:T(8,128)}), f32[8,40,128]{2,1,0:T(8,128)S(1)}, u32[]{:S(2)}, u32[]{:S(2)}) async-start(f32[8,40,128]{2,1,0:T(8,128)} %shard_map.126), calls=%async_computation.1 | async-start | bytes 327680 | tf_op jit(solution)/shard_map/all_to_all | solution.py:309
  72.4 9.2 %collective-permute-start.6 = (bf16[64,384]{1,0:T(8,128)(2,1)S(1)}, bf16[64,384]{1,0:T(8,128)(2,1)S(1)}, u32[]{:S(2)}, u32[]{:S(2)}) collective-permute-start(bf16[64,384]{1,0:T(8,128)(2,1)S(1)} %get-tuple-element.45), channel_id=1, source_target_pairs={{0,4},{4,8},{8,12},{12,16},{16,20},{20,24},{24,28},{28,32},{32,36}... | collective-permute-start | bytes 147464 | tf_op jit(solution)/shard_map/ppermute | solution.py:301
  72.8 8.8 %collective-permute-start.7 = (bf16[64,384]{1,0:T(8,128)(2,1)S(1)}, bf16[64,384]{1,0:T(8,128)(2,1)S(1)}, u32[]{:S(2)}, u32[]{:S(2)}) collective-permute-start(bf16[64,384]{1,0:T(8,128)(2,1)S(1)} %get-tuple-element.46), channel_id=1, source_target_pairs={{0,252},{4,0},{8,4},{12,8},{16,12},{20,16},{24,20},{28,24},{32,28}... | collective-permute-start | bytes 147464 | tf_op jit(solution)/shard_map/ppermute | solution.py:301
  82.5 19.6 %all-to-all-start.2 = ((f32[32,40,128]{2,1,0:T(8,128)}), f32[32,40,128]{2,1,0:T(8,128)S(1)}, u32[]{:S(2)}, u32[]{:S(2)}) async-start(f32[32,40,128]{2,1,0:T(8,128)} %shard_map.127), calls=%async_computation.2 | async-start | bytes 1310720 | tf_op jit(solution)/shard_map/all_to_all | solution.py:309
  89.0 1.4 %copy-start.10 = (bf16[1024,768]{1,0:T(8,128)(2,1)S(1)}, bf16[1024,768]{1,0:T(8,128)(2,1)}, u32[]{:S(2)}) copy-start(bf16[1024,768]{1,0:T(8,128)(2,1)} %copy-done.9) | copy-start | bytes 4718596

commit v3 on v2

--- a/solution.py
+++ b/solution.py
@@ -15,10 +15,10 @@
 NEAR = 9 * SAMP
 PAD = PTS + WIN
 ROWS = 1280
-CHUNK = ROWS // 32
+HALF = ROWS // 2
 GX = ("z", "y", "xl")
 GY = ("xh", "c")
-GROUP = ("c", "y", "xl", "xh")
+XY = ("y", "xl", "xh")
 SCALE = DEPTH ** (-0.5)
 LOG2E = 1.4426950408889634
 F32 = jnp.float32
@@ -26,7 +26,7 @@
 VMEM = pl.BlockSpec(memory_space=pltpu.VMEM)
 SMEM = pl.BlockSpec(memory_space=pltpu.SMEM)
 ANY = pl.BlockSpec(memory_space=pl.ANY)
-UNROLL = 4
+TOGETHER = 4
 
 
 def nn(a, b):
@@ -57,6 +57,13 @@
 
 def gain_column(gain):
     return jnp.broadcast_to(gain[...], (128, C)).T
+
+
+def order_kernel(place, own, first, second, across):
+    odd = place[1]
+    across[SAMP:2 * SAMP, :] = own[...]
+    across[pl.ds(pl.multiple_of(2 * SAMP * (1 - odd), SAMP), SAMP), :] = first[...]
+    across[pl.ds(pl.multiple_of(2 * SAMP * odd, SAMP), SAMP), :] = second[...]
 
 
 def prepare_kernel(after, points, gain, wq, wk, wv, wo, cot, picks_row, picks_col,
@@ -107,11 +114,15 @@
     lax.fori_loop(0, 9, columns_hot, 0)
 
 
-def attend_kernel(lengths, low, middle, high, gain, w_in, qa, ka, va, da, kvb, qdb, onehot, onehot_t,
-                  d_near, d_low, d_high, rest, grads, near_hat, near_normed,
-                  near_kv, pick, d_pick, oa_s, dqa_s, dka_s, dva_s, dkvb_s, dqob_s):
-    near_points = jnp.concatenate([low[...], middle[...], high[...]], axis=0)
-    hat, _inv = standardize(near_points.astype(F32), 1)
+def attend_kernel(lengths, place, own_near, first, second, gain, w_in, qa, ka, va, da, kvb, qdb, onehot, onehot_t,
+                  d_near, d_first, d_second, rest, grads, near_hat, near_normed,
+                  near_points, near_kv, pick, d_pick, oa_s, dqa_s, dka_s, dva_s, dkvb_s, dqob_s):
+    odd = place[0]
+    strip = 3 * SAMP
+    near_points[strip:2 * strip, :] = own_near[...]
+    near_points[pl.ds(pl.multiple_of(2 * strip * (1 - odd), SAMP), strip), :] = first[...]
+    near_points[pl.ds(pl.multiple_of(2 * strip * odd, SAMP), strip), :] = second[...]
+    hat, _inv = standardize(near_points[...].astype(F32), 1)
     near_hat[...] = hat
     normed = (hat * gain[...]).astype(BF16)
     near_normed[...] = normed
@@ -136,9 +147,6 @@
     def down(parts):
         return jnp.concatenate(parts, axis=0)
 
-    def along(parts):
-        return jnp.concatenate(parts, axis=1)
-
     def softmax(scores, bias):
         scores = scores + bias
         top = jnp.max(scores, axis=-1, keepdims=True)
@@ -150,61 +158,100 @@
         inner = jnp.sum(d_probs * probs, axis=-1, keepdims=True)
         return (probs * (d_probs - inner)).astype(BF16)
 
-    def head(x, h):
-        return x[:, 128 * h:128 * (h + 1)]
-
-    def window(w, offset):
+    def cut(x):
+        return [x[WIN * h:WIN * (h + 1)] for h in range(4)]
+
+    def merge(x):
+        parts = [part * lane for part, lane in zip(cut(x), lanes32)]
+        return (parts[0] + parts[1]) + (parts[2] + parts[3])
+
+    lanes32 = [lane.astype(F32) for lane in lanes]
+
+    def load(w, offset):
         count = lengths[w]
         rows = pl.ds(offset, WIN)
         own = pl.ds(pl.multiple_of(w * WIN, WIN), WIN)
         bias = jnp.where((key_id >= count) & (key_id < WIN), -1e30, 0.0)
         alive = slot < count
-        keys = per_head(down([ka[rows, :].astype(BF16), pick[own, 0:128]]))
-        values = per_head(down([va[rows, :].astype(BF16), pick[own, 128:256]]))
-        both = per_head(down([kvb[rows, :].astype(BF16), pick[own, 256:384]]))
-        q = qa[rows, :].astype(BF16)
-        d = jnp.where(alive, da[rows, :], 0.0).astype(BF16)
-        qd = jnp.where(alive, qdb[rows, :], 0.0).astype(BF16)
-        scores = nt(q, keys)
-        d_probs = nt(d, values)
-        mixed = nt(qd, both)
-        probs = [softmax(head(scores, h), bias) for h in range(4)]
-        probs_b = [softmax(head(mixed, h), bias) for h in range(2)]
-        probs16 = [p.astype(BF16) for p in probs]
-        d_scores = [score_gradient(p, head(d_probs, h)) for h, p in enumerate(probs)]
-        back = [score_gradient(p, head(mixed, 2 + h)) for h, p in enumerate(probs_b)]
+        keys = down([ka[rows, :].astype(BF16), pick[own, 0:128]])
+        values = down([va[rows, :].astype(BF16), pick[own, 128:256]])
+        both = down([kvb[rows, :].astype(BF16), pick[own, 256:384]])
+        qe = per_head(qa[rows, :].astype(BF16))
+        de = per_head(jnp.where(alive, da[rows, :], 0.0).astype(BF16))
+        qde = per_head(jnp.where(alive, qdb[rows, :], 0.0).astype(BF16))
+        return rows, own, bias, keys, values, both, qe, de, qde
+
+    def scored(item):
+        _, _, _, keys, values, both, qe, de, qde = item
+        return nt(qe, keys), nt(de, values), nt(qde, both)
+
+    def weighed(item, found):
+        bias = item[2]
+        scores, d_probs, mixed = [cut(x) for x in found]
+        probs = [softmax(x, bias) for x in scores]
+        probs_b = [softmax(x, bias) for x in mixed[:2]]
+        d_scores = [score_gradient(p, x) for p, x in zip(probs, d_probs)]
+        back = [score_gradient(p, x) for p, x in zip(probs_b, mixed[2:])]
         back = back + [p.astype(BF16) for p in probs_b]
-        oa_s[rows, :] = nn(along(probs16), values)
-        dqa_s[rows, :] = nn(along(d_scores), keys) * SCALE
-        dqob_s[rows, :] = nn(along(back), both) * half_scale
-        d_keys = tn(down(d_scores), per_head(q)) * SCALE
-        d_values = tn(down(probs16), per_head(d))
-        d_both = tn(down(back), per_head(qd)) * half_scale
+        return down([p.astype(BF16) for p in probs]), down(d_scores), down(back)
+
+    def stored(item, found):
+        rows, own, _, keys, values, both, qe, de, qde = item
+        probs, d_scores, back = found
+        oa_s[rows, :] = merge(nn(probs, values))
+        dqa_s[rows, :] = merge(nn(d_scores, keys)) * SCALE
+        dqob_s[rows, :] = merge(nn(back, both)) * half_scale
+        d_keys = tn(d_scores, qe) * SCALE
+        d_values = tn(probs, de)
+        d_both = tn(back, qde) * half_scale
         dka_s[rows, :] = d_keys[:WIN]
         dva_s[rows, :] = d_values[:WIN]
         dkvb_s[rows, :] = d_both[:WIN]
         d_pick[own, 0:128] = d_keys[WIN:].astype(BF16)
         d_pick[own, 128:256] = d_values[WIN:].astype(BF16)
         d_pick[own, 256:384] = d_both[WIN:].astype(BF16)
-        return offset + count
-
-    lax.fori_loop(0, NWIN, window, jnp.int32(0), unroll=UNROLL)
+
+    def windows(group, offset):
+        items = []
+        for j in range(TOGETHER):
+            items.append(load(group * TOGETHER + j, offset))
+            offset = offset + lengths[group * TOGETHER + j]
+        found = [scored(item) for item in items]
+        found = [weighed(item, x) for item, x in zip(items, found)]
+        for item, x in zip(items, found):
+            stored(item, x)
+        return offset
+
+    lax.fori_loop(0, NWIN // TOGETHER, windows, jnp.int32(0))
 
     near = nn(onehot_t[...], d_pick[...])
     near16 = near.astype(BF16)
     d_near[...] = near16
+    side = place[1]
     for i in range(3):
-        d_low[i] = near16[192 * i:192 * i + 64]
-        d_high[i] = near16[192 * i + 128:192 * i + 192]
+        d_first[i] = d_near[pl.ds(pl.multiple_of(192 * i + 128 * (1 - side), SAMP), SAMP), :]
+        d_second[i] = d_near[pl.ds(pl.multiple_of(192 * i + 128 * side, SAMP), SAMP), :]
     rest[...] = (near - near16.astype(F32)).astype(BF16)
     for i, ref in enumerate((dqa_s, dka_s, dva_s, dkvb_s, dqob_s, oa_s)):
         grads[:, 128 * i:128 * (i + 1)] = ref[:PTS, :].astype(BF16)
 
 
-def weights_kernel(points, cot, w_in, normed_t, grads, d_near, rest, near_hat, near_normed, packed):
-    wide = nn(normed_t[...], grads[:, 0:640])
+def weights_kernel(points, cot, w_in, normed_t, grads, wide, out, gain_sum):
+    wide[...] = nn(normed_t[...], grads[:, 0:640])
+    out[...] = nn(cot[...], grads[:, 512:768])
+
+    def gain_part(i, total):
+        rows = pl.ds(pl.multiple_of(i * 128, 128), 128)
+        hat, _inv = standardize(points[:, rows].astype(F32), 0)
+        return total + nt(w_in[...], grads[rows, 0:640]) * hat
+
+    total = lax.fori_loop(0, PTS // 128, gain_part, jnp.zeros((C, 128), F32))
+    gain_sum[...] = jnp.sum(total.T, axis=0, keepdims=True)
+
+
+def near_kernel(place, w_in, wide, out, gain_sum, d_near, rest, near_hat, near_normed, got, got_too,
+                keep, send, first, second, middle, packed, sides):
     near_wide = tn(near_normed[...], d_near[...]) + tn(near_normed[...], rest[...])
-    out = nn(cot[...], grads[:, 512:768])
     packed[0:192, :] = wide[:, 0:128]
     packed[192:384, :] = wide[:, 128:256] + near_wide[:, 0:128]
     packed[384:576, :] = wide[:, 256:384] + near_wide[:, 128:256]
@@ -212,33 +259,26 @@
     packed[768:960, :] = wide[:, 384:512] + near_wide[:, 256:384]
     lane = lax.broadcasted_iota(jnp.int32, (C, 128), 1)
     packed[960:1152, :] = jnp.where(lane < 64, wide[:, 512:640], out[:, 0:128])
-
-    def gain_part(i, total):
-        rows = pl.ds(pl.multiple_of(i * 128, 128), 128)
-        hat, _inv = standardize(points[:, rows].astype(F32), 0)
-        return total + nt(w_in[...], grads[rows, 0:640]) * hat
-
-    total = lax.fori_loop(0, PTS // 128, gain_part, jnp.zeros((C, 128), F32))
     w_kv = w_in[:, 128:512]
     d = nt(d_near[...], w_kv) + nt(rest[...], w_kv)
     near_total = jnp.sum((d * near_hat[...]).reshape(NEAR // 8, 8, C), axis=0)
-    gain_sum = jnp.sum(total.T, axis=0, keepdims=True) + jnp.sum(near_total, axis=0, keepdims=True)
+    gains = gain_sum[...] + jnp.sum(near_total, axis=0, keepdims=True)
     packed[1152:, :] = jnp.zeros((ROWS - 1152, 128), F32)
-    packed[1152:1153, :] = gain_sum[:, :128]
-    packed[1153:1154, 0:64] = gain_sum[:, 128:]
-
-
-def sides_kernel(d_near, upper, lower, up, down, middle):
-    def side(i):
+    packed[1152:1153, :] = gains[:, :128]
+    packed[1153:1154, 0:64] = gains[:, 128:]
+    for i in range(3):
         own = d_near[192 * i + 64:192 * i + 128, :].astype(F32)
-        return own + upper[i].astype(F32) + lower[i].astype(F32)
-
-    up[...] = side(2).astype(BF16)
-    down[...] = side(0).astype(BF16)
-    middle[...] = side(1)
-
-
-def fold_kernel(upper, lower, parts, out):
+        sides[SAMP * i:SAMP * (i + 1), :] = own + got[i].astype(F32) + got_too[i].astype(F32)
+    odd = place[0]
+    first[...] = sides[pl.ds(pl.multiple_of(2 * SAMP * (1 - odd), SAMP), SAMP), :].astype(BF16)
+    second[...] = sides[pl.ds(pl.multiple_of(2 * SAMP * odd, SAMP), SAMP), :].astype(BF16)
+    middle[...] = sides[SAMP:2 * SAMP, :]
+    mine = place[1]
+    keep[...] = packed[pl.ds(pl.multiple_of(mine * HALF, HALF), HALF), :]
+    send[...] = packed[pl.ds(pl.multiple_of((1 - mine) * HALF, HALF), HALF), :]
+
+
+def fold_kernel(after, parts, out):
     total = parts[0]
     for i in range(1, parts.shape[0]):
         total = total + parts[i]
@@ -273,8 +313,11 @@
     lax.fori_loop(0, PTS // chunk, part, 0)
 
 
-def unpack_kernel(after, gathered, weights, gain_gradient, packed):
-    packed[...] = gathered[...] * (PTS * 256) ** (-0.5)
+def unpack_kernel(place, own, other, weights, gain_gradient, packed):
+    mine = place[1]
+    factor = (PTS * 256) ** (-0.5)
+    packed[pl.ds(pl.multiple_of(mine * HALF, HALF), HALF), :] = own[...] * factor
+    packed[pl.ds(pl.multiple_of((1 - mine) * HALF, HALF), HALF), :] = other[...] * factor
     for i, (tail, side) in enumerate(((960, 0), (768, 0), (768, 64))):
         weights[i, :, 0:128] = packed[192 * i:192 * (i + 1), :]
         weights[i, :, 128:C] = packed[tail:tail + 192, side:side + 64]
@@ -296,13 +339,14 @@
     )
 
 
-def moved(block, axes, count, distance):
-    route = [(i, (i + distance) % count) for i in range(count)]
-    return lax.ppermute(block, axes, route)
-
-
-def extended(rows, axes, count):
-    return jnp.concatenate([moved(rows, axes, count, 1), rows, moved(rows, axes, count, -1)], axis=0)
+def neighbours(first, second, axes, count):
+    pairs = [(i, i ^ 1) for i in range(count)]
+    across = [(i, min(max(((i + 1) ^ 1) - 1, 0), count - 1)) for i in range(count)]
+    return lax.ppermute(first, axes, pairs), lax.ppermute(second, axes, across)
+
+
+def swapped(x):
+    return lax.ppermute(x, "c", [(0, 1), (1, 0)])
 
 
 def exchanged(x, axes):
@@ -318,22 +362,36 @@
         picks.reshape(1, NWIN * WIN), picks.reshape(NWIN * WIN, 1))
 
 
-def local_attend(lengths, near, gain, w_in, projections, hots):
+def local_order(place, own, first, second):
+    return call(order_kernel, [((3 * SAMP, C), BF16)], [SMEM] + [VMEM] * 3, limit=6)(
+        place, own, first, second)[0]
+
+
+def local_attend(lengths, place, near, gain, w_in, projections, hots):
     big = ((PAD, 128), F32)
     near_out = ((NEAR, 2 * C), BF16)
+    side = ((3, SAMP, 2 * C), BF16)
     return call(
         attend_kernel,
-        [near_out] + [((3, SAMP, 2 * C), BF16)] * 2 + [near_out, ((PTS, 6 * 128), BF16), ((NEAR, C), F32), ((NEAR, C), BF16)],
-        [SMEM] + [VMEM] * 13,
-        [near_out] + [((NWIN * WIN, 2 * C), BF16)] * 2 + [big] * 6,
-        limit=26, micros=18.0,
-    )(lengths, *near, gain.reshape(1, C), w_in, *projections, *hots)
-
-
-def local_weights(points, cotangent, w_in, normed_t, grads, d_near, rest, near_hat, near_normed):
-    return call(
-        weights_kernel, [((ROWS, 128), F32)], [VMEM] * 9, limit=14, micros=3.0
-    )(points, cotangent, w_in, normed_t, grads, d_near, rest, near_hat, near_normed)[0]
+        [near_out, side, side, near_out, ((PTS, 6 * 128), BF16), ((NEAR, C), F32), ((NEAR, C), BF16)],
+        [SMEM] * 2 + [VMEM] * 13,
+        [((NEAR, C), BF16), near_out] + [((NWIN * WIN, 2 * C), BF16)] * 2 + [big] * 6,
+        limit=26, micros=14.0,
+    )(lengths, place, *near, gain.reshape(1, C), w_in, *projections, *hots)
+
+
+def local_weights(points, cotangent, w_in, normed_t, grads):
+    outs = [((C, 640), F32), ((C, 256), F32), ((1, C), F32)]
+    return call(weights_kernel, outs, [VMEM] * 5, limit=12, micros=3.0)(
+        points, cotangent, w_in, normed_t, grads)
+
+
+def local_near(place, w_in, sums, d_near, rest, near_hat, near_normed, got):
+    side = ((SAMP, 2 * C), BF16)
+    outs = [((HALF, 128), F32)] * 2 + [side, side, ((SAMP, 2 * C), F32)]
+    scratch = [((ROWS, 128), F32), ((3 * SAMP, 2 * C), F32)]
+    return call(near_kernel, outs, [SMEM] + [VMEM] * 10, scratch, limit=12)(
+        place, w_in, *sums, d_near, rest, near_hat, near_normed, *got)
 
 
 def local_finish(points, gain, w_in, w_back, cotangent, grads, middle, upper, lower):
@@ -342,21 +400,16 @@
         points, gain.reshape(1, C), w_in, w_back, cotangent, grads, middle, upper, lower)
 
 
-def local_sides(d_near, upper, lower):
-    outs = [((SAMP, 2 * C), BF16)] * 2 + [((SAMP, 2 * C), F32)]
-    return call(sides_kernel, outs, [VMEM] * 3, limit=6)(d_near, upper, lower)
-
-
-def local_fold(upper, lower, parts, copies):
+def local_fold(after, parts, copies):
     outs = [((copies,) + parts.shape[1:], F32)]
-    return call(fold_kernel, outs, [ANY, ANY, VMEM], limit=6)(upper, lower, parts)[0]
-
-
-def local_unpack(after, gathered):
+    return call(fold_kernel, outs, [ANY, VMEM], limit=6)(after, parts)[0]
+
+
+def local_unpack(place, own, other):
     return call(
-        unpack_kernel, [((4, C, C), F32), ((1, C), F32)], [ANY, VMEM], [((ROWS, 128), F32)],
+        unpack_kernel, [((4, C, C), F32), ((1, C), F32)], [SMEM, VMEM, VMEM], [((ROWS, 128), F32)],
         limit=8, micros=1.0,
-    )(after, gathered)
+    )(place, own, other)
 
 
 def body(points, gain, w_query, w_key, w_value, w_out, lengths, picks, cotangent):
@@ -364,25 +417,25 @@
     cotangent = cotangent[0, 0].T
     lengths = lengths.reshape(NWIN)
     sample = call(sample_kernel, [((SAMP, C), BF16)], [VMEM], limit=6)(points)[0]
-    across = extended(sample, GY, 4)
-    near = (moved(across, GX, 64, 1), across, moved(across, GX, 64, -1))
+    place = jnp.stack([lax.axis_index("xl"), lax.axis_index("c")]).astype(jnp.int32)
+    across = local_order(place, sample, *neighbours(sample, sample, GY, 4))
+    near = (across,) + neighbours(across, across, GX, 64)
     *projections, normed_t, w_in, w_back, onehot, onehot_t = local_prepare(
         across, points, gain, w_query, w_key, w_value, w_out, cotangent, picks)
     hots = (onehot, onehot_t)
-    d_near, d_low, d_high, rest, grads, near_hat, near_normed = local_attend(
-        lengths, near, gain, w_in, projections, hots)
-    upper = moved(d_high, GY, 4, 1)
-    lower = moved(d_low, GY, 4, -1)
-    packed = local_weights(points, cotangent, w_in, normed_t, grads, d_near, rest, near_hat, near_normed)
-    mixed = exchanged(packed.reshape(32, CHUNK, 128), GROUP)
-    mixed = exchanged(local_fold(upper, lower, mixed, 8), "z")
-    up, down, middle = local_sides(d_near, upper, lower)
-    upper = moved(up, GX, 64, 1)
-    lower = moved(down, GX, 64, -1)
-    gathered = exchanged(local_fold(upper, lower, mixed, 32), GROUP).reshape(ROWS, 128)
+    d_near, d_first, d_second, rest, grads, near_hat, near_normed = local_attend(
+        lengths, place, near, gain, w_in, projections, hots)
+    got = neighbours(d_first, d_second, GY, 4)
+    sums = local_weights(points, cotangent, w_in, normed_t, grads)
+    keep, send, first, second, middle = local_near(
+        place, w_in, sums, d_near, rest, near_hat, near_normed, got)
+    got = neighbours(first, second, GX, 64)
     layer_out, feature_gradient, token = local_finish(
-        points, gain, w_in, w_back, cotangent, grads, middle, upper, lower)
-    weights, gain_gradient = local_unpack(token, gathered)
+        points, gain, w_in, w_back, cotangent, grads, middle, *got)
+    mixed = exchanged((keep + swapped(send)).reshape(16, HALF // 16, 128), XY)
+    mixed = exchanged(local_fold(got[0], mixed, 8), "z")
+    own = exchanged(local_fold(token, mixed, 16), XY).reshape(HALF, 128)
+    weights, gain_gradient = local_unpack(place, own, swapped(own))
     return layer_out.T[None, None], feature_gradient.T[None, None], weights, gain_gradient.reshape(C)
 
 

time: 104 us -> 98.4 us (0.946)
  blocking collectives: 0 us -> 12.1 us
  waiting for transfers between devices: 24.6 us -> 12.9 us
  Pallas kernels: 35.1 us -> 30.8 us
  local copies, waits for them, and re-layouts: 3.24 us -> 1.87 us
    all_to_all x0 -> x1, blocking collectives: none -> 12.1 us  [exchanged(): return lax.all_to_all(x, axes, 0, 0, tiled=True)]
    ppermute x8 -> x10, waiting for transfers between devices: 17.4 us -> 7.69 us  [the longest x4 4.09 us: neighbours(): lax.ppermute(first, axes, pairs)]
    pallas_call x6 -> x7, Pallas kernels: 25.1 us -> 20.8 us  [the longest x1 13.8 us: local_attend(): call(attend_kernel, [near_out, side, side, near_out, ((PTS, 6 * 128), BF1...]
    all_to_all x3 -> x2, starting transfers between devices: 17.2 us -> 14.9 us  [exchanged(): return lax.all_to_all(x, axes, 0, 0, tiled=True)]
    all_to_all x3 -> x2, waiting for transfers between devices: 7.22 us -> 5.25 us  [exchanged(): return lax.all_to_all(x, axes, 0, 0, tiled=True)]
    unnamed x24, local copies, waits for them, and re-layouts: 2.43 us -> 1.06 us
    ppermute x8 -> x10, starting transfers between devices: 22.1 us -> 23.5 us  [the longest x4 12.7 us: neighbours(): lax.ppermute(second, axes, across)]
  transfers between devices with their start and end apart: 11 -> 12, of which waited for: 6 -> 7; matrix products, arithmetic and copies ran while one was open for 1% -> 1% of each run, Pallas kernels for 10% -> 13%
where the time goes in v3:
time: 98.4 us; the launch traced here: 97.9 us
  starting transfers between devices  38.3 us (39%)
  Pallas kernels  30.8 us (31%)
  waiting for transfers between devices  12.9 us (13%)
  blocking collectives  12.1 us (12%)
  local copies, waits for them, and re-layouts  1.87 us (2%)
    all_to_all x2, starting transfers between devices, exchanged(): return lax.all_to_all(x, axes, 0, 0, tiled=True)  14.9 us
    pallas_call x1, Pallas kernels, local_attend(): call(attend_kernel, [near_out, side, side, near_out, ((PTS, 6 * 128), BF1...  13.8 us
    ppermute x4, starting transfers between devices, neighbours(): lax.ppermute(second, axes, across)  12.7 us
    all_to_all x1, blocking collectives, exchanged(): return lax.all_to_all(x, axes, 0, 0, tiled=True)  12.1 us
    ppermute x4, starting transfers between devices, neighbours(): lax.ppermute(first, axes, pairs)  5.9 us
    pallas_call x1, Pallas kernels, local_prepare(): call(prepare_kernel, outs, [ANY] + [VMEM] * 9, limit=24, micros=5.0)  5.3 us
    all_to_all x2, waiting for transfers between devices, exchanged(): return lax.all_to_all(x, axes, 0, 0, tiled=True)  5.25 us
    ppermute x2, starting transfers between devices, swapped(): return lax.ppermute(x, 'c', [(0, 1), (1, 0)])  4.9 us
  transfers between devices with their start and end apart: 12, of which 7 were waited for; matrix products, arithmetic and copies ran while one was open for 1% of the time, Pallas kernels for 13%

profile of v3, /device:TPU:1, one launch (start us, length us, event | category | flops | bytes accessed | tf_op | source)
XLA Modules:
  0.0 97.9 jit_solution(15330984501720046585)
XLA Ops:
  0.6 1.0 %copy-done = bf16[1,1,1024,192]{2,3,1,0:T(8,128)(2,1)S(1)} copy-done((bf16[1,1,1024,192]{2,3,1,0:T(8,128)(2,1)S(1)}, bf16[1,1,1024,192]{2,3,1,0:T(8,128)(2,1)}, u32[]{:S(2)}) %copy-start) | copy-done | bytes 393240
  1.6 0.2 shard_map.120.own
  1.9 6.0 %collective-permute-start.1 = (bf16[64,192]{1,0:T(8,128)(2,1)S(1)}, bf16[64,192]{1,0:T(8,128)(2,1)S(1)}, u32[]{:S(2)}, u32[]{:S(2)}) collective-permute-start(bf16[64,192]{1,0:T(8,128)(2,1)S(1)} %shard_map.120.own), channel_id=1, source_target_pairs={{0,0},{1,2},{2,1},{3,3},{4,4},{5,6},{6,5},{7,7},{8,8},{9,10},{10,9... | collective-permute-start | bytes 73736 | tf_op jit(solution)/shard_map/ppermute | solution.py:345
  7.9 0.1 collective-permute-start
  8.2 0.7 reshape.38.picks_col
  9.0 0.5 collective-permute-done.1.second
  9.5 0.6 shard_map.121.after.own_near
  10.1 0.7 collective-permute-start.3
  10.7 3.8 %collective-permute-start.2 = (bf16[192,192]{1,0:T(8,128)(2,1)S(1)}, bf16[192,192]{1,0:T(8,128)(2,1)S(1)}, u32[]{:S(2)}, u32[]{:S(2)}) collective-permute-start(bf16[192,192]{1,0:T(8,128)(2,1)S(1)} %shard_map.121.after.own_near), channel_id=1, source_target_pairs={{0,4},{4,0},{8,12},{12,8},{16,20},{20,16},{24,28},{28,24},{32,36},... | collective-permute-start | bytes 221192 | tf_op jit(solution)/shard_map/ppermute | solution.py:345
  14.6 5.3 %shard_map.122 = (f32[1088,128]{1,0:T(8,128)S(1)}, f32[1088,128]{1,0:T(8,128)S(1)}, f32[1088,128]{1,0:T(8,128)S(1)}, f32[1088,128]{1,0:T(8,128)S(1)}, f32[1088,1...) custom-call(bf16[192,192]{1,0:T(8,128)(2,1)S(1)} %shard_map.121.afte, ...), custom_call_target="tpu_custom_call" | custom-call | flops 5000000000 | bytes 15000000 | tf_op jit(solution)/shard_map/pallas_call | solution.py:360
  20.0 13.8 %shard_map.123 = (bf16[576,384]{1,0:T(8,128)(2,1)S(1)}, bf16[3,64,384]{2,1,0:T(8,128)(2,1)S(1)}, bf16[3,64,384]{2,1,0:T(8,128)(2,1)S(1)}, bf16[576,384]{1,0:T(8,...) custom-call(s32[24]{0:T(128)S(1)} %bitcast.35, ...), custom_call_target="tpu_custom_call" | custom-call | flops 14000000000 | bytes 42000000 | tf_op jit(solution)/shard_map/pallas_call | solution.py:374
  33.8 0.6 collective-permute-start.4
  34.4 5.2 %collective-permute-start.5 = (bf16[3,64,384]{2,1,0:T(8,128)(2,1)S(1)}, bf16[3,64,384]{2,1,0:T(8,128)(2,1)S(1)}, u32[]{:S(2)}, u32[]{:S(2)}) collective-permute-start(bf16[3,64,384]{2,1,0:T(8,128)(2,1)S(1)} %get-tuple-element.55), channel_id=1, source_target_pairs={{0,0},{1,2},{2,1},{3,3},{4,4},{5,6},{6,5},{7,7},{8,8},{9,10},{10,9... | collective-permute-start | bytes 442376 | tf_op jit(solution)/shard_map/ppermute | solution.py:345
  39.6 2.6 %shard_map.124 = (f32[192,640]{1,0:T(8,128)S(1)}, f32[192,256]{1,0:T(8,128)S(1)}, f32[1,192]{1,0:T(1,128)S(1)}) custom-call(bf16[192,1024]{1,0:T(8,128)(2,1)S(1)} %bitcast.27, bf16[192,1024]{1,0:T(8,128)(2,1)S(1)} %bitcast.30, bf16[192,640]{1,0:T(8,128)(2,1)S(1)} %get-tuple-element.35.w_in, bf16[192,1024]{1,0:T(8,128)(2,1)S(1)} %get-tuple-element.46.normed_t, ...), custom_call_target="tpu_custom_call" | custom-call | flops 3000000000 | bytes 9000000 | tf_op jit(solution)/shard_map/pallas_call | solution.py:385
  42.2 0.2 collective-permute-done.5.got_too
  42.4 1.5 %shard_map.125 = (f32[640,128]{1,0:T(8,128)S(1)}, f32[640,128]{1,0:T(8,128)S(1)}, bf16[64,384]{1,0:T(8,128)(2,1)S(1)}, bf16[64,384]{1,0:T(8,128)(2,1)S(1)}, f32[64,384]{1,0:T(8,128)S(1)}) custom-call(s32[2]{0:T(128)S(1)} %pad_add_fusion.place, bf16[192,640]{1,0:T(8,128)(2,1)S(1)} %get-tuple-element.35.w_in, f32[192,640]{1,0:T(8,128)S(1)} %get-tuple-element.47.wide, ...), custom_call_target="tpu_custom_call" | custom-call | flops 1000000000 | bytes 3000000 | tf_op jit(solution)/shard_map/pallas_call | solution.py:393
  43.9 0.1 collective-permute-start.8
  44.0 1.6 %collective-permute-done.8 = f32[640,128]{1,0:T(8,128)S(1)} collective-permute-done((f32[640,128]{1,0:T(8,128)S(1)}, f32[640,128]{1,0:T(8,128)S(1)}, u32[]{:S(2)}, u32[]{:S(2)}) %collective-permute-start.8) | collective-permute-done | bytes 327712 | tf_op jit(solution)/shard_map/ppermute | solution.py:349
  45.6 0.8 add.3
  46.4 6.8 %all-to-all-start = ((f32[16,40,128]{2,1,0:T(8,128)}), f32[16,40,128]{2,1,0:T(8,128)S(1)}, u32[]{:S(2)}, u32[]{:S(2)}) async-start(f32[16,40,128]{2,1,0:T(8,128)} %bitcast.14), calls=%async_computation | async-start | bytes 655360 | tf_op jit(solution)/shard_map/all_to_all | solution.py:353
  53.2 1.4 %collective-permute-start.6 = (bf16[64,384]{1,0:T(8,128)(2,1)S(1)}, bf16[64,384]{1,0:T(8,128)(2,1)S(1)}, u32[]{:S(2)}, u32[]{:S(2)}) collective-permute-start(bf16[64,384]{1,0:T(8,128)(2,1)S(1)} %get-tuple-element.57), channel_id=1, source_target_pairs={{0,4},{4,0},{8,12},{12,8},{16,20},{20,16},{24,28},{28,24},{32,36},... | collective-permute-start | bytes 147464 | tf_op jit(solution)/shard_map/ppermute | solution.py:345
  54.6 0.8 collective-permute-start.7
  55.3 4.1 %collective-permute-done.6.upper.after = bf16[64,384]{1,0:T(8,128)(2,1)S(1)} collective-permute-done((bf16[64,384]{1,0:T(8,128)(2,1)S(1)}, bf16[64,384]{1,0:T(8,128)(2,1)S(1)}, u32[]{:S(2)}, u32[]{:S(2)}) %collective-permute-start.6) | collective-permute-done | bytes 49184 | tf_op jit(solution)/shard_map/ppermute | solution.py:345
  59.4 1.5 %all-to-all-done.parts = f32[16,40,128]{2,1,0:T(8,128)S(1)} async-done(((f32[16,40,128]{2,1,0:T(8,128)}), f32[16,40,128]{2,1,0:T(8,128)S(1)}, u32[]{:S(2)}, u32[]{:S(2)}) %all-to-all-start) | async-done | bytes 327712 | tf_op jit(solution)/shard_map/all_to_all | solution.py:353
  60.9 0.7 shard_map.127
  61.6 8.1 %all-to-all-start.1 = ((f32[8,40,128]{2,1,0:T(8,128)}), f32[8,40,128]{2,1,0:T(8,128)S(1)}, u32[]{:S(2)}, u32[]{:S(2)}) async-start(f32[8,40,128]{2,1,0:T(8,128)} %shard_map.127), calls=%async_computation.1 | async-start | bytes 327680 | tf_op jit(solution)/shard_map/all_to_all | solution.py:353
  69.7 4.5 %shard_map.126 = (bf16[192,1024]{1,0:T(8,128)(2,1)}, f32[192,1024]{1,0:T(8,128)}, f32[8,128]{1,0:T(8,128)S(1)}) custom-call(bf16[192,1024]{1,0:T(8,128)(2,1)S(1)} %bitcast.28, f32[1,192]{1,0:T(1,128)S(1)} %bitcast.34, bf16[192,640]{1,0:T(8,128)(2,1)S(1)} %get-tuple-element.35.w_in, bf16[192,256]{1,0:T(8,128)(2,1)S(1)} %copy-done.10, ...), custom_call_target="tpu_custom_call" | custom-call | flops 4000000000 | bytes 12000000 | tf_op jit(solution)/shard_map/pallas_call | solution.py:399
  74.2 3.8 %all-to-all-done.1.parts = f32[8,40,128]{2,1,0:T(8,128)S(1)} async-done(((f32[8,40,128]{2,1,0:T(8,128)}), f32[8,40,128]{2,1,0:T(8,128)S(1)}, u32[]{:S(2)}, u32[]{:S(2)}) %all-to-all-start.1) | async-done | bytes 163872 | tf_op jit(solution)/shard_map/all_to_all | solution.py:353
  78.0 12.1 %all_to_all.15 = f32[16,40,128]{2,1,0:T(8,128)S(1)} all-to-all(f32[16,40,128]{2,1,0:T(8,128)S(1)} %shard_map.128), channel_id=1, replica_groups=mesh['z'=8,'y'=4,'xl'=2,'xh'=2,'c'=2] {'y','xl','xh'}, dimensions={0} | all-to-all | bytes 655360 | tf_op jit(solution)/shard_map/all_to_all | solution.py:353
  90.1 4.8 %collective-permute-start.9 = (f32[640,128]{1,0:T(8,128)S(1)}, f32[640,128]{1,0:T(8,128)S(1)}, u32[]{:S(2)}, u32[]{:S(2)}) collective-permute-start(f32[640,128]{1,0:T(8,128)S(1)} %bitcast.23), channel_id=1, source_target_pairs={{0,1},{1,0},{2,3},{3,2},{4,5},{5,4},{6,7},{7,6},{8,9},{9,8},{10,11... | collective-permute-start | bytes 983048 | tf_op jit(solution)/shard_map/ppermute | solution.py:349
  94.9 1.3 %collective-permute-done.9.other = f32[640,128]{1,0:T(8,128)S(1)} collective-permute-done((f32[640,128]{1,0:T(8,128)S(1)}, f32[640,128]{1,0:T(8,128)S(1)}, u32[]{:S(2)}, u32[]{:S(2)}) %collective-permute-start.9) | collective-permute-done | bytes 327712 | tf_op jit(solution)/shard_map/ppermute | solution.py:349
  96.2 1.7 %shard_map.129 = (f32[4,192,192]{2,1,0:T(8,128)}, f32[1,192]{1,0:T(1,128)}) custom-call(s32[2]{0:T(128)S(1)} %pad_add_fusion.place, f32[640,128]{1,0:T(8,128)S(1)} %bitcast.24, f32[640,128]{1,0:T(8,128)S(1)} %collective-permute-done.9.other), custom_call_target="tpu_custom_call" | custom-call | flops 1000000000 | bytes 3000000 | tf_op jit(solution)/shard_map/pallas_call | solution.py:409
  (31 shorter events, 0.3 us)
Async XLA Ops:
  0.6 1.0 %copy-start = (bf16[1,1,1024,192]{2,3,1,0:T(8,128)(2,1)S(1)}, bf16[1,1,1024,192]{2,3,1,0:T(8,128)(2,1)}, u32[]{:S(2)}) copy-start(bf16[1,1,1024,192]{2,3,1,0:T(8,128)(2,1)} %param.9) | copy-start | bytes 1179652
  1.6 6.5 %copy-start.11 = (s32[1,1,24,64]{3,2,1,0:T(8,128)S(1)}, s32[1,1,24,64]{3,2,1,0:T(8,128)}, u32[]{:S(2)}) copy-start(s32[1,1,24,64]{3,2,1,0:T(8,128)} %param.16) | copy-start | bytes 18436
  1.9 7.6 %collective-permute-start.1 = (bf16[64,192]{1,0:T(8,128)(2,1)S(1)}, bf16[64,192]{1,0:T(8,128)(2,1)S(1)}, u32[]{:S(2)}, u32[]{:S(2)}) collective-permute-start(bf16[64,192]{1,0:T(8,128)(2,1)S(1)} %shard_map.120.own), channel_id=1, source_target_pairs={{0,0},{1,2},{2,1},{3,3},{4,4},{5,6},{6,5},{7,7},{8,8},{9,10},{10,9... | collective-permute-start | bytes 73736 | tf_op jit(solution)/shard_map/ppermute | solution.py:345
  7.9 1.6 %collective-permute-start = (bf16[64,192]{1,0:T(8,128)(2,1)S(1)}, bf16[64,192]{1,0:T(8,128)(2,1)S(1)}, u32[]{:S(2)}, u32[]{:S(2)}) collective-permute-start(bf16[64,192]{1,0:T(8,128)(2,1)S(1)} %shard_map.120.own), channel_id=1, source_target_pairs={{0,1},{1,0},{2,3},{3,2},{4,5},{5,4},{6,7},{7,6},{8,9},{9,8},{10,11... | collective-permute-start | bytes 73736 | tf_op jit(solution)/shard_map/ppermute | solution.py:345
  8.9 5.6 %copy-start.1 = (bf16[1,1,1024,192]{2,3,1,0:T(8,128)(2,1)S(1)}, bf16[1,1,1024,192]{2,3,1,0:T(8,128)(2,1)}, u32[]{:S(2)}) copy-start(bf16[1,1,1024,192]{2,3,1,0:T(8,128)(2,1)} %param.9) | copy-start | bytes 1179652
  8.9 5.6 %copy-start.2 = (bf16[1,1,1024,192]{2,3,1,0:T(8,128)(2,1)S(1)}, bf16[1,1,1024,192]{2,3,1,0:T(8,128)(2,1)}, u32[]{:S(2)}) copy-start(bf16[1,1,1024,192]{2,3,1,0:T(8,128)(2,1)} %param.17) | copy-start | bytes 1179652
  9.0 5.6 %copy-start.3 = (bf16[192,192]{1,0:T(8,128)(2,1)S(1)}, bf16[192,192]{1,0:T(8,128)(2,1)}, u32[]{:S(2)}) copy-start(bf16[192,192]{1,0:T(8,128)(2,1)} %wq.1) | copy-start | bytes 221188
  9.0 5.6 %copy-start.4 = (bf16[192,192]{1,0:T(8,128)(2,1)S(1)}, bf16[192,192]{1,0:T(8,128)(2,1)}, u32[]{:S(2)}) copy-start(bf16[192,192]{1,0:T(8,128)(2,1)} %wk.1) | copy-start | bytes 221188
  9.0 5.6 %copy-start.5 = (bf16[192,192]{1,0:T(8,128)(2,1)S(1)}, bf16[192,192]{1,0:T(8,128)(2,1)}, u32[]{:S(2)}) copy-start(bf16[192,192]{1,0:T(8,128)(2,1)} %wv.1) | copy-start | bytes 221188
  9.0 5.6 %copy-start.6 = (bf16[192,192]{1,0:T(8,128)(2,1)S(1)}, bf16[192,192]{1,0:T(8,128)(2,1)}, u32[]{:S(2)}) copy-start(bf16[192,192]{1,0:T(8,128)(2,1)} %wo.1) | copy-start | bytes 221188
  9.0 5.6 %copy-start.7 = (f32[192]{0:T(256)S(1)}, f32[192]{0:T(256)}, u32[]{:S(2)}) copy-start(f32[192]{0:T(256)} %param.10) | copy-start | bytes 2308
  10.1 9.9 %collective-permute-start.3 = (bf16[192,192]{1,0:T(8,128)(2,1)S(1)}, bf16[192,192]{1,0:T(8,128)(2,1)S(1)}, u32[]{:S(2)}, u32[]{:S(2)}) collective-permute-start(bf16[192,192]{1,0:T(8,128)(2,1)S(1)} %shard_map.121.after.own_near), channel_id=1, source_target_pairs={{0,0},{4,8},{8,4},{12,16},{16,12},{20,24},{24,20},{28,32},{32,28},... | collective-permute-start | bytes 221192 | tf_op jit(solution)/shard_map/ppermute | solution.py:345
  10.7 9.2 %collective-permute-start.2 = (bf16[192,192]{1,0:T(8,128)(2,1)S(1)}, bf16[192,192]{1,0:T(8,128)(2,1)S(1)}, u32[]{:S(2)}, u32[]{:S(2)}) collective-permute-start(bf16[192,192]{1,0:T(8,128)(2,1)S(1)} %shard_map.121.after.own_near), channel_id=1, source_target_pairs={{0,4},{4,0},{8,12},{12,8},{16,20},{20,16},{24,28},{28,24},{32,36},... | collective-permute-start | bytes 221192 | tf_op jit(solution)/shard_map/ppermute | solution.py:345
  14.6 5.4 %copy-start.8 = (s32[1,1,24]{2,1,0:T(1,128)S(1)}, s32[1,1,24]{2,1,0:T(1,128)}, u32[]{:S(2)}) copy-start(s32[1,1,24]{2,1,0:T(1,128)} %param.15) | copy-start | bytes 292
  19.9 13.9 %copy-start.9 = (bf16[192,256]{1,0:T(8,128)(2,1)}, bf16[192,256]{1,0:T(8,128)(2,1)S(1)}, u32[]{:S(2)}) copy-start(bf16[192,256]{1,0:T(8,128)(2,1)S(1)} %get-tuple-element.36.w_back) | copy-start | bytes 294916
  33.8 8.4 %collective-permute-start.4 = (bf16[3,64,384]{2,1,0:T(8,128)(2,1)S(1)}, bf16[3,64,384]{2,1,0:T(8,128)(2,1)S(1)}, u32[]{:S(2)}, u32[]{:S(2)}) collective-permute-start(bf16[3,64,384]{2,1,0:T(8,128)(2,1)S(1)} %get-tuple-element.54), channel_id=1, source_target_pairs={{0,1},{1,0},{2,3},{3,2},{4,5},{5,4},{6,7},{7,6},{8,9},{9,8},{10,11... | collective-permute-start | bytes 442376 | tf_op jit(solution)/shard_map/ppermute | solution.py:345
  34.4 8.0 %collective-permute-start.5 = (bf16[3,64,384]{2,1,0:T(8,128)(2,1)S(1)}, bf16[3,64,384]{2,1,0:T(8,128)(2,1)S(1)}, u32[]{:S(2)}, u32[]{:S(2)}) collective-permute-start(bf16[3,64,384]{2,1,0:T(8,128)(2,1)S(1)} %get-tuple-element.55), channel_id=1, source_target_pairs={{0,0},{1,2},{2,1},{3,3},{4,4},{5,6},{6,5},{7,7},{8,8},{9,10},{10,9... | collective-permute-start | bytes 442376 | tf_op jit(solution)/shard_map/ppermute | solution.py:345
  43.9 1.7 %collective-permute-start.8 = (f32[640,128]{1,0:T(8,128)S(1)}, f32[640,128]{1,0:T(8,128)S(1)}, u32[]{:S(2)}, u32[]{:S(2)}) collective-permute-start(f32[640,128]{1,0:T(8,128)S(1)} %get-tuple-element.63), channel_id=1, source_target_pairs={{0,1},{1,0},{2,3},{3,2},{4,5},{5,4},{6,7},{7,6},{8,9},{9,8},{10,11... | collective-permute-start | bytes 983048 | tf_op jit(solution)/shard_map/ppermute | solution.py:349
  46.4 14.5 %all-to-all-start = ((f32[16,40,128]{2,1,0:T(8,128)}), f32[16,40,128]{2,1,0:T(8,128)S(1)}, u32[]{:S(2)}, u32[]{:S(2)}) async-start(f32[16,40,128]{2,1,0:T(8,128)} %bitcast.14), calls=%async_computation | async-start | bytes 655360 | tf_op jit(solution)/shard_map/all_to_all | solution.py:353
  53.2 6.2 %collective-permute-start.6 = (bf16[64,384]{1,0:T(8,128)(2,1)S(1)}, bf16[64,384]{1,0:T(8,128)(2,1)S(1)}, u32[]{:S(2)}, u32[]{:S(2)}) collective-permute-start(bf16[64,384]{1,0:T(8,128)(2,1)S(1)} %get-tuple-element.57), channel_id=1, source_target_pairs={{0,4},{4,0},{8,12},{12,8},{16,20},{20,16},{24,28},{28,24},{32,36},... | collective-permute-start | bytes 147464 | tf_op jit(solution)/shard_map/ppermute | solution.py:345
  54.6 15.1 %copy-start.10 = (bf16[192,256]{1,0:T(8,128)(2,1)S(1)}, bf16[192,256]{1,0:T(8,128)(2,1)}, u32[]{:S(2)}) copy-start(bf16[192,256]{1,0:T(8,128)(2,1)} %copy-done.9) | copy-start | bytes 294916
  54.6 15.1 %collective-permute-start.7 = (bf16[64,384]{1,0:T(8,128)(2,1)S(1)}, bf16[64,384]{1,0:T(8,128)(2,1)S(1)}, u32[]{:S(2)}, u32[]{:S(2)}) collective-permute-start(bf16[64,384]{1,0:T(8,128)(2,1)S(1)} %get-tuple-element.58), channel_id=1, source_target_pairs={{0,0},{4,8},{8,4},{12,16},{16,12},{20,24},{24,20},{28,32},{32,28},... | collective-permute-start | bytes 147464 | tf_op jit(solution)/shard_map/ppermute | solution.py:345
  61.6 16.4 %all-to-all-start.1 = ((f32[8,40,128]{2,1,0:T(8,128)}), f32[8,40,128]{2,1,0:T(8,128)S(1)}, u32[]{:S(2)}, u32[]{:S(2)}) async-start(f32[8,40,128]{2,1,0:T(8,128)} %shard_map.127), calls=%async_computation.1 | async-start | bytes 327680 | tf_op jit(solution)/shard_map/all_to_all | solution.py:353
  90.1 6.1 %collective-permute-start.9 = (f32[640,128]{1,0:T(8,128)S(1)}, f32[640,128]{1,0:T(8,128)S(1)}, u32[]{:S(2)}, u32[]{:S(2)}) collective-permute-start(f32[640,128]{1,0:T(8,128)S(1)} %bitcast.23), channel_id=1, source_target_pairs={{0,1},{1,0},{2,3},{3,2},{4,5},{5,4},{6,7},{7,6},{8,9},{9,8},{10,11... | collective-permute-start | bytes 983048 | tf_op jit(solution)/shard_map/ppermute | solution.py:349

commit v4 on v3

--- a/solution.py
+++ b/solution.py
@@ -26,7 +26,7 @@
 VMEM = pl.BlockSpec(memory_space=pltpu.VMEM)
 SMEM = pl.BlockSpec(memory_space=pltpu.SMEM)
 ANY = pl.BlockSpec(memory_space=pl.ANY)
-TOGETHER = 4
+TOGETHER = 6
 
 
 def nn(a, b):
@@ -92,7 +92,7 @@
             ref[rows, :] = x.astype(BF16).astype(F32)
         return 0
 
-    lax.fori_loop(0, PTS // chunk, project, 0)
+    lax.fori_loop(0, PTS // chunk, project, 0, unroll=8)
     zeros = jnp.zeros((WIN, 128), F32)
     for ref in (qa, ka, va, da, kvb, qdb):
         ref[PTS:, :] = zeros
@@ -103,7 +103,7 @@
         onehot[rows, :] = jnp.where(picks_col[rows, :] == ids, 1.0, 0.0).astype(BF16)
         return 0
 
-    lax.fori_loop(0, NWIN, rows_hot, 0)
+    lax.fori_loop(0, NWIN, rows_hot, 0, unroll=12)
 
     def columns_hot(i, _):
         rows = pl.ds(pl.multiple_of(i * SAMP, SAMP), SAMP)
@@ -111,7 +111,7 @@
         onehot_t[rows, :] = jnp.where(picks_row[...] == ids, 1.0, 0.0).astype(BF16)
         return 0
 
-    lax.fori_loop(0, 9, columns_hot, 0)
+    lax.fori_loop(0, 9, columns_hot, 0, unroll=9)
 
 
 def attend_kernel(lengths, place, own_near, first, second, gain, w_in, qa, ka, va, da, kvb, qdb, onehot, onehot_t,
@@ -128,12 +128,12 @@
     near_normed[...] = normed
     near_kv[...] = nn(normed, w_in[:, 128:512]).astype(BF16)
 
-    def choose(i, _):
-        rows = pl.ds(pl.multiple_of(i * 256, 256), 256)
+    def choose(group):
+        size = TOGETHER * WIN
+        rows = pl.ds(pl.multiple_of(group * size, size), size)
         pick[rows, :] = nn(onehot[rows, :], near_kv[...]).astype(BF16)
-        return 0
-
-    lax.fori_loop(0, NWIN * WIN // 256, choose, 0)
+
+    choose(0)
 
     lane_head = lax.broadcasted_iota(jnp.int32, (1, 128), 1) // DEPTH
     lanes = [jnp.where(lane_head == h, 1.0, 0.0).astype(BF16) for h in range(4)]
@@ -147,6 +147,13 @@
     def down(parts):
         return jnp.concatenate(parts, axis=0)
 
+    ones = jnp.ones((256, 128), BF16)
+
+    def row_sum(x):
+        high = x.astype(BF16)
+        low = (x - high.astype(F32)).astype(BF16)
+        return nn(jnp.concatenate([high, low], axis=1), ones)
+
     def softmax(scores, bias):
         scores = scores + bias
         top = jnp.max(scores, axis=-1, keepdims=True)
@@ -155,7 +162,7 @@
 
     def score_gradient(probs, d_probs):
         d_probs = d_probs.astype(BF16).astype(F32)
-        inner = jnp.sum(d_probs * probs, axis=-1, keepdims=True)
+        inner = row_sum(d_probs * probs)
         return (probs * (d_probs - inner)).astype(BF16)
 
     def cut(x):
@@ -217,6 +224,7 @@
             items.append(load(group * TOGETHER + j, offset))
             offset = offset + lengths[group * TOGETHER + j]
         found = [scored(item) for item in items]
+        choose(lax.rem(group + 1, NWIN // TOGETHER))
         found = [weighed(item, x) for item, x in zip(items, found)]
         for item, x in zip(items, found):
             stored(item, x)
@@ -236,22 +244,12 @@
         grads[:, 128 * i:128 * (i + 1)] = ref[:PTS, :].astype(BF16)
 
 
-def weights_kernel(points, cot, w_in, normed_t, grads, wide, out, gain_sum):
-    wide[...] = nn(normed_t[...], grads[:, 0:640])
-    out[...] = nn(cot[...], grads[:, 512:768])
-
-    def gain_part(i, total):
-        rows = pl.ds(pl.multiple_of(i * 128, 128), 128)
-        hat, _inv = standardize(points[:, rows].astype(F32), 0)
-        return total + nt(w_in[...], grads[rows, 0:640]) * hat
-
-    total = lax.fori_loop(0, PTS // 128, gain_part, jnp.zeros((C, 128), F32))
-    gain_sum[...] = jnp.sum(total.T, axis=0, keepdims=True)
-
-
-def near_kernel(place, w_in, wide, out, gain_sum, d_near, rest, near_hat, near_normed, got, got_too,
-                keep, send, first, second, middle, packed, sides):
-    near_wide = tn(near_normed[...], d_near[...]) + tn(near_normed[...], rest[...])
+def weights_kernel(points, cot, w_in, normed_t, grads, d_near, rest, near_hat, near_normed, place,
+                   keep, send, packed):
+    wide = nn(normed_t[...], grads[:, 0:640])
+    out = nn(cot[...], grads[:, 512:768])
+    near_wide = tn(near_normed[...], jnp.concatenate([d_near[...], rest[...]], axis=1))
+    near_wide = near_wide[:, 0:384] + near_wide[:, 384:768]
     packed[0:192, :] = wide[:, 0:128]
     packed[192:384, :] = wide[:, 128:256] + near_wide[:, 0:128]
     packed[384:576, :] = wide[:, 256:384] + near_wide[:, 128:256]
@@ -259,13 +257,26 @@
     packed[768:960, :] = wide[:, 384:512] + near_wide[:, 256:384]
     lane = lax.broadcasted_iota(jnp.int32, (C, 128), 1)
     packed[960:1152, :] = jnp.where(lane < 64, wide[:, 512:640], out[:, 0:128])
+
+    def gain_part(i, total):
+        rows = pl.ds(pl.multiple_of(i * 128, 128), 128)
+        hat, _inv = standardize(points[:, rows].astype(F32), 0)
+        return total + nt(w_in[...], grads[rows, 0:640]) * hat
+
+    total = lax.fori_loop(0, PTS // 128, gain_part, jnp.zeros((C, 128), F32), unroll=8)
     w_kv = w_in[:, 128:512]
     d = nt(d_near[...], w_kv) + nt(rest[...], w_kv)
     near_total = jnp.sum((d * near_hat[...]).reshape(NEAR // 8, 8, C), axis=0)
-    gains = gain_sum[...] + jnp.sum(near_total, axis=0, keepdims=True)
+    gains = jnp.sum(total.T, axis=0, keepdims=True) + jnp.sum(near_total, axis=0, keepdims=True)
     packed[1152:, :] = jnp.zeros((ROWS - 1152, 128), F32)
     packed[1152:1153, :] = gains[:, :128]
     packed[1153:1154, 0:64] = gains[:, 128:]
+    mine = place[1]
+    keep[...] = packed[pl.ds(pl.multiple_of(mine * HALF, HALF), HALF), :]
+    send[...] = packed[pl.ds(pl.multiple_of((1 - mine) * HALF, HALF), HALF), :]
+
+
+def sides_kernel(place, send, d_near, got, got_too, same, first, second, middle, sides):
     for i in range(3):
         own = d_near[192 * i + 64:192 * i + 128, :].astype(F32)
         sides[SAMP * i:SAMP * (i + 1), :] = own + got[i].astype(F32) + got_too[i].astype(F32)
@@ -273,9 +284,6 @@
     first[...] = sides[pl.ds(pl.multiple_of(2 * SAMP * (1 - odd), SAMP), SAMP), :].astype(BF16)
     second[...] = sides[pl.ds(pl.multiple_of(2 * SAMP * odd, SAMP), SAMP), :].astype(BF16)
     middle[...] = sides[SAMP:2 * SAMP, :]
-    mine = place[1]
-    keep[...] = packed[pl.ds(pl.multiple_of(mine * HALF, HALF), HALF), :]
-    send[...] = packed[pl.ds(pl.multiple_of((1 - mine) * HALF, HALF), HALF), :]
 
 
 def fold_kernel(after, parts, out):
@@ -310,7 +318,7 @@
         layer_out[:, rows] = (x + nt(w_back[...], grads[rows, 512:768])).astype(BF16)
         return 0
 
-    lax.fori_loop(0, PTS // chunk, part, 0)
+    lax.fori_loop(0, PTS // chunk, part, 0, unroll=8)
 
 
 def unpack_kernel(place, own, other, weights, gain_gradient, packed):
@@ -327,12 +335,13 @@
     gain_gradient[:, 128:C] = packed[1153:1154, 0:64]
 
 
-def call(kernel, outs, specs, scratch=(), limit=24, micros=1.0):
+def call(kernel, outs, specs, scratch=(), limit=24, micros=1.0, aliases=None):
     return pl.pallas_call(
         kernel,
         out_shape=[jax.ShapeDtypeStruct(s, t) for s, t in outs],
         in_specs=specs,
-        out_specs=[VMEM] * len(outs),
+        out_specs=[ANY if i in (aliases or {}).values() else VMEM for i in range(len(outs))],
+        input_output_aliases=aliases or {},
         scratch_shapes=[pltpu.VMEM(s, t) for s, t in scratch],
         cost_estimate=pl.CostEstimate(flops=int(micros * 1e9), bytes_accessed=int(micros * 3e6), transcendentals=0),
         compiler_params=pltpu.CompilerParams(vmem_limit_bytes=limit * 1024 * 1024),
@@ -380,18 +389,17 @@
     )(lengths, place, *near, gain.reshape(1, C), w_in, *projections, *hots)
 
 
-def local_weights(points, cotangent, w_in, normed_t, grads):
-    outs = [((C, 640), F32), ((C, 256), F32), ((1, C), F32)]
-    return call(weights_kernel, outs, [VMEM] * 5, limit=12, micros=3.0)(
-        points, cotangent, w_in, normed_t, grads)
-
-
-def local_near(place, w_in, sums, d_near, rest, near_hat, near_normed, got):
+def local_weights(points, cotangent, w_in, normed_t, grads, d_near, rest, near_hat, near_normed, place):
+    return call(weights_kernel, [((HALF, 128), F32)] * 2, [VMEM] * 9 + [SMEM], [((ROWS, 128), F32)],
+                limit=14, micros=3.0)(
+        points, cotangent, w_in, normed_t, grads, d_near, rest, near_hat, near_normed, place)
+
+
+def local_sides(place, send, d_near, got):
     side = ((SAMP, 2 * C), BF16)
-    outs = [((HALF, 128), F32)] * 2 + [side, side, ((SAMP, 2 * C), F32)]
-    scratch = [((ROWS, 128), F32), ((3 * SAMP, 2 * C), F32)]
-    return call(near_kernel, outs, [SMEM] + [VMEM] * 10, scratch, limit=12)(
-        place, w_in, *sums, d_near, rest, near_hat, near_normed, *got)
+    outs = [((HALF, 128), F32), side, side, ((SAMP, 2 * C), F32)]
+    return call(sides_kernel, outs, [SMEM, ANY] + [VMEM] * 3, [((3 * SAMP, 2 * C), F32)], limit=6,
+                aliases={1: 0})(place, send, d_near, *got)
 
 
 def local_finish(points, gain, w_in, w_back, cotangent, grads, middle, upper, lower):
@@ -426,9 +434,9 @@
     d_near, d_first, d_second, rest, grads, near_hat, near_normed = local_attend(
         lengths, place, near, gain, w_in, projections, hots)
     got = neighbours(d_first, d_second, GY, 4)
-    sums = local_weights(points, cotangent, w_in, normed_t, grads)
-    keep, send, first, second, middle = local_near(
-        place, w_in, sums, d_near, rest, near_hat, near_normed, got)
+    keep, send = local_weights(
+        points, cotangent, w_in, normed_t, grads, d_near, rest, near_hat, near_normed, place)
+    send, first, second, middle = local_sides(place, send, d_near, got)
     got = neighbours(first, second, GX, 64)
     layer_out, feature_gradient, token = local_finish(
         points, gain, w_in, w_back, cotangent, grads, middle, *got)

time: 98.4 us -> 92.8 us (0.943)
  Pallas kernels: 30.8 us -> 21.5 us
  waiting for transfers between devices: 12.9 us -> 18.3 us
  starting transfers between devices: 38.3 us -> 36.1 us
    pallas_call x1, Pallas kernels: 13.8 us -> 10.2 us  [local_attend(): call(attend_kernel, [near_out, side, side, near_out, ((PTS, 6 * 128), BF1...]
    pallas_call x1, Pallas kernels: 5.3 us -> 1.89 us  [local_prepare(): call(prepare_kernel, outs, [ANY] + [VMEM] * 9, limit=24, micros=5.0)]
    ppermute x4, waiting for transfers between devices: 4.09 us -> 6.44 us  [neighbours(): lax.ppermute(first, axes, pairs)]
    ppermute x4, waiting for transfers between devices: 0.72 us -> 2.52 us  [neighbours(): lax.ppermute(second, axes, across)]
    ppermute x4, starting transfers between devices: 12.7 us -> 11 us  [neighbours(): lax.ppermute(second, axes, across)]
    all_to_all x2, waiting for transfers between devices: 5.25 us -> 6.5 us  [exchanged(): return lax.all_to_all(x, axes, 0, 0, tiled=True)]
    pallas_call x1, Pallas kernels: 4.49 us -> 3.24 us  [local_finish(): call(finish_kernel, outs, [VMEM] * 9, [((SAMP, 2 * C), BF16)], limit=12,...]
    pallas_call x2, Pallas kernels: 4.04 us -> 3 us  [the longest x1 2.39 us: local_weights(): call(weights_kernel, [((HALF, 128), F32)] * 2, [VMEM] * 9 + [SMEM], [((RO...]
  transfers between devices with their start and end apart: 12 -> 12, of which waited for: 7 -> 8; matrix products, arithmetic and copies ran while one was open for 1% -> 1% of each run, Pallas kernels for 13% -> 9%
where the time goes in v4:
time: 92.8 us; the launch traced here: 92.3 us
  starting transfers between devices  36.1 us (39%)
  Pallas kernels  21.5 us (23%)
  waiting for transfers between devices  18.3 us (20%)
  blocking collectives  12.1 us (13%)
  local copies, waits for them, and re-layouts  2.5 us (3%)
    all_to_all x2, starting transfers between devices, exchanged(): return lax.all_to_all(x, axes, 0, 0, tiled=True)  14 us
    all_to_all x1, blocking collectives, exchanged(): return lax.all_to_all(x, axes, 0, 0, tiled=True)  12.1 us
    ppermute x4, starting transfers between devices, neighbours(): lax.ppermute(second, axes, across)  11 us
    pallas_call x1, Pallas kernels, local_attend(): call(attend_kernel, [near_out, side, side, near_out, ((PTS, 6 * 128), BF1...  10.2 us
    all_to_all x2, waiting for transfers between devices, exchanged(): return lax.all_to_all(x, axes, 0, 0, tiled=True)  6.5 us
    ppermute x4, waiting for transfers between devices, neighbours(): lax.ppermute(first, axes, pairs)  6.44 us
    ppermute x4, starting transfers between devices, neighbours(): lax.ppermute(first, axes, pairs)  6.15 us
    ppermute x2, starting transfers between devices, swapped(): return lax.ppermute(x, 'c', [(0, 1), (1, 0)])  4.9 us
  transfers between devices with their start and end apart: 12, of which 8 were waited for; matrix products, arithmetic and copies ran while one was open for 1% of the time, Pallas kernels for 9%

profile of v4, /device:TPU:1, one launch (start us, length us, event | category | flops | bytes accessed | tf_op | source)
XLA Modules:
  0.0 92.3 jit_solution(16152951380077063417)
XLA Ops:
  0.6 1.0 %copy-done = bf16[1,1,1024,192]{2,3,1,0:T(8,128)(2,1)S(1)} copy-done((bf16[1,1,1024,192]{2,3,1,0:T(8,128)(2,1)S(1)}, bf16[1,1,1024,192]{2,3,1,0:T(8,128)(2,1)}, u32[]{:S(2)}) %copy-start) | copy-done | bytes 393240
  1.6 0.2 shard_map.120.own
  1.9 6.0 %collective-permute-start.1 = (bf16[64,192]{1,0:T(8,128)(2,1)S(1)}, bf16[64,192]{1,0:T(8,128)(2,1)S(1)}, u32[]{:S(2)}, u32[]{:S(2)}) collective-permute-start(bf16[64,192]{1,0:T(8,128)(2,1)S(1)} %shard_map.120.own), channel_id=1, source_target_pairs={{0,0},{1,2},{2,1},{3,3},{4,4},{5,6},{6,5},{7,7},{8,8},{9,10},{10,9... | collective-permute-start | bytes 73736 | tf_op jit(solution)/shard_map/ppermute | solution.py:354
  8.2 0.7 reshape.38.picks_col
  9.0 0.5 collective-permute-done.1.second
  9.5 0.6 shard_map.121.after.own_near
  10.1 0.7 collective-permute-start.3
  10.7 3.8 %collective-permute-start.2 = (bf16[192,192]{1,0:T(8,128)(2,1)S(1)}, bf16[192,192]{1,0:T(8,128)(2,1)S(1)}, u32[]{:S(2)}, u32[]{:S(2)}) collective-permute-start(bf16[192,192]{1,0:T(8,128)(2,1)S(1)} %shard_map.121.after.own_near), channel_id=1, source_target_pairs={{0,4},{4,0},{8,12},{12,8},{16,20},{20,16},{24,28},{28,24},{32,36},... | collective-permute-start | bytes 221192 | tf_op jit(solution)/shard_map/ppermute | solution.py:354
  14.6 1.9 %shard_map.122 = (f32[1088,128]{1,0:T(8,128)S(1)}, f32[1088,128]{1,0:T(8,128)S(1)}, f32[1088,128]{1,0:T(8,128)S(1)}, f32[1088,128]{1,0:T(8,128)S(1)}, f32[1088,1...) custom-call(bf16[192,192]{1,0:T(8,128)(2,1)S(1)} %shard_map.121.afte, ...), custom_call_target="tpu_custom_call" | custom-call | flops 5000000000 | bytes 15000000 | tf_op jit(solution)/shard_map/pallas_call | solution.py:369
  16.5 0.6 copy-done.9
  17.2 2.3 %collective-permute-done.2.first = bf16[192,192]{1,0:T(8,128)(2,1)S(1)} collective-permute-done((bf16[192,192]{1,0:T(8,128)(2,1)S(1)}, bf16[192,192]{1,0:T(8,128)(2,1)S(1)}, u32[]{:S(2)}, u32[]{:S(2)}) %collective-permute-start.2) | collective-permute-done | bytes 73760 | tf_op jit(solution)/shard_map/ppermute | solution.py:354
  19.5 10.2 %shard_map.123 = (bf16[576,384]{1,0:T(8,128)(2,1)S(1)}, bf16[3,64,384]{2,1,0:T(8,128)(2,1)S(1)}, bf16[3,64,384]{2,1,0:T(8,128)(2,1)S(1)}, bf16[576,384]{1,0:T(8,...) custom-call(s32[24]{0:T(128)S(1)} %bitcast.35, ...), custom_call_target="tpu_custom_call" | custom-call | flops 14000000000 | bytes 42000000 | tf_op jit(solution)/shard_map/pallas_call | solution.py:383
  29.7 0.9 collective-permute-start.4
  30.6 3.5 %collective-permute-start.5 = (bf16[3,64,384]{2,1,0:T(8,128)(2,1)S(1)}, bf16[3,64,384]{2,1,0:T(8,128)(2,1)S(1)}, u32[]{:S(2)}, u32[]{:S(2)}) collective-permute-start(bf16[3,64,384]{2,1,0:T(8,128)(2,1)S(1)} %get-tuple-element.51), channel_id=1, source_target_pairs={{0,0},{1,2},{2,1},{3,3},{4,4},{5,6},{6,5},{7,7},{8,8},{9,10},{10,9... | collective-permute-start | bytes 442376 | tf_op jit(solution)/shard_map/ppermute | solution.py:354
  34.1 2.4 %shard_map.124 = (f32[640,128]{1,0:T(8,128)S(1)}, f32[640,128]{1,0:T(8,128)S(1)}) custom-call(bf16[192,1024]{1,0:T(8,128)(2,1)S(1)} %bitcast.27, bf16[192,1024]{1,0:T(8,128)(2,1)S(1)} %bitcast.30, bf16[192,640]{1,0:T(8,128)(2,1)S(1)} %get-tuple-element.33.w_in, bf16[192,1024]{1,0:T(8,128)(2,1)S(1)} %get-tuple-element.44.normed_t, ...), custom_call_target="tpu_custom_call" | custom-call | flops 3000000000 | bytes 9000000 | tf_op jit(solution)/shard_map/pallas_call | solution.py:393
  36.5 2.0 %collective-permute-done.5.got_too = bf16[3,64,384]{2,1,0:T(8,128)(2,1)S(1)} collective-permute-done((bf16[3,64,384]{2,1,0:T(8,128)(2,1)S(1)}, bf16[3,64,384]{2,1,0:T(8,128)(2,1)S(1)}, u32[]{:S(2)}, u32[]{:S(2)}) %collective-permute-start.5) | collective-permute-done | bytes 147488 | tf_op jit(solution)/shard_map/ppermute | solution.py:354
  38.5 0.6 shard_map.125
  39.2 1.6 %collective-permute-done.8 = f32[640,128]{1,0:T(8,128)S(1)} collective-permute-done((f32[640,128]{1,0:T(8,128)S(1)}, f32[640,128]{1,0:T(8,128)S(1)}, u32[]{:S(2)}, u32[]{:S(2)}) %collective-permute-start.8) | collective-permute-done | bytes 327712 | tf_op jit(solution)/shard_map/ppermute | solution.py:358
  40.8 0.8 add.3
  41.6 5.9 %all-to-all-start = ((f32[16,40,128]{2,1,0:T(8,128)}), f32[16,40,128]{2,1,0:T(8,128)S(1)}, u32[]{:S(2)}, u32[]{:S(2)}) async-start(f32[16,40,128]{2,1,0:T(8,128)} %bitcast.36), calls=%async_computation | async-start | bytes 655360 | tf_op jit(solution)/shard_map/all_to_all | solution.py:362
  47.5 1.4 %collective-permute-start.6 = (bf16[64,384]{1,0:T(8,128)(2,1)S(1)}, bf16[64,384]{1,0:T(8,128)(2,1)S(1)}, u32[]{:S(2)}, u32[]{:S(2)}) collective-permute-start(bf16[64,384]{1,0:T(8,128)(2,1)S(1)} %get-tuple-element.53), channel_id=1, source_target_pairs={{0,4},{4,0},{8,12},{12,8},{16,20},{20,16},{24,28},{28,24},{32,36},... | collective-permute-start | bytes 147464 | tf_op jit(solution)/shard_map/ppermute | solution.py:354
  48.8 0.8 collective-permute-start.7
  49.6 4.1 %collective-permute-done.6.upper.after = bf16[64,384]{1,0:T(8,128)(2,1)S(1)} collective-permute-done((bf16[64,384]{1,0:T(8,128)(2,1)S(1)}, bf16[64,384]{1,0:T(8,128)(2,1)S(1)}, u32[]{:S(2)}, u32[]{:S(2)}) %collective-permute-start.6) | collective-permute-done | bytes 49184 | tf_op jit(solution)/shard_map/ppermute | solution.py:354
  53.7 1.5 %all-to-all-done.parts = f32[16,40,128]{2,1,0:T(8,128)S(1)} async-done(((f32[16,40,128]{2,1,0:T(8,128)}), f32[16,40,128]{2,1,0:T(8,128)S(1)}, u32[]{:S(2)}, u32[]{:S(2)}) %all-to-all-start) | async-done | bytes 327712 | tf_op jit(solution)/shard_map/all_to_all | solution.py:362
  55.2 0.7 shard_map.127
  55.9 8.2 %all-to-all-start.1 = ((f32[8,40,128]{2,1,0:T(8,128)}), f32[8,40,128]{2,1,0:T(8,128)S(1)}, u32[]{:S(2)}, u32[]{:S(2)}) async-start(f32[8,40,128]{2,1,0:T(8,128)} %shard_map.127), calls=%async_computation.1 | async-start | bytes 327680 | tf_op jit(solution)/shard_map/all_to_all | solution.py:362
  64.1 3.2 %shard_map.126 = (bf16[192,1024]{1,0:T(8,128)(2,1)}, f32[192,1024]{1,0:T(8,128)}, f32[8,128]{1,0:T(8,128)S(1)}) custom-call(bf16[192,1024]{1,0:T(8,128)(2,1)S(1)} %bitcast.28, f32[1,192]{1,0:T(1,128)S(1)} %bitcast.34, bf16[192,640]{1,0:T(8,128)(2,1)S(1)} %get-tuple-element.33.w_in, bf16[192,256]{1,0:T(8,128)(2,1)S(1)} %copy-done.10, ...), custom_call_target="tpu_custom_call" | custom-call | flops 4000000000 | bytes 12000000 | tf_op jit(solution)/shard_map/pallas_call | solution.py:407
  67.3 5.0 %all-to-all-done.1.parts = f32[8,40,128]{2,1,0:T(8,128)S(1)} async-done(((f32[8,40,128]{2,1,0:T(8,128)}), f32[8,40,128]{2,1,0:T(8,128)S(1)}, u32[]{:S(2)}, u32[]{:S(2)}) %all-to-all-start.1) | async-done | bytes 163872 | tf_op jit(solution)/shard_map/all_to_all | solution.py:362
  72.4 12.1 %all_to_all.15 = f32[16,40,128]{2,1,0:T(8,128)S(1)} all-to-all(f32[16,40,128]{2,1,0:T(8,128)S(1)} %shard_map.128), channel_id=1, replica_groups=mesh['z'=8,'y'=4,'xl'=2,'xh'=2,'c'=2] {'y','xl','xh'}, dimensions={0} | all-to-all | bytes 655360 | tf_op jit(solution)/shard_map/all_to_all | solution.py:362
  84.5 4.8 %collective-permute-start.9 = (f32[640,128]{1,0:T(8,128)S(1)}, f32[640,128]{1,0:T(8,128)S(1)}, u32[]{:S(2)}, u32[]{:S(2)}) collective-permute-start(f32[640,128]{1,0:T(8,128)S(1)} %bitcast.23), channel_id=1, source_target_pairs={{0,1},{1,0},{2,3},{3,2},{4,5},{5,4},{6,7},{7,6},{8,9},{9,8},{10,11... | collective-permute-start | bytes 983048 | tf_op jit(solution)/shard_map/ppermute | solution.py:358
  89.3 1.3 %collective-permute-done.9.other = f32[640,128]{1,0:T(8,128)S(1)} collective-permute-done((f32[640,128]{1,0:T(8,128)S(1)}, f32[640,128]{1,0:T(8,128)S(1)}, u32[]{:S(2)}, u32[]{:S(2)}) %collective-permute-start.9) | collective-permute-done | bytes 327712 | tf_op jit(solution)/shard_map/ppermute | solution.py:358
  90.6 1.7 %shard_map.129 = (f32[4,192,192]{2,1,0:T(8,128)}, f32[1,192]{1,0:T(1,128)}) custom-call(s32[2]{0:T(128)S(1)} %pad_add_fusion.place, f32[640,128]{1,0:T(8,128)S(1)} %bitcast.24, f32[640,128]{1,0:T(8,128)S(1)} %collective-permute-done.9.other), custom_call_target="tpu_custom_call" | custom-call | flops 1000000000 | bytes 3000000 | tf_op jit(solution)/shard_map/pallas_call | solution.py:417
  (31 shorter events, 0.4 us)
Async XLA Ops:
  0.6 1.0 %copy-start = (bf16[1,1,1024,192]{2,3,1,0:T(8,128)(2,1)S(1)}, bf16[1,1,1024,192]{2,3,1,0:T(8,128)(2,1)}, u32[]{:S(2)}) copy-start(bf16[1,1,1024,192]{2,3,1,0:T(8,128)(2,1)} %param.9) | copy-start | bytes 1179652
  1.6 6.5 %copy-start.11 = (s32[1,1,24,64]{3,2,1,0:T(8,128)S(1)}, s32[1,1,24,64]{3,2,1,0:T(8,128)}, u32[]{:S(2)}) copy-start(s32[1,1,24,64]{3,2,1,0:T(8,128)} %param.16) | copy-start | bytes 18436
  1.9 7.6 %collective-permute-start.1 = (bf16[64,192]{1,0:T(8,128)(2,1)S(1)}, bf16[64,192]{1,0:T(8,128)(2,1)S(1)}, u32[]{:S(2)}, u32[]{:S(2)}) collective-permute-start(bf16[64,192]{1,0:T(8,128)(2,1)S(1)} %shard_map.120.own), channel_id=1, source_target_pairs={{0,0},{1,2},{2,1},{3,3},{4,4},{5,6},{6,5},{7,7},{8,8},{9,10},{10,9... | collective-permute-start | bytes 73736 | tf_op jit(solution)/shard_map/ppermute | solution.py:354
  7.9 1.6 %collective-permute-start = (bf16[64,192]{1,0:T(8,128)(2,1)S(1)}, bf16[64,192]{1,0:T(8,128)(2,1)S(1)}, u32[]{:S(2)}, u32[]{:S(2)}) collective-permute-start(bf16[64,192]{1,0:T(8,128)(2,1)S(1)} %shard_map.120.own), channel_id=1, source_target_pairs={{0,1},{1,0},{2,3},{3,2},{4,5},{5,4},{6,7},{7,6},{8,9},{9,8},{10,11... | collective-permute-start | bytes 73736 | tf_op jit(solution)/shard_map/ppermute | solution.py:354
  8.9 5.6 %copy-start.1 = (bf16[1,1,1024,192]{2,3,1,0:T(8,128)(2,1)S(1)}, bf16[1,1,1024,192]{2,3,1,0:T(8,128)(2,1)}, u32[]{:S(2)}) copy-start(bf16[1,1,1024,192]{2,3,1,0:T(8,128)(2,1)} %param.9) | copy-start | bytes 1179652
  8.9 5.6 %copy-start.2 = (bf16[1,1,1024,192]{2,3,1,0:T(8,128)(2,1)S(1)}, bf16[1,1,1024,192]{2,3,1,0:T(8,128)(2,1)}, u32[]{:S(2)}) copy-start(bf16[1,1,1024,192]{2,3,1,0:T(8,128)(2,1)} %param.17) | copy-start | bytes 1179652
  9.0 5.6 %copy-start.3 = (bf16[192,192]{1,0:T(8,128)(2,1)S(1)}, bf16[192,192]{1,0:T(8,128)(2,1)}, u32[]{:S(2)}) copy-start(bf16[192,192]{1,0:T(8,128)(2,1)} %wq.1) | copy-start | bytes 221188
  9.0 5.6 %copy-start.4 = (bf16[192,192]{1,0:T(8,128)(2,1)S(1)}, bf16[192,192]{1,0:T(8,128)(2,1)}, u32[]{:S(2)}) copy-start(bf16[192,192]{1,0:T(8,128)(2,1)} %wk.1) | copy-start | bytes 221188
  9.0 5.6 %copy-start.5 = (bf16[192,192]{1,0:T(8,128)(2,1)S(1)}, bf16[192,192]{1,0:T(8,128)(2,1)}, u32[]{:S(2)}) copy-start(bf16[192,192]{1,0:T(8,128)(2,1)} %wv.1) | copy-start | bytes 221188
  9.0 5.6 %copy-start.6 = (bf16[192,192]{1,0:T(8,128)(2,1)S(1)}, bf16[192,192]{1,0:T(8,128)(2,1)}, u32[]{:S(2)}) copy-start(bf16[192,192]{1,0:T(8,128)(2,1)} %wo.1) | copy-start | bytes 221188
  9.0 5.6 %copy-start.7 = (f32[192]{0:T(256)S(1)}, f32[192]{0:T(256)}, u32[]{:S(2)}) copy-start(f32[192]{0:T(256)} %param.10) | copy-start | bytes 2308
  10.1 7.1 %collective-permute-start.3 = (bf16[192,192]{1,0:T(8,128)(2,1)S(1)}, bf16[192,192]{1,0:T(8,128)(2,1)S(1)}, u32[]{:S(2)}, u32[]{:S(2)}) collective-permute-start(bf16[192,192]{1,0:T(8,128)(2,1)S(1)} %shard_map.121.after.own_near), channel_id=1, source_target_pairs={{0,0},{4,8},{8,4},{12,16},{16,12},{20,24},{24,20},{28,32},{32,28},... | collective-permute-start | bytes 221192 | tf_op jit(solution)/shard_map/ppermute | solution.py:354
  10.7 8.8 %collective-permute-start.2 = (bf16[192,192]{1,0:T(8,128)(2,1)S(1)}, bf16[192,192]{1,0:T(8,128)(2,1)S(1)}, u32[]{:S(2)}, u32[]{:S(2)}) collective-permute-start(bf16[192,192]{1,0:T(8,128)(2,1)S(1)} %shard_map.121.after.own_near), channel_id=1, source_target_pairs={{0,4},{4,0},{8,12},{12,8},{16,20},{20,16},{24,28},{28,24},{32,36},... | collective-permute-start | bytes 221192 | tf_op jit(solution)/shard_map/ppermute | solution.py:354
  14.6 4.9 %copy-start.8 = (s32[1,1,24]{2,1,0:T(1,128)S(1)}, s32[1,1,24]{2,1,0:T(1,128)}, u32[]{:S(2)}) copy-start(s32[1,1,24]{2,1,0:T(1,128)} %param.15) | copy-start | bytes 292
  16.5 0.6 copy-start.9
  29.7 6.8 %collective-permute-start.4 = (bf16[3,64,384]{2,1,0:T(8,128)(2,1)S(1)}, bf16[3,64,384]{2,1,0:T(8,128)(2,1)S(1)}, u32[]{:S(2)}, u32[]{:S(2)}) collective-permute-start(bf16[3,64,384]{2,1,0:T(8,128)(2,1)S(1)} %get-tuple-element.50), channel_id=1, source_target_pairs={{0,1},{1,0},{2,3},{3,2},{4,5},{5,4},{6,7},{7,6},{8,9},{9,8},{10,11... | collective-permute-start | bytes 442376 | tf_op jit(solution)/shard_map/ppermute | solution.py:354
  30.6 8.0 %collective-permute-start.5 = (bf16[3,64,384]{2,1,0:T(8,128)(2,1)S(1)}, bf16[3,64,384]{2,1,0:T(8,128)(2,1)S(1)}, u32[]{:S(2)}, u32[]{:S(2)}) collective-permute-start(bf16[3,64,384]{2,1,0:T(8,128)(2,1)S(1)} %get-tuple-element.51), channel_id=1, source_target_pairs={{0,0},{1,2},{2,1},{3,3},{4,4},{5,6},{6,5},{7,7},{8,8},{9,10},{10,9... | collective-permute-start | bytes 442376 | tf_op jit(solution)/shard_map/ppermute | solution.py:354
  39.1 1.7 %collective-permute-start.8 = (f32[640,128]{1,0:T(8,128)S(1)}, f32[640,128]{1,0:T(8,128)S(1)}, u32[]{:S(2)}, u32[]{:S(2)}) collective-permute-start(f32[640,128]{1,0:T(8,128)S(1)} %get-tuple-element.59), channel_id=1, source_target_pairs={{0,1},{1,0},{2,3},{3,2},{4,5},{5,4},{6,7},{7,6},{8,9},{9,8},{10,11... | collective-permute-start | bytes 983048 | tf_op jit(solution)/shard_map/ppermute | solution.py:358
  41.6 13.6 %all-to-all-start = ((f32[16,40,128]{2,1,0:T(8,128)}), f32[16,40,128]{2,1,0:T(8,128)S(1)}, u32[]{:S(2)}, u32[]{:S(2)}) async-start(f32[16,40,128]{2,1,0:T(8,128)} %bitcast.36), calls=%async_computation | async-start | bytes 655360 | tf_op jit(solution)/shard_map/all_to_all | solution.py:362
  47.5 6.2 %collective-permute-start.6 = (bf16[64,384]{1,0:T(8,128)(2,1)S(1)}, bf16[64,384]{1,0:T(8,128)(2,1)S(1)}, u32[]{:S(2)}, u32[]{:S(2)}) collective-permute-start(bf16[64,384]{1,0:T(8,128)(2,1)S(1)} %get-tuple-element.53), channel_id=1, source_target_pairs={{0,4},{4,0},{8,12},{12,8},{16,20},{20,16},{24,28},{28,24},{32,36},... | collective-permute-start | bytes 147464 | tf_op jit(solution)/shard_map/ppermute | solution.py:354
  48.8 15.2 %copy-start.10 = (bf16[192,256]{1,0:T(8,128)(2,1)S(1)}, bf16[192,256]{1,0:T(8,128)(2,1)}, u32[]{:S(2)}) copy-start(bf16[192,256]{1,0:T(8,128)(2,1)} %copy-done.9) | copy-start | bytes 294916
  48.8 15.2 %collective-permute-start.7 = (bf16[64,384]{1,0:T(8,128)(2,1)S(1)}, bf16[64,384]{1,0:T(8,128)(2,1)S(1)}, u32[]{:S(2)}, u32[]{:S(2)}) collective-permute-start(bf16[64,384]{1,0:T(8,128)(2,1)S(1)} %get-tuple-element.54), channel_id=1, source_target_pairs={{0,0},{4,8},{8,4},{12,16},{16,12},{20,24},{24,20},{28,32},{32,28},... | collective-permute-start | bytes 147464 | tf_op jit(solution)/shard_map/ppermute | solution.py:354
  55.9 16.5 %all-to-all-start.1 = ((f32[8,40,128]{2,1,0:T(8,128)}), f32[8,40,128]{2,1,0:T(8,128)S(1)}, u32[]{:S(2)}, u32[]{:S(2)}) async-start(f32[8,40,128]{2,1,0:T(8,128)} %shard_map.127), calls=%async_computation.1 | async-start | bytes 327680 | tf_op jit(solution)/shard_map/all_to_all | solution.py:362
  84.5 6.1 %collective-permute-start.9 = (f32[640,128]{1,0:T(8,128)S(1)}, f32[640,128]{1,0:T(8,128)S(1)}, u32[]{:S(2)}, u32[]{:S(2)}) collective-permute-start(f32[640,128]{1,0:T(8,128)S(1)} %bitcast.23), channel_id=1, source_target_pairs={{0,1},{1,0},{2,3},{3,2},{4,5},{5,4},{6,7},{7,6},{8,9},{9,8},{10,11... | collective-permute-start | bytes 983048 | tf_op jit(solution)/shard_map/ppermute | solution.py:358

commit v5 on v4

--- a/solution.py
+++ b/solution.py
@@ -276,7 +276,7 @@
     send[...] = packed[pl.ds(pl.multiple_of((1 - mine) * HALF, HALF), HALF), :]
 
 
-def sides_kernel(place, send, d_near, got, got_too, same, first, second, middle, sides):
+def sides_kernel(place, d_near, got, got_too, first, second, middle, sides):
     for i in range(3):
         own = d_near[192 * i + 64:192 * i + 128, :].astype(F32)
         sides[SAMP * i:SAMP * (i + 1), :] = own + got[i].astype(F32) + got_too[i].astype(F32)
@@ -395,11 +395,11 @@
         points, cotangent, w_in, normed_t, grads, d_near, rest, near_hat, near_normed, place)
 
 
-def local_sides(place, send, d_near, got):
+def local_sides(place, d_near, got):
     side = ((SAMP, 2 * C), BF16)
-    outs = [((HALF, 128), F32), side, side, ((SAMP, 2 * C), F32)]
-    return call(sides_kernel, outs, [SMEM, ANY] + [VMEM] * 3, [((3 * SAMP, 2 * C), F32)], limit=6,
-                aliases={1: 0})(place, send, d_near, *got)
+    outs = [side, side, ((SAMP, 2 * C), F32)]
+    return call(sides_kernel, outs, [SMEM] + [VMEM] * 3, [((3 * SAMP, 2 * C), F32)], limit=6)(
+        place, d_near, *got)
 
 
 def local_finish(points, gain, w_in, w_back, cotangent, grads, middle, upper, lower):
@@ -436,13 +436,13 @@
     got = neighbours(d_first, d_second, GY, 4)
     keep, send = local_weights(
         points, cotangent, w_in, normed_t, grads, d_near, rest, near_hat, near_normed, place)
-    send, first, second, middle = local_sides(place, send, d_near, got)
+    mixed = exchanged((keep + swapped(send)).reshape(16, HALF // 16, 128), XY)
+    mixed = exchanged(local_fold(got[0], mixed, 8), "z")
+    first, second, middle = local_sides(place, d_near, got)
     got = neighbours(first, second, GX, 64)
+    own = exchanged(local_fold(got[0], mixed, 16), XY).reshape(HALF, 128)
     layer_out, feature_gradient, token = local_finish(
         points, gain, w_in, w_back, cotangent, grads, middle, *got)
-    mixed = exchanged((keep + swapped(send)).reshape(16, HALF // 16, 128), XY)
-    mixed = exchanged(local_fold(got[0], mixed, 8), "z")
-    own = exchanged(local_fold(token, mixed, 16), XY).reshape(HALF, 128)
     weights, gain_gradient = local_unpack(place, own, swapped(own))
     return layer_out.T[None, None], feature_gradient.T[None, None], weights, gain_gradient.reshape(C)
 

time: 92.8 us -> 88.3 us (0.952)
  blocking collectives: 12.1 us -> 0 us
  starting transfers between devices: 36.1 us -> 40.8 us
  waiting for transfers between devices: 18.3 us -> 21.1 us
    all_to_all x1 -> x0, blocking collectives: 12.1 us -> none  [exchanged(): return lax.all_to_all(x, axes, 0, 0, tiled=True)]
    all_to_all x2 -> x3, waiting for transfers between devices: 6.5 us -> 13.7 us  [exchanged(): return lax.all_to_all(x, axes, 0, 0, tiled=True)]
    all_to_all x2 -> x3, starting transfers between devices: 14 us -> 18.3 us  [exchanged(): return lax.all_to_all(x, axes, 0, 0, tiled=True)]
    ppermute x4, waiting for transfers between devices: 2.52 us -> 0.5 us  [neighbours(): lax.ppermute(second, axes, across)]
    ppermute x2, waiting for transfers between devices: 2.87 us -> 1.26 us  [swapped(): return lax.ppermute(x, 'c', [(0, 1), (1, 0)])]
    ppermute x4, starting transfers between devices: 11 us -> 12.2 us  [neighbours(): lax.ppermute(second, axes, across)]
    ppermute x4, starting transfers between devices: 6.15 us -> 4.98 us  [neighbours(): lax.ppermute(first, axes, pairs)]
  transfers between devices with their start and end apart: 12 -> 13, of which waited for: 8 -> 7; matrix products, arithmetic and copies ran while one was open for 1% -> 1% of each run, Pallas kernels for 9% -> 7%
where the time goes in v5:
time: 88.3 us; the launch traced here: 87.8 us
  starting transfers between devices  40.8 us (46%)
  Pallas kernels  22.2 us (25%)
  waiting for transfers between devices  21.1 us (24%)
  local copies, waits for them, and re-layouts  1.88 us (2%)
  between operations  0.93 us (1%)
    all_to_all x3, starting transfers between devices, exchanged(): return lax.all_to_all(x, axes, 0, 0, tiled=True)  18.3 us
    all_to_all x3, waiting for transfers between devices, exchanged(): return lax.all_to_all(x, axes, 0, 0, tiled=True)  13.7 us
    ppermute x4, starting transfers between devices, neighbours(): lax.ppermute(second, axes, across)  12.2 us
    pallas_call x1, Pallas kernels, local_attend(): call(attend_kernel, [near_out, side, side, near_out, ((PTS, 6 * 128), BF1...  10.2 us
    ppermute x4, waiting for transfers between devices, neighbours(): lax.ppermute(first, axes, pairs)  5.67 us
    ppermute x2, starting transfers between devices, swapped(): return lax.ppermute(x, 'c', [(0, 1), (1, 0)])  5.28 us
    ppermute x4, starting transfers between devices, neighbours(): lax.ppermute(first, axes, pairs)  4.98 us
    pallas_call x1, Pallas kernels, local_finish(): call(finish_kernel, outs, [VMEM] * 9, [((SAMP, 2 * C), BF16)], limit=12,...  3.22 us
  transfers between devices with their start and end apart: 13, of which 7 were waited for; matrix products, arithmetic and copies ran while one was open for 1% of the time, Pallas kernels for 7%

profile of v5, /device:TPU:1, one launch (start us, length us, event | category | flops | bytes accessed | tf_op | source)
XLA Modules:
  0.0 87.8 jit_solution(6729422357984789312)
XLA Ops:
  0.6 1.0 %copy-done = bf16[1,1,1024,192]{2,3,1,0:T(8,128)(2,1)S(1)} copy-done((bf16[1,1,1024,192]{2,3,1,0:T(8,128)(2,1)S(1)}, bf16[1,1,1024,192]{2,3,1,0:T(8,128)(2,1)}, u32[]{:S(2)}) %copy-start) | copy-done | bytes 393240
  1.6 0.2 shard_map.120.own
  1.9 6.0 %collective-permute-start.1 = (bf16[64,192]{1,0:T(8,128)(2,1)S(1)}, bf16[64,192]{1,0:T(8,128)(2,1)S(1)}, u32[]{:S(2)}, u32[]{:S(2)}) collective-permute-start(bf16[64,192]{1,0:T(8,128)(2,1)S(1)} %shard_map.120.own), channel_id=1, source_target_pairs={{0,0},{1,2},{2,1},{3,3},{4,4},{5,6},{6,5},{7,7},{8,8},{9,10},{10,9... | collective-permute-start | bytes 73736 | tf_op jit(solution)/shard_map/ppermute | solution.py:354
  8.2 0.7 reshape.38.picks_col
  9.0 0.5 collective-permute-done.1.second
  9.5 0.6 shard_map.121.after.own_near
  10.1 0.7 collective-permute-start.3
  10.7 3.8 %collective-permute-start.2 = (bf16[192,192]{1,0:T(8,128)(2,1)S(1)}, bf16[192,192]{1,0:T(8,128)(2,1)S(1)}, u32[]{:S(2)}, u32[]{:S(2)}) collective-permute-start(bf16[192,192]{1,0:T(8,128)(2,1)S(1)} %shard_map.121.after.own_near), channel_id=1, source_target_pairs={{0,4},{4,0},{8,12},{12,8},{16,20},{20,16},{24,28},{28,24},{32,36},... | collective-permute-start | bytes 221192 | tf_op jit(solution)/shard_map/ppermute | solution.py:354
  14.6 1.9 %shard_map.122 = (f32[1088,128]{1,0:T(8,128)S(1)}, f32[1088,128]{1,0:T(8,128)S(1)}, f32[1088,128]{1,0:T(8,128)S(1)}, f32[1088,128]{1,0:T(8,128)S(1)}, f32[1088,1...) custom-call(bf16[192,192]{1,0:T(8,128)(2,1)S(1)} %shard_map.121.afte, ...), custom_call_target="tpu_custom_call" | custom-call | flops 5000000000 | bytes 15000000 | tf_op jit(solution)/shard_map/pallas_call | solution.py:369
  16.5 3.0 %collective-permute-done.2.first = bf16[192,192]{1,0:T(8,128)(2,1)S(1)} collective-permute-done((bf16[192,192]{1,0:T(8,128)(2,1)S(1)}, bf16[192,192]{1,0:T(8,128)(2,1)S(1)}, u32[]{:S(2)}, u32[]{:S(2)}) %collective-permute-start.2) | collective-permute-done | bytes 73760 | tf_op jit(solution)/shard_map/ppermute | solution.py:354
  19.5 10.2 %shard_map.123 = (bf16[576,384]{1,0:T(8,128)(2,1)S(1)}, bf16[3,64,384]{2,1,0:T(8,128)(2,1)S(1)}, bf16[3,64,384]{2,1,0:T(8,128)(2,1)S(1)}, bf16[576,384]{1,0:T(8,...) custom-call(s32[24]{0:T(128)S(1)} %bitcast.35, ...), custom_call_target="tpu_custom_call" | custom-call | flops 14000000000 | bytes 42000000 | tf_op jit(solution)/shard_map/pallas_call | solution.py:383
  29.7 2.4 %shard_map.126 = (f32[640,128]{1,0:T(8,128)S(1)}, f32[640,128]{1,0:T(8,128)S(1)}) custom-call(bf16[192,1024]{1,0:T(8,128)(2,1)S(1)} %bitcast.27, bf16[192,1024]{1,0:T(8,128)(2,1)S(1)} %bitcast.30, bf16[192,640]{1,0:T(8,128)(2,1)S(1)} %get-tuple-element.31.w_in, bf16[192,1024]{1,0:T(8,128)(2,1)S(1)} %get-tuple-element.50.normed_t, ...), custom_call_target="tpu_custom_call" | custom-call | flops 3000000000 | bytes 9000000 | tf_op jit(solution)/shard_map/pallas_call | solution.py:393
  32.1 0.9 %collective-permute-start.8 = (f32[640,128]{1,0:T(8,128)S(1)}, f32[640,128]{1,0:T(8,128)S(1)}, u32[]{:S(2)}, u32[]{:S(2)}) collective-permute-start(f32[640,128]{1,0:T(8,128)S(1)} %get-tuple-element.55), channel_id=1, source_target_pairs={{0,1},{1,0},{2,3},{3,2},{4,5},{5,4},{6,7},{7,6},{8,9},{9,8},{10,11... | collective-permute-start | bytes 983048 | tf_op jit(solution)/shard_map/ppermute | solution.py:358
  33.0 1.3 %collective-permute-done.8 = f32[640,128]{1,0:T(8,128)S(1)} collective-permute-done((f32[640,128]{1,0:T(8,128)S(1)}, f32[640,128]{1,0:T(8,128)S(1)}, u32[]{:S(2)}, u32[]{:S(2)}) %collective-permute-start.8) | collective-permute-done | bytes 327712 | tf_op jit(solution)/shard_map/ppermute | solution.py:358
  34.3 0.8 add.3
  35.0 6.2 %all-to-all-start = ((f32[16,40,128]{2,1,0:T(8,128)}), f32[16,40,128]{2,1,0:T(8,128)S(1)}, u32[]{:S(2)}, u32[]{:S(2)}) async-start(f32[16,40,128]{2,1,0:T(8,128)} %bitcast.14), calls=%async_computation | async-start | bytes 655360 | tf_op jit(solution)/shard_map/all_to_all | solution.py:362
  41.2 0.7 collective-permute-start.4
  42.0 4.9 %collective-permute-start.5 = (bf16[3,64,384]{2,1,0:T(8,128)(2,1)S(1)}, bf16[3,64,384]{2,1,0:T(8,128)(2,1)S(1)}, u32[]{:S(2)}, u32[]{:S(2)}) collective-permute-start(bf16[3,64,384]{2,1,0:T(8,128)(2,1)S(1)} %get-tuple-element.44), channel_id=1, source_target_pairs={{0,0},{1,2},{2,1},{3,3},{4,4},{5,6},{6,5},{7,7},{8,8},{9,10},{10,9... | collective-permute-start | bytes 442376 | tf_op jit(solution)/shard_map/ppermute | solution.py:354
  46.9 2.1 %all-to-all-done.parts = f32[16,40,128]{2,1,0:T(8,128)S(1)} async-done(((f32[16,40,128]{2,1,0:T(8,128)}), f32[16,40,128]{2,1,0:T(8,128)S(1)}, u32[]{:S(2)}, u32[]{:S(2)}) %all-to-all-start) | async-done | bytes 327712 | tf_op jit(solution)/shard_map/all_to_all | solution.py:362
  49.0 0.7 shard_map.127
  49.7 8.2 %all-to-all-start.1 = ((f32[8,40,128]{2,1,0:T(8,128)}), f32[8,40,128]{2,1,0:T(8,128)S(1)}, u32[]{:S(2)}, u32[]{:S(2)}) async-start(f32[8,40,128]{2,1,0:T(8,128)} %shard_map.127), calls=%async_computation.1 | async-start | bytes 327680 | tf_op jit(solution)/shard_map/all_to_all | solution.py:362
  57.9 0.6 shard_map.124
  58.5 0.3 collective-permute-start.6
  58.8 2.7 %collective-permute-done.6.upper.after = bf16[64,384]{1,0:T(8,128)(2,1)S(1)} collective-permute-done((bf16[64,384]{1,0:T(8,128)(2,1)S(1)}, bf16[64,384]{1,0:T(8,128)(2,1)S(1)}, u32[]{:S(2)}, u32[]{:S(2)}) %collective-permute-start.6) | collective-permute-done | bytes 49184 | tf_op jit(solution)/shard_map/ppermute | solution.py:354
  61.5 4.7 %all-to-all-done.1.parts = f32[8,40,128]{2,1,0:T(8,128)S(1)} async-done(((f32[8,40,128]{2,1,0:T(8,128)}), f32[8,40,128]{2,1,0:T(8,128)S(1)}, u32[]{:S(2)}, u32[]{:S(2)}) %all-to-all-start.1) | async-done | bytes 163872 | tf_op jit(solution)/shard_map/all_to_all | solution.py:362
  66.3 0.8 shard_map.128
  67.0 3.9 %all-to-all-start.2 = ((f32[16,40,128]{2,1,0:T(8,128)}), f32[16,40,128]{2,1,0:T(8,128)S(1)}, u32[]{:S(2)}, u32[]{:S(2)}) async-start(f32[16,40,128]{2,1,0:T(8,128)} %shard_map.128), calls=%async_computation.2 | async-start | bytes 655360 | tf_op jit(solution)/shard_map/all_to_all | solution.py:362
  70.9 0.7 collective-permute-start.7
  71.6 6.9 %all-to-all-done.2 = f32[16,40,128]{2,1,0:T(8,128)S(1)} async-done(((f32[16,40,128]{2,1,0:T(8,128)}), f32[16,40,128]{2,1,0:T(8,128)S(1)}, u32[]{:S(2)}, u32[]{:S(2)}) %all-to-all-start.2) | async-done | bytes 327712 | tf_op jit(solution)/shard_map/all_to_all | solution.py:362
  78.5 4.4 %collective-permute-start.9 = (f32[640,128]{1,0:T(8,128)S(1)}, f32[640,128]{1,0:T(8,128)S(1)}, u32[]{:S(2)}, u32[]{:S(2)}) collective-permute-start(f32[640,128]{1,0:T(8,128)S(1)} %bitcast.23), channel_id=1, source_target_pairs={{0,1},{1,0},{2,3},{3,2},{4,5},{5,4},{6,7},{7,6},{8,9},{9,8},{10,11... | collective-permute-start | bytes 983048 | tf_op jit(solution)/shard_map/ppermute | solution.py:358
  82.9 3.2 %shard_map.125 = (bf16[192,1024]{1,0:T(8,128)(2,1)}, f32[192,1024]{1,0:T(8,128)}, f32[8,128]{1,0:T(8,128)}) custom-call(bf16[192,1024]{1,0:T(8,128)(2,1)S(1)} %bitcast.28, f32[1,192]{1,0:T(1,128)S(1)} %bitcast.34, bf16[192,640]{1,0:T(8,128)(2,1)S(1)} %get-tuple-element.31.w_in, bf16[192,256]{1,0:T(8,128)(2,1)S(1)} %copy-done.12, ...), custom_call_target="tpu_custom_call" | custom-call | flops 4000000000 | bytes 12000000 | tf_op jit(solution)/shard_map/pallas_call | solution.py:407
  86.1 1.7 %shard_map.129 = (f32[4,192,192]{2,1,0:T(8,128)}, f32[1,192]{1,0:T(1,128)}) custom-call(s32[2]{0:T(128)S(1)} %pad_add_fusion.place, f32[640,128]{1,0:T(8,128)S(1)} %bitcast.24, f32[640,128]{1,0:T(8,128)S(1)} %collective-permute-done.9.other), custom_call_target="tpu_custom_call" | custom-call | flops 1000000000 | bytes 3000000 | tf_op jit(solution)/shard_map/pallas_call | solution.py:417
  (36 shorter events, 0.3 us)
Async XLA Ops:
  0.6 1.0 %copy-start = (bf16[1,1,1024,192]{2,3,1,0:T(8,128)(2,1)S(1)}, bf16[1,1,1024,192]{2,3,1,0:T(8,128)(2,1)}, u32[]{:S(2)}) copy-start(bf16[1,1,1024,192]{2,3,1,0:T(8,128)(2,1)} %param.9) | copy-start | bytes 1179652
  1.6 6.5 %copy-start.13 = (s32[1,1,24,64]{3,2,1,0:T(8,128)S(1)}, s32[1,1,24,64]{3,2,1,0:T(8,128)}, u32[]{:S(2)}) copy-start(s32[1,1,24,64]{3,2,1,0:T(8,128)} %param.16) | copy-start | bytes 18436
  1.9 7.6 %collective-permute-start.1 = (bf16[64,192]{1,0:T(8,128)(2,1)S(1)}, bf16[64,192]{1,0:T(8,128)(2,1)S(1)}, u32[]{:S(2)}, u32[]{:S(2)}) collective-permute-start(bf16[64,192]{1,0:T(8,128)(2,1)S(1)} %shard_map.120.own), channel_id=1, source_target_pairs={{0,0},{1,2},{2,1},{3,3},{4,4},{5,6},{6,5},{7,7},{8,8},{9,10},{10,9... | collective-permute-start | bytes 73736 | tf_op jit(solution)/shard_map/ppermute | solution.py:354
  7.9 1.6 %collective-permute-start = (bf16[64,192]{1,0:T(8,128)(2,1)S(1)}, bf16[64,192]{1,0:T(8,128)(2,1)S(1)}, u32[]{:S(2)}, u32[]{:S(2)}) collective-permute-start(bf16[64,192]{1,0:T(8,128)(2,1)S(1)} %shard_map.120.own), channel_id=1, source_target_pairs={{0,1},{1,0},{2,3},{3,2},{4,5},{5,4},{6,7},{7,6},{8,9},{9,8},{10,11... | collective-permute-start | bytes 73736 | tf_op jit(solution)/shard_map/ppermute | solution.py:354
  8.9 5.6 %copy-start.1 = (bf16[1,1,1024,192]{2,3,1,0:T(8,128)(2,1)S(1)}, bf16[1,1,1024,192]{2,3,1,0:T(8,128)(2,1)}, u32[]{:S(2)}) copy-start(bf16[1,1,1024,192]{2,3,1,0:T(8,128)(2,1)} %param.9) | copy-start | bytes 1179652
  8.9 5.6 %copy-start.2 = (bf16[1,1,1024,192]{2,3,1,0:T(8,128)(2,1)S(1)}, bf16[1,1,1024,192]{2,3,1,0:T(8,128)(2,1)}, u32[]{:S(2)}) copy-start(bf16[1,1,1024,192]{2,3,1,0:T(8,128)(2,1)} %param.17) | copy-start | bytes 1179652
  9.0 5.6 %copy-start.3 = (bf16[192,192]{1,0:T(8,128)(2,1)S(1)}, bf16[192,192]{1,0:T(8,128)(2,1)}, u32[]{:S(2)}) copy-start(bf16[192,192]{1,0:T(8,128)(2,1)} %wq.1) | copy-start | bytes 221188
  9.0 5.6 %copy-start.4 = (bf16[192,192]{1,0:T(8,128)(2,1)S(1)}, bf16[192,192]{1,0:T(8,128)(2,1)}, u32[]{:S(2)}) copy-start(bf16[192,192]{1,0:T(8,128)(2,1)} %wk.1) | copy-start | bytes 221188
  9.0 5.6 %copy-start.5 = (bf16[192,192]{1,0:T(8,128)(2,1)S(1)}, bf16[192,192]{1,0:T(8,128)(2,1)}, u32[]{:S(2)}) copy-start(bf16[192,192]{1,0:T(8,128)(2,1)} %wv.1) | copy-start | bytes 221188
  9.0 5.6 %copy-start.6 = (bf16[192,192]{1,0:T(8,128)(2,1)S(1)}, bf16[192,192]{1,0:T(8,128)(2,1)}, u32[]{:S(2)}) copy-start(bf16[192,192]{1,0:T(8,128)(2,1)} %wo.1) | copy-start | bytes 221188
  9.0 5.6 %copy-start.7 = (f32[192]{0:T(256)S(1)}, f32[192]{0:T(256)}, u32[]{:S(2)}) copy-start(f32[192]{0:T(256)} %param.10) | copy-start | bytes 2308
  10.1 6.4 %collective-permute-start.3 = (bf16[192,192]{1,0:T(8,128)(2,1)S(1)}, bf16[192,192]{1,0:T(8,128)(2,1)S(1)}, u32[]{:S(2)}, u32[]{:S(2)}) collective-permute-start(bf16[192,192]{1,0:T(8,128)(2,1)S(1)} %shard_map.121.after.own_near), channel_id=1, source_target_pairs={{0,0},{4,8},{8,4},{12,16},{16,12},{20,24},{24,20},{28,32},{32,28},... | collective-permute-start | bytes 221192 | tf_op jit(solution)/shard_map/ppermute | solution.py:354
  10.7 8.8 %collective-permute-start.2 = (bf16[192,192]{1,0:T(8,128)(2,1)S(1)}, bf16[192,192]{1,0:T(8,128)(2,1)S(1)}, u32[]{:S(2)}, u32[]{:S(2)}) collective-permute-start(bf16[192,192]{1,0:T(8,128)(2,1)S(1)} %shard_map.121.after.own_near), channel_id=1, source_target_pairs={{0,4},{4,0},{8,12},{12,8},{16,20},{20,16},{24,28},{28,24},{32,36},... | collective-permute-start | bytes 221192 | tf_op jit(solution)/shard_map/ppermute | solution.py:354
  14.6 4.9 %copy-start.8 = (s32[1,1,24]{2,1,0:T(1,128)S(1)}, s32[1,1,24]{2,1,0:T(1,128)}, u32[]{:S(2)}) copy-start(s32[1,1,24]{2,1,0:T(1,128)} %param.15) | copy-start | bytes 292
  16.5 13.2 %copy-start.11 = (bf16[192,256]{1,0:T(8,128)(2,1)}, bf16[192,256]{1,0:T(8,128)(2,1)S(1)}, u32[]{:S(2)}) copy-start(bf16[192,256]{1,0:T(8,128)(2,1)S(1)} %get-tuple-element.32.w_back) | copy-start | bytes 294916
  29.7 2.4 %copy-start.9 = (bf16[1024,768]{1,0:T(8,128)(2,1)}, bf16[1024,768]{1,0:T(8,128)(2,1)S(1)}, u32[]{:S(2)}) copy-start(bf16[1024,768]{1,0:T(8,128)(2,1)S(1)} %get-tuple-element.41.grads) | copy-start | bytes 4718596
  32.1 2.1 %collective-permute-start.8 = (f32[640,128]{1,0:T(8,128)S(1)}, f32[640,128]{1,0:T(8,128)S(1)}, u32[]{:S(2)}, u32[]{:S(2)}) collective-permute-start(f32[640,128]{1,0:T(8,128)S(1)} %get-tuple-element.55), channel_id=1, source_target_pairs={{0,1},{1,0},{2,3},{3,2},{4,5},{5,4},{6,7},{7,6},{8,9},{9,8},{10,11... | collective-permute-start | bytes 983048 | tf_op jit(solution)/shard_map/ppermute | solution.py:358
  35.0 13.9 %all-to-all-start = ((f32[16,40,128]{2,1,0:T(8,128)}), f32[16,40,128]{2,1,0:T(8,128)S(1)}, u32[]{:S(2)}, u32[]{:S(2)}) async-start(f32[16,40,128]{2,1,0:T(8,128)} %bitcast.14), calls=%async_computation | async-start | bytes 655360 | tf_op jit(solution)/shard_map/all_to_all | solution.py:362
  41.2 5.6 %collective-permute-start.4 = (bf16[3,64,384]{2,1,0:T(8,128)(2,1)S(1)}, bf16[3,64,384]{2,1,0:T(8,128)(2,1)S(1)}, u32[]{:S(2)}, u32[]{:S(2)}) collective-permute-start(bf16[3,64,384]{2,1,0:T(8,128)(2,1)S(1)} %get-tuple-element.43), channel_id=1, source_target_pairs={{0,1},{1,0},{2,3},{3,2},{4,5},{5,4},{6,7},{7,6},{8,9},{9,8},{10,11... | collective-permute-start | bytes 442376 | tf_op jit(solution)/shard_map/ppermute | solution.py:354
  42.0 15.9 %collective-permute-start.5 = (bf16[3,64,384]{2,1,0:T(8,128)(2,1)S(1)}, bf16[3,64,384]{2,1,0:T(8,128)(2,1)S(1)}, u32[]{:S(2)}, u32[]{:S(2)}) collective-permute-start(bf16[3,64,384]{2,1,0:T(8,128)(2,1)S(1)} %get-tuple-element.44), channel_id=1, source_target_pairs={{0,0},{1,2},{2,1},{3,3},{4,4},{5,6},{6,5},{7,7},{8,8},{9,10},{10,9... | collective-permute-start | bytes 442376 | tf_op jit(solution)/shard_map/ppermute | solution.py:354
  49.7 16.6 %all-to-all-start.1 = ((f32[8,40,128]{2,1,0:T(8,128)}), f32[8,40,128]{2,1,0:T(8,128)S(1)}, u32[]{:S(2)}, u32[]{:S(2)}) async-start(f32[8,40,128]{2,1,0:T(8,128)} %shard_map.127), calls=%async_computation.1 | async-start | bytes 327680 | tf_op jit(solution)/shard_map/all_to_all | solution.py:362
  58.5 24.4 %copy-start.10 = (bf16[1024,768]{1,0:T(8,128)(2,1)S(1)}, bf16[1024,768]{1,0:T(8,128)(2,1)}, u32[]{:S(2)}) copy-start(bf16[1024,768]{1,0:T(8,128)(2,1)} %copy-done.9) | copy-start | bytes 4718596
  58.5 24.4 %copy-start.12 = (bf16[192,256]{1,0:T(8,128)(2,1)S(1)}, bf16[192,256]{1,0:T(8,128)(2,1)}, u32[]{:S(2)}) copy-start(bf16[192,256]{1,0:T(8,128)(2,1)} %copy-done.11) | copy-start | bytes 294916
  58.5 3.0 %collective-permute-start.6 = (bf16[64,384]{1,0:T(8,128)(2,1)S(1)}, bf16[64,384]{1,0:T(8,128)(2,1)S(1)}, u32[]{:S(2)}, u32[]{:S(2)}) collective-permute-start(bf16[64,384]{1,0:T(8,128)(2,1)S(1)} %get-tuple-element.46), channel_id=1, source_target_pairs={{0,4},{4,0},{8,12},{12,8},{16,20},{20,16},{24,28},{28,24},{32,36},... | collective-permute-start | bytes 147464 | tf_op jit(solution)/shard_map/ppermute | solution.py:354
  67.0 11.5 %all-to-all-start.2 = ((f32[16,40,128]{2,1,0:T(8,128)}), f32[16,40,128]{2,1,0:T(8,128)S(1)}, u32[]{:S(2)}, u32[]{:S(2)}) async-start(f32[16,40,128]{2,1,0:T(8,128)} %shard_map.128), calls=%async_computation.2 | async-start | bytes 655360 | tf_op jit(solution)/shard_map/all_to_all | solution.py:362
  70.9 12.0 %collective-permute-start.7 = (bf16[64,384]{1,0:T(8,128)(2,1)S(1)}, bf16[64,384]{1,0:T(8,128)(2,1)S(1)}, u32[]{:S(2)}, u32[]{:S(2)}) collective-permute-start(bf16[64,384]{1,0:T(8,128)(2,1)S(1)} %get-tuple-element.47), channel_id=1, source_target_pairs={{0,0},{4,8},{8,4},{12,16},{16,12},{20,24},{24,20},{28,32},{32,28},... | collective-permute-start | bytes 147464 | tf_op jit(solution)/shard_map/ppermute | solution.py:354
  78.5 7.6 %collective-permute-start.9 = (f32[640,128]{1,0:T(8,128)S(1)}, f32[640,128]{1,0:T(8,128)S(1)}, u32[]{:S(2)}, u32[]{:S(2)}) collective-permute-start(f32[640,128]{1,0:T(8,128)S(1)} %bitcast.23), channel_id=1, source_target_pairs={{0,1},{1,0},{2,3},{3,2},{4,5},{5,4},{6,7},{7,6},{8,9},{9,8},{10,11... | collective-permute-start | bytes 983048 | tf_op jit(solution)/shard_map/ppermute | solution.py:358

commit v6 on v5

--- a/solution.py
+++ b/solution.py
@@ -321,18 +321,28 @@
     lax.fori_loop(0, PTS // chunk, part, 0, unroll=8)
 
 
-def unpack_kernel(place, own, other, weights, gain_gradient, packed):
-    mine = place[1]
+def unpack_kernel(place, own, other, weights, gain_gradient):
     factor = (PTS * 256) ** (-0.5)
-    packed[pl.ds(pl.multiple_of(mine * HALF, HALF), HALF), :] = own[...] * factor
-    packed[pl.ds(pl.multiple_of((1 - mine) * HALF, HALF), HALF), :] = other[...] * factor
-    for i, (tail, side) in enumerate(((960, 0), (768, 0), (768, 64))):
-        weights[i, :, 0:128] = packed[192 * i:192 * (i + 1), :]
-        weights[i, :, 128:C] = packed[tail:tail + 192, side:side + 64]
-    weights[3, 0:128, :] = packed[576:768, :].T
-    weights[3, 128:C, :] = packed[960:1152, :].T[64:128, :]
-    gain_gradient[:, 0:128] = packed[1152:1153, :]
-    gain_gradient[:, 128:C] = packed[1153:1154, 0:64]
+
+    def write(low, high):
+        for i in range(3):
+            weights[i, :, 0:128] = low[192 * i:192 * (i + 1), :] * factor
+        weights[0, :, 128:C] = high[320:512, 0:64] * factor
+        weights[1, :, 128:C] = high[128:320, 0:64] * factor
+        weights[2, :, 128:C] = high[128:320, 64:128] * factor
+        weights[3, 0:128, 0:64] = (low[576:640, :] * factor).T
+        weights[3, 0:128, 64:C] = (high[0:128, :] * factor).T
+        weights[3, 128:C, :] = (high[320:512, :] * factor).T[64:128, :]
+        gain_gradient[:, 0:128] = high[512:513, :] * factor
+        gain_gradient[:, 128:C] = high[513:514, 0:64] * factor
+
+    @pl.when(place[1] == 0)
+    def _():
+        write(own, other)
+
+    @pl.when(place[1] != 0)
+    def _():
+        write(other, own)
 
 
 def call(kernel, outs, specs, scratch=(), limit=24, micros=1.0, aliases=None):
@@ -415,7 +425,7 @@
 
 def local_unpack(place, own, other):
     return call(
-        unpack_kernel, [((4, C, C), F32), ((1, C), F32)], [SMEM, VMEM, VMEM], [((ROWS, 128), F32)],
+        unpack_kernel, [((4, C, C), F32), ((1, C), F32)], [SMEM, VMEM, VMEM],
         limit=8, micros=1.0,
     )(place, own, other)
 

time: 88.3 us -> 88.3 us (level)
  no operation moved by 1% of the time
where the time goes in v6:
time: 88.3 us; the launch traced here: 87.8 us
  starting transfers between devices  40.8 us (46%)
  Pallas kernels  22.2 us (25%)
  waiting for transfers between devices  21.1 us (24%)
  local copies, waits for them, and re-layouts  1.88 us (2%)
  between operations  0.93 us (1%)
    all_to_all x3, starting transfers between devices, exchanged(): return lax.all_to_all(x, axes, 0, 0, tiled=True)  18.3 us
    all_to_all x3, waiting for transfers between devices, exchanged(): return lax.all_to_all(x, axes, 0, 0, tiled=True)  13.7 us
    ppermute x4, starting transfers between devices, neighbours(): lax.ppermute(second, axes, across)  12.2 us
    pallas_call x1, Pallas kernels, local_attend(): call(attend_kernel, [near_out, side, side, near_out, ((PTS, 6 * 128), BF1...  10.2 us
    ppermute x4, waiting for transfers between devices, neighbours(): lax.ppermute(first, axes, pairs)  5.67 us
    ppermute x2, starting transfers between devices, swapped(): return lax.ppermute(x, 'c', [(0, 1), (1, 0)])  5.27 us
    ppermute x4, starting transfers between devices, neighbours(): lax.ppermute(first, axes, pairs)  4.98 us
    pallas_call x1, Pallas kernels, local_finish(): call(finish_kernel, outs, [VMEM] * 9, [((SAMP, 2 * C), BF16)], limit=12,...  3.22 us
  transfers between devices with their start and end apart: 13, of which 7 were waited for; matrix products, arithmetic and copies ran while one was open for 1% of the time, Pallas kernels for 7%

profile of v6, /device:TPU:1, one launch (start us, length us, event | category | flops | bytes accessed | tf_op | source)
XLA Modules:
  0.0 87.8 jit_solution(7409544410671043958)
XLA Ops:
  0.6 1.0 %copy-done = bf16[1,1,1024,192]{2,3,1,0:T(8,128)(2,1)S(1)} copy-done((bf16[1,1,1024,192]{2,3,1,0:T(8,128)(2,1)S(1)}, bf16[1,1,1024,192]{2,3,1,0:T(8,128)(2,1)}, u32[]{:S(2)}) %copy-start) | copy-done | bytes 393240
  1.6 0.2 shard_map.120.own
  1.9 6.0 %collective-permute-start.1 = (bf16[64,192]{1,0:T(8,128)(2,1)S(1)}, bf16[64,192]{1,0:T(8,128)(2,1)S(1)}, u32[]{:S(2)}, u32[]{:S(2)}) collective-permute-start(bf16[64,192]{1,0:T(8,128)(2,1)S(1)} %shard_map.120.own), channel_id=1, source_target_pairs={{0,0},{1,2},{2,1},{3,3},{4,4},{5,6},{6,5},{7,7},{8,8},{9,10},{10,9... | collective-permute-start | bytes 73736 | tf_op jit(solution)/shard_map/ppermute | solution.py:364
  8.2 0.7 reshape.38.picks_col
  9.0 0.5 collective-permute-done.1.second
  9.5 0.6 shard_map.121.after.own_near
  10.1 0.7 collective-permute-start.3
  10.7 3.8 %collective-permute-start.2 = (bf16[192,192]{1,0:T(8,128)(2,1)S(1)}, bf16[192,192]{1,0:T(8,128)(2,1)S(1)}, u32[]{:S(2)}, u32[]{:S(2)}) collective-permute-start(bf16[192,192]{1,0:T(8,128)(2,1)S(1)} %shard_map.121.after.own_near), channel_id=1, source_target_pairs={{0,4},{4,0},{8,12},{12,8},{16,20},{20,16},{24,28},{28,24},{32,36},... | collective-permute-start | bytes 221192 | tf_op jit(solution)/shard_map/ppermute | solution.py:364
  14.6 1.9 %shard_map.122 = (f32[1088,128]{1,0:T(8,128)S(1)}, f32[1088,128]{1,0:T(8,128)S(1)}, f32[1088,128]{1,0:T(8,128)S(1)}, f32[1088,128]{1,0:T(8,128)S(1)}, f32[1088,1...) custom-call(bf16[192,192]{1,0:T(8,128)(2,1)S(1)} %shard_map.121.afte, ...), custom_call_target="tpu_custom_call" | custom-call | flops 5000000000 | bytes 15000000 | tf_op jit(solution)/shard_map/pallas_call | solution.py:379
  16.5 3.0 %collective-permute-done.2.first = bf16[192,192]{1,0:T(8,128)(2,1)S(1)} collective-permute-done((bf16[192,192]{1,0:T(8,128)(2,1)S(1)}, bf16[192,192]{1,0:T(8,128)(2,1)S(1)}, u32[]{:S(2)}, u32[]{:S(2)}) %collective-permute-start.2) | collective-permute-done | bytes 73760 | tf_op jit(solution)/shard_map/ppermute | solution.py:364
  19.5 10.2 %shard_map.123 = (bf16[576,384]{1,0:T(8,128)(2,1)S(1)}, bf16[3,64,384]{2,1,0:T(8,128)(2,1)S(1)}, bf16[3,64,384]{2,1,0:T(8,128)(2,1)S(1)}, bf16[576,384]{1,0:T(8,...) custom-call(s32[24]{0:T(128)S(1)} %bitcast.35, ...), custom_call_target="tpu_custom_call" | custom-call | flops 14000000000 | bytes 42000000 | tf_op jit(solution)/shard_map/pallas_call | solution.py:393
  29.7 2.4 %shard_map.126 = (f32[640,128]{1,0:T(8,128)S(1)}, f32[640,128]{1,0:T(8,128)S(1)}) custom-call(bf16[192,1024]{1,0:T(8,128)(2,1)S(1)} %bitcast.27, bf16[192,1024]{1,0:T(8,128)(2,1)S(1)} %bitcast.30, bf16[192,640]{1,0:T(8,128)(2,1)S(1)} %get-tuple-element.31.w_in, bf16[192,1024]{1,0:T(8,128)(2,1)S(1)} %get-tuple-element.50.normed_t, ...), custom_call_target="tpu_custom_call" | custom-call | flops 3000000000 | bytes 9000000 | tf_op jit(solution)/shard_map/pallas_call | solution.py:403
  32.1 0.9 %collective-permute-start.8 = (f32[640,128]{1,0:T(8,128)S(1)}, f32[640,128]{1,0:T(8,128)S(1)}, u32[]{:S(2)}, u32[]{:S(2)}) collective-permute-start(f32[640,128]{1,0:T(8,128)S(1)} %get-tuple-element.55), channel_id=1, source_target_pairs={{0,1},{1,0},{2,3},{3,2},{4,5},{5,4},{6,7},{7,6},{8,9},{9,8},{10,11... | collective-permute-start | bytes 983048 | tf_op jit(solution)/shard_map/ppermute | solution.py:368
  33.0 1.3 %collective-permute-done.8 = f32[640,128]{1,0:T(8,128)S(1)} collective-permute-done((f32[640,128]{1,0:T(8,128)S(1)}, f32[640,128]{1,0:T(8,128)S(1)}, u32[]{:S(2)}, u32[]{:S(2)}) %collective-permute-start.8) | collective-permute-done | bytes 327712 | tf_op jit(solution)/shard_map/ppermute | solution.py:368
  34.3 0.8 add.3
  35.0 6.2 %all-to-all-start = ((f32[16,40,128]{2,1,0:T(8,128)}), f32[16,40,128]{2,1,0:T(8,128)S(1)}, u32[]{:S(2)}, u32[]{:S(2)}) async-start(f32[16,40,128]{2,1,0:T(8,128)} %bitcast.14), calls=%async_computation | async-start | bytes 655360 | tf_op jit(solution)/shard_map/all_to_all | solution.py:372
  41.2 0.7 collective-permute-start.4
  42.0 4.9 %collective-permute-start.5 = (bf16[3,64,384]{2,1,0:T(8,128)(2,1)S(1)}, bf16[3,64,384]{2,1,0:T(8,128)(2,1)S(1)}, u32[]{:S(2)}, u32[]{:S(2)}) collective-permute-start(bf16[3,64,384]{2,1,0:T(8,128)(2,1)S(1)} %get-tuple-element.44), channel_id=1, source_target_pairs={{0,0},{1,2},{2,1},{3,3},{4,4},{5,6},{6,5},{7,7},{8,8},{9,10},{10,9... | collective-permute-start | bytes 442376 | tf_op jit(solution)/shard_map/ppermute | solution.py:364
  46.9 2.1 %all-to-all-done.parts = f32[16,40,128]{2,1,0:T(8,128)S(1)} async-done(((f32[16,40,128]{2,1,0:T(8,128)}), f32[16,40,128]{2,1,0:T(8,128)S(1)}, u32[]{:S(2)}, u32[]{:S(2)}) %all-to-all-start) | async-done | bytes 327712 | tf_op jit(solution)/shard_map/all_to_all | solution.py:372
  49.0 0.7 shard_map.127
  49.7 8.2 %all-to-all-start.1 = ((f32[8,40,128]{2,1,0:T(8,128)}), f32[8,40,128]{2,1,0:T(8,128)S(1)}, u32[]{:S(2)}, u32[]{:S(2)}) async-start(f32[8,40,128]{2,1,0:T(8,128)} %shard_map.127), calls=%async_computation.1 | async-start | bytes 327680 | tf_op jit(solution)/shard_map/all_to_all | solution.py:372
  57.8 0.6 shard_map.124
  58.5 0.3 collective-permute-start.6
  58.8 2.7 %collective-permute-done.6.upper.after = bf16[64,384]{1,0:T(8,128)(2,1)S(1)} collective-permute-done((bf16[64,384]{1,0:T(8,128)(2,1)S(1)}, bf16[64,384]{1,0:T(8,128)(2,1)S(1)}, u32[]{:S(2)}, u32[]{:S(2)}) %collective-permute-start.6) | collective-permute-done | bytes 49184 | tf_op jit(solution)/shard_map/ppermute | solution.py:364
  61.5 4.7 %all-to-all-done.1.parts = f32[8,40,128]{2,1,0:T(8,128)S(1)} async-done(((f32[8,40,128]{2,1,0:T(8,128)}), f32[8,40,128]{2,1,0:T(8,128)S(1)}, u32[]{:S(2)}, u32[]{:S(2)}) %all-to-all-start.1) | async-done | bytes 163872 | tf_op jit(solution)/shard_map/all_to_all | solution.py:372
  66.2 0.8 shard_map.128
  67.0 3.9 %all-to-all-start.2 = ((f32[16,40,128]{2,1,0:T(8,128)}), f32[16,40,128]{2,1,0:T(8,128)S(1)}, u32[]{:S(2)}, u32[]{:S(2)}) async-start(f32[16,40,128]{2,1,0:T(8,128)} %shard_map.128), calls=%async_computation.2 | async-start | bytes 655360 | tf_op jit(solution)/shard_map/all_to_all | solution.py:372
  70.9 0.7 collective-permute-start.7
  71.6 6.9 %all-to-all-done.2 = f32[16,40,128]{2,1,0:T(8,128)S(1)} async-done(((f32[16,40,128]{2,1,0:T(8,128)}), f32[16,40,128]{2,1,0:T(8,128)S(1)}, u32[]{:S(2)}, u32[]{:S(2)}) %all-to-all-start.2) | async-done | bytes 327712 | tf_op jit(solution)/shard_map/all_to_all | solution.py:372
  78.4 4.4 %collective-permute-start.9 = (f32[640,128]{1,0:T(8,128)S(1)}, f32[640,128]{1,0:T(8,128)S(1)}, u32[]{:S(2)}, u32[]{:S(2)}) collective-permute-start(f32[640,128]{1,0:T(8,128)S(1)} %bitcast.23), channel_id=1, source_target_pairs={{0,1},{1,0},{2,3},{3,2},{4,5},{5,4},{6,7},{7,6},{8,9},{9,8},{10,11... | collective-permute-start | bytes 983048 | tf_op jit(solution)/shard_map/ppermute | solution.py:368
  82.8 3.2 %shard_map.125 = (bf16[192,1024]{1,0:T(8,128)(2,1)}, f32[192,1024]{1,0:T(8,128)}, f32[8,128]{1,0:T(8,128)}) custom-call(bf16[192,1024]{1,0:T(8,128)(2,1)S(1)} %bitcast.28, f32[1,192]{1,0:T(1,128)S(1)} %bitcast.34, bf16[192,640]{1,0:T(8,128)(2,1)S(1)} %get-tuple-element.31.w_in, bf16[192,256]{1,0:T(8,128)(2,1)S(1)} %copy-done.12, ...), custom_call_target="tpu_custom_call" | custom-call | flops 4000000000 | bytes 12000000 | tf_op jit(solution)/shard_map/pallas_call | solution.py:417
  86.1 1.7 %shard_map.129 = (f32[4,192,192]{2,1,0:T(8,128)}, f32[1,192]{1,0:T(1,128)}) custom-call(s32[2]{0:T(128)S(1)} %pad_add_fusion.place, f32[640,128]{1,0:T(8,128)S(1)} %bitcast.24, f32[640,128]{1,0:T(8,128)S(1)} %collective-permute-done.9.other), custom_call_target="tpu_custom_call" | custom-call | flops 1000000000 | bytes 3000000 | tf_op jit(solution)/shard_map/pallas_call | solution.py:427
  (36 shorter events, 0.3 us)
Async XLA Ops:
  0.6 1.0 %copy-start = (bf16[1,1,1024,192]{2,3,1,0:T(8,128)(2,1)S(1)}, bf16[1,1,1024,192]{2,3,1,0:T(8,128)(2,1)}, u32[]{:S(2)}) copy-start(bf16[1,1,1024,192]{2,3,1,0:T(8,128)(2,1)} %param.9) | copy-start | bytes 1179652
  1.6 6.5 %copy-start.13 = (s32[1,1,24,64]{3,2,1,0:T(8,128)S(1)}, s32[1,1,24,64]{3,2,1,0:T(8,128)}, u32[]{:S(2)}) copy-start(s32[1,1,24,64]{3,2,1,0:T(8,128)} %param.16) | copy-start | bytes 18436
  1.9 7.6 %collective-permute-start.1 = (bf16[64,192]{1,0:T(8,128)(2,1)S(1)}, bf16[64,192]{1,0:T(8,128)(2,1)S(1)}, u32[]{:S(2)}, u32[]{:S(2)}) collective-permute-start(bf16[64,192]{1,0:T(8,128)(2,1)S(1)} %shard_map.120.own), channel_id=1, source_target_pairs={{0,0},{1,2},{2,1},{3,3},{4,4},{5,6},{6,5},{7,7},{8,8},{9,10},{10,9... | collective-permute-start | bytes 73736 | tf_op jit(solution)/shard_map/ppermute | solution.py:364
  7.9 1.6 %collective-permute-start = (bf16[64,192]{1,0:T(8,128)(2,1)S(1)}, bf16[64,192]{1,0:T(8,128)(2,1)S(1)}, u32[]{:S(2)}, u32[]{:S(2)}) collective-permute-start(bf16[64,192]{1,0:T(8,128)(2,1)S(1)} %shard_map.120.own), channel_id=1, source_target_pairs={{0,1},{1,0},{2,3},{3,2},{4,5},{5,4},{6,7},{7,6},{8,9},{9,8},{10,11... | collective-permute-start | bytes 73736 | tf_op jit(solution)/shard_map/ppermute | solution.py:364
  8.9 5.6 %copy-start.1 = (bf16[1,1,1024,192]{2,3,1,0:T(8,128)(2,1)S(1)}, bf16[1,1,1024,192]{2,3,1,0:T(8,128)(2,1)}, u32[]{:S(2)}) copy-start(bf16[1,1,1024,192]{2,3,1,0:T(8,128)(2,1)} %param.9) | copy-start | bytes 1179652
  8.9 5.6 %copy-start.2 = (bf16[1,1,1024,192]{2,3,1,0:T(8,128)(2,1)S(1)}, bf16[1,1,1024,192]{2,3,1,0:T(8,128)(2,1)}, u32[]{:S(2)}) copy-start(bf16[1,1,1024,192]{2,3,1,0:T(8,128)(2,1)} %param.17) | copy-start | bytes 1179652
  9.0 5.6 %copy-start.3 = (bf16[192,192]{1,0:T(8,128)(2,1)S(1)}, bf16[192,192]{1,0:T(8,128)(2,1)}, u32[]{:S(2)}) copy-start(bf16[192,192]{1,0:T(8,128)(2,1)} %wq.1) | copy-start | bytes 221188
  9.0 5.6 %copy-start.4 = (bf16[192,192]{1,0:T(8,128)(2,1)S(1)}, bf16[192,192]{1,0:T(8,128)(2,1)}, u32[]{:S(2)}) copy-start(bf16[192,192]{1,0:T(8,128)(2,1)} %wk.1) | copy-start | bytes 221188
  9.0 5.6 %copy-start.5 = (bf16[192,192]{1,0:T(8,128)(2,1)S(1)}, bf16[192,192]{1,0:T(8,128)(2,1)}, u32[]{:S(2)}) copy-start(bf16[192,192]{1,0:T(8,128)(2,1)} %wv.1) | copy-start | bytes 221188
  9.0 5.6 %copy-start.6 = (bf16[192,192]{1,0:T(8,128)(2,1)S(1)}, bf16[192,192]{1,0:T(8,128)(2,1)}, u32[]{:S(2)}) copy-start(bf16[192,192]{1,0:T(8,128)(2,1)} %wo.1) | copy-start | bytes 221188
  9.0 5.6 %copy-start.7 = (f32[192]{0:T(256)S(1)}, f32[192]{0:T(256)}, u32[]{:S(2)}) copy-start(f32[192]{0:T(256)} %param.10) | copy-start | bytes 2308
  10.1 6.4 %collective-permute-start.3 = (bf16[192,192]{1,0:T(8,128)(2,1)S(1)}, bf16[192,192]{1,0:T(8,128)(2,1)S(1)}, u32[]{:S(2)}, u32[]{:S(2)}) collective-permute-start(bf16[192,192]{1,0:T(8,128)(2,1)S(1)} %shard_map.121.after.own_near), channel_id=1, source_target_pairs={{0,0},{4,8},{8,4},{12,16},{16,12},{20,24},{24,20},{28,32},{32,28},... | collective-permute-start | bytes 221192 | tf_op jit(solution)/shard_map/ppermute | solution.py:364
  10.7 8.8 %collective-permute-start.2 = (bf16[192,192]{1,0:T(8,128)(2,1)S(1)}, bf16[192,192]{1,0:T(8,128)(2,1)S(1)}, u32[]{:S(2)}, u32[]{:S(2)}) collective-permute-start(bf16[192,192]{1,0:T(8,128)(2,1)S(1)} %shard_map.121.after.own_near), channel_id=1, source_target_pairs={{0,4},{4,0},{8,12},{12,8},{16,20},{20,16},{24,28},{28,24},{32,36},... | collective-permute-start | bytes 221192 | tf_op jit(solution)/shard_map/ppermute | solution.py:364
  14.6 4.9 %copy-start.8 = (s32[1,1,24]{2,1,0:T(1,128)S(1)}, s32[1,1,24]{2,1,0:T(1,128)}, u32[]{:S(2)}) copy-start(s32[1,1,24]{2,1,0:T(1,128)} %param.15) | copy-start | bytes 292
  16.5 13.2 %copy-start.11 = (bf16[192,256]{1,0:T(8,128)(2,1)}, bf16[192,256]{1,0:T(8,128)(2,1)S(1)}, u32[]{:S(2)}) copy-start(bf16[192,256]{1,0:T(8,128)(2,1)S(1)} %get-tuple-element.32.w_back) | copy-start | bytes 294916
  29.7 2.4 %copy-start.9 = (bf16[1024,768]{1,0:T(8,128)(2,1)}, bf16[1024,768]{1,0:T(8,128)(2,1)S(1)}, u32[]{:S(2)}) copy-start(bf16[1024,768]{1,0:T(8,128)(2,1)S(1)} %get-tuple-element.41.grads) | copy-start | bytes 4718596
  32.1 2.1 %collective-permute-start.8 = (f32[640,128]{1,0:T(8,128)S(1)}, f32[640,128]{1,0:T(8,128)S(1)}, u32[]{:S(2)}, u32[]{:S(2)}) collective-permute-start(f32[640,128]{1,0:T(8,128)S(1)} %get-tuple-element.55), channel_id=1, source_target_pairs={{0,1},{1,0},{2,3},{3,2},{4,5},{5,4},{6,7},{7,6},{8,9},{9,8},{10,11... | collective-permute-start | bytes 983048 | tf_op jit(solution)/shard_map/ppermute | solution.py:368
  35.0 14.0 %all-to-all-start = ((f32[16,40,128]{2,1,0:T(8,128)}), f32[16,40,128]{2,1,0:T(8,128)S(1)}, u32[]{:S(2)}, u32[]{:S(2)}) async-start(f32[16,40,128]{2,1,0:T(8,128)} %bitcast.14), calls=%async_computation | async-start | bytes 655360 | tf_op jit(solution)/shard_map/all_to_all | solution.py:372
  41.2 5.6 %collective-permute-start.4 = (bf16[3,64,384]{2,1,0:T(8,128)(2,1)S(1)}, bf16[3,64,384]{2,1,0:T(8,128)(2,1)S(1)}, u32[]{:S(2)}, u32[]{:S(2)}) collective-permute-start(bf16[3,64,384]{2,1,0:T(8,128)(2,1)S(1)} %get-tuple-element.43), channel_id=1, source_target_pairs={{0,1},{1,0},{2,3},{3,2},{4,5},{5,4},{6,7},{7,6},{8,9},{9,8},{10,11... | collective-permute-start | bytes 442376 | tf_op jit(solution)/shard_map/ppermute | solution.py:364
  42.0 15.9 %collective-permute-start.5 = (bf16[3,64,384]{2,1,0:T(8,128)(2,1)S(1)}, bf16[3,64,384]{2,1,0:T(8,128)(2,1)S(1)}, u32[]{:S(2)}, u32[]{:S(2)}) collective-permute-start(bf16[3,64,384]{2,1,0:T(8,128)(2,1)S(1)} %get-tuple-element.44), channel_id=1, source_target_pairs={{0,0},{1,2},{2,1},{3,3},{4,4},{5,6},{6,5},{7,7},{8,8},{9,10},{10,9... | collective-permute-start | bytes 442376 | tf_op jit(solution)/shard_map/ppermute | solution.py:364
  49.7 16.6 %all-to-all-start.1 = ((f32[8,40,128]{2,1,0:T(8,128)}), f32[8,40,128]{2,1,0:T(8,128)S(1)}, u32[]{:S(2)}, u32[]{:S(2)}) async-start(f32[8,40,128]{2,1,0:T(8,128)} %shard_map.127), calls=%async_computation.1 | async-start | bytes 327680 | tf_op jit(solution)/shard_map/all_to_all | solution.py:372
  58.5 24.4 %copy-start.10 = (bf16[1024,768]{1,0:T(8,128)(2,1)S(1)}, bf16[1024,768]{1,0:T(8,128)(2,1)}, u32[]{:S(2)}) copy-start(bf16[1024,768]{1,0:T(8,128)(2,1)} %copy-done.9) | copy-start | bytes 4718596
  58.5 24.4 %copy-start.12 = (bf16[192,256]{1,0:T(8,128)(2,1)S(1)}, bf16[192,256]{1,0:T(8,128)(2,1)}, u32[]{:S(2)}) copy-start(bf16[192,256]{1,0:T(8,128)(2,1)} %copy-done.11) | copy-start | bytes 294916
  58.5 3.0 %collective-permute-start.6 = (bf16[64,384]{1,0:T(8,128)(2,1)S(1)}, bf16[64,384]{1,0:T(8,128)(2,1)S(1)}, u32[]{:S(2)}, u32[]{:S(2)}) collective-permute-start(bf16[64,384]{1,0:T(8,128)(2,1)S(1)} %get-tuple-element.46), channel_id=1, source_target_pairs={{0,4},{4,0},{8,12},{12,8},{16,20},{20,16},{24,28},{28,24},{32,36},... | collective-permute-start | bytes 147464 | tf_op jit(solution)/shard_map/ppermute | solution.py:364
  67.0 11.5 %all-to-all-start.2 = ((f32[16,40,128]{2,1,0:T(8,128)}), f32[16,40,128]{2,1,0:T(8,128)S(1)}, u32[]{:S(2)}, u32[]{:S(2)}) async-start(f32[16,40,128]{2,1,0:T(8,128)} %shard_map.128), calls=%async_computation.2 | async-start | bytes 655360 | tf_op jit(solution)/shard_map/all_to_all | solution.py:372
  70.9 12.0 %collective-permute-start.7 = (bf16[64,384]{1,0:T(8,128)(2,1)S(1)}, bf16[64,384]{1,0:T(8,128)(2,1)S(1)}, u32[]{:S(2)}, u32[]{:S(2)}) collective-permute-start(bf16[64,384]{1,0:T(8,128)(2,1)S(1)} %get-tuple-element.47), channel_id=1, source_target_pairs={{0,0},{4,8},{8,4},{12,16},{16,12},{20,24},{24,20},{28,32},{32,28},... | collective-permute-start | bytes 147464 | tf_op jit(solution)/shard_map/ppermute | solution.py:364
  78.4 7.6 %collective-permute-start.9 = (f32[640,128]{1,0:T(8,128)S(1)}, f32[640,128]{1,0:T(8,128)S(1)}, u32[]{:S(2)}, u32[]{:S(2)}) collective-permute-start(f32[640,128]{1,0:T(8,128)S(1)} %bitcast.23), channel_id=1, source_target_pairs={{0,1},{1,0},{2,3},{3,2},{4,5},{5,4},{6,7},{7,6},{8,9},{9,8},{10,11... | collective-permute-start | bytes 983048 | tf_op jit(solution)/shard_map/ppermute | solution.py:368
